TPU v7x, 32 devices: a whole 2x2x4 slice. The times are simulated.
32 devices in a mesh: ctx: 4 (over z), fsdp: 8 (over y, x, core).
Axes of the slice: x: 2, y: 2, z: 4, core: 2. Of those that a mesh axis runs over, the one named last changes fastest.
Arguments:
- tokens: bfloat16 [8, 1024, 1024], P('fsdp', 'ctx'), may hold values from -6 to 6
- w_qkv: bfloat16 [1024, 3072], P('fsdp'), may hold values from -0.1875 to 0.1875
- b_query: bfloat16 [1024], P('fsdp'), may hold values from -3 to 3
- b_value: bfloat16 [1024], P('fsdp'), may hold values from -3 to 3
- w_attn_out: bfloat16 [1024, 1024], P('fsdp'), may hold values from -3 to 3
- b_attn_out: bfloat16 [1024], P('fsdp'), may hold values from -3 to 3
- norm1_gain: bfloat16 [1024], P('fsdp'), may hold values from 0.5 to 1.5
- norm1_shift: bfloat16 [1024], P('fsdp'), may hold values from -3 to 3
- w_up: bfloat16 [1024, 4096], P('fsdp'), may hold values from -0.1875 to 0.1875
- b_up: bfloat16 [4096], P('fsdp'), may hold values from -3 to 3
- w_down: bfloat16 [4096, 1024], P('fsdp'), may hold values from -0.09375 to 0.09375
- b_down: bfloat16 [1024], P('fsdp'), may hold values from -3 to 3
- norm2_gain: bfloat16 [1024], P('fsdp'), may hold values from 0.5 to 1.5
- norm2_shift: bfloat16 [1024], P('fsdp'), may hold values from -3 to 3
- d_out: bfloat16 [8, 1024, 1024], P('fsdp', 'ctx'), may hold values from -6 to 6
Outputs:
- output: bfloat16 [8, 1024, 1024], P('fsdp', 'ctx')
- d_tokens: float32 [8, 1024, 1024], P('fsdp', 'ctx')
- grad_w_qkv: float32 [1024, 3072], P('fsdp')
- grad_b_query: float32 [1024], P('fsdp')
- grad_b_value: float32 [1024], P('fsdp')
- grad_w_attn_out: float32 [1024, 1024], P('fsdp')
- grad_b_attn_out: float32 [1024], P('fsdp')
- grad_norm1_gain: float32 [1024], P('fsdp')
- grad_norm1_shift: float32 [1024], P('fsdp')
- grad_w_up: float32 [1024, 4096], P('fsdp')
- grad_b_up: float32 [4096], P('fsdp')
- grad_w_down: float32 [4096, 1024], P('fsdp')
- grad_b_down: float32 [1024], P('fsdp')
- grad_norm2_gain: float32 [1024], P('fsdp')
- grad_norm2_shift: float32 [1024], P('fsdp')
All inputs are finite; a program needn't handle non-finite values.
Results may differ from a plain program's by a relative error of at most 0.028.
Values may be sent and summed in bfloat16 or wider, within the bound.
A program may use at most 192 MiB of HBM per device.

v0:
```python
import jax
import jax.numpy as jnp
from jax import lax
from jax.sharding import PartitionSpec as P

HEADS = 16
HEAD_DIM = 64


norm_eps = 1e-05


def layer_norm(inputs, gain, shift):
    center = inputs - jnp.mean(inputs, axis=-1, keepdims=True)
    variance = jnp.mean(center * center, axis=-1, keepdims=True)
    return center * lax.rsqrt(variance + norm_eps) * gain + shift


def gelu_exact(hidden):
    return jax.nn.gelu(hidden, approximate=False)


def per_device(
    tokens,
    w_qkv,
    b_query,
    b_value,
    w_attn_out,
    b_attn_out,
    norm1_gain,
    norm1_shift,
    w_up,
    b_up,
    w_down,
    b_down,
    norm2_gain,
    norm2_shift,
    d_out,
):
    gathered = (
        lax.all_gather(w_qkv, "fsdp", axis=0, tiled=True),
        lax.all_gather(b_query, "fsdp", axis=0, tiled=True),
        lax.all_gather(b_value, "fsdp", axis=0, tiled=True),
        lax.all_gather(w_attn_out, "fsdp", axis=0, tiled=True),
        lax.all_gather(b_attn_out, "fsdp", axis=0, tiled=True),
        lax.all_gather(norm1_gain, "fsdp", axis=0, tiled=True),
        lax.all_gather(norm1_shift, "fsdp", axis=0, tiled=True),
        lax.all_gather(w_up, "fsdp", axis=0, tiled=True),
        lax.all_gather(b_up, "fsdp", axis=0, tiled=True),
        lax.all_gather(w_down, "fsdp", axis=0, tiled=True),
        lax.all_gather(b_down, "fsdp", axis=0, tiled=True),
        lax.all_gather(norm2_gain, "fsdp", axis=0, tiled=True),
        lax.all_gather(norm2_shift, "fsdp", axis=0, tiled=True),
    )
    (
        input_proj,
        query_bias,
        value_bias,
        out_weight,
        out_bias,
        gain_one,
        shift_one,
        up_weight,
        up_bias,
        down_weight,
        down_bias,
        gain_two,
        shift_two,
    ) = gathered
    seq_local, block_rows, width = tokens.shape
    row_count = seq_local * block_rows
    tok_rows = tokens.reshape(row_count, width)
    score_scale = HEAD_DIM ** (-0.5)
    head_shape = (seq_local, block_rows, HEADS, HEAD_DIM)
    proj_all = jnp.dot(tok_rows, input_proj, preferred_element_type=jnp.float32)
    queries = (proj_all[:, :width] + query_bias.astype(jnp.float32)).astype(jnp.bfloat16)
    key_send = (
        proj_all[:, width : 2 * width].astype(jnp.bfloat16).reshape(seq_local, block_rows, width)
    )
    value_send = (proj_all[:, 2 * width :] + value_bias.astype(jnp.float32)).astype(jnp.bfloat16)
    value_send = value_send.reshape(seq_local, block_rows, width)
    query_heads = queries.reshape(head_shape)
    shard_kv = (
        lax.all_gather(key_send, "ctx", axis=1, tiled=True),
        lax.all_gather(value_send, "ctx", axis=1, tiled=True),
    )
    row_max = jnp.full((seq_local, HEADS, block_rows), -1e30, jnp.float32)
    key_part = shard_kv[0].reshape(seq_local, -1, HEADS, HEAD_DIM)
    value_part = shard_kv[1].reshape(seq_local, -1, HEADS, HEAD_DIM)
    scores = (
        jnp.einsum("sqhd,skhd->shqk", query_heads, key_part, preferred_element_type=jnp.float32)
        * score_scale
    )
    new_max = jnp.maximum(row_max, jnp.max(scores, axis=-1))
    attn_prob = jnp.exp(scores - new_max[..., None])
    row_total = jnp.sum(attn_prob, axis=-1)
    accumulated = jnp.einsum(
        "shqk,skhd->shqd",
        attn_prob.astype(jnp.bfloat16),
        value_part,
        preferred_element_type=jnp.float32,
    )
    row_max, row_total, accumulated = (new_max, row_total, accumulated)
    mixed_out = accumulated / row_total[..., None]
    log_total = row_max + jnp.log(row_total)
    attn_in = mixed_out.transpose(0, 2, 1, 3).reshape(row_count, width).astype(jnp.bfloat16)
    attn_out = jnp.dot(attn_in, out_weight, preferred_element_type=jnp.float32) + out_bias.astype(
        jnp.float32
    )
    resid_one = tok_rows.astype(jnp.float32) + attn_out
    normed = layer_norm(resid_one, gain_one.astype(jnp.float32), shift_one.astype(jnp.float32))
    normed_low = normed.astype(jnp.bfloat16)
    hidden = jnp.dot(normed_low, up_weight, preferred_element_type=jnp.float32) + up_bias.astype(
        jnp.float32
    )
    activated = gelu_exact(hidden).astype(jnp.bfloat16)
    branch = jnp.dot(activated, down_weight, preferred_element_type=jnp.float32) + down_bias.astype(
        jnp.float32
    )
    resid_two = normed + branch
    result = layer_norm(resid_two, gain_two.astype(jnp.float32), shift_two.astype(jnp.float32))
    output = result.astype(jnp.bfloat16).reshape(seq_local, block_rows, width)
    input_proj, out_weight, up_weight, down_weight, gain_one, gain_two = (
        lax.all_gather(w_qkv, "fsdp", axis=0, tiled=True),
        lax.all_gather(w_attn_out, "fsdp", axis=0, tiled=True),
        lax.all_gather(w_up, "fsdp", axis=0, tiled=True),
        lax.all_gather(w_down, "fsdp", axis=0, tiled=True),
        lax.all_gather(norm1_gain, "fsdp", axis=0, tiled=True),
        lax.all_gather(norm2_gain, "fsdp", axis=0, tiled=True),
    )
    cotangent = d_out.reshape(row_count, width).astype(jnp.float32)
    norm_pull = jax.vjp(
        layer_norm, resid_two, gain_two.astype(jnp.float32), shift_two.astype(jnp.float32)
    )[1]
    grad_resid_two, grad_gain_two, grad_shift_two = norm_pull(cotangent)
    grad_branch = grad_resid_two.astype(jnp.bfloat16)
    grad_down = jnp.einsum("tf,td->fd", activated, grad_branch, preferred_element_type=jnp.float32)
    grad_down_bias = jnp.sum(grad_branch.astype(jnp.float32), axis=0)
    grad_act = jnp.einsum("td,fd->tf", grad_branch, down_weight, preferred_element_type=jnp.float32)
    grad_hidden = jax.vjp(gelu_exact, hidden)[1](grad_act)[0].astype(jnp.bfloat16)
    grad_up = jnp.einsum("td,tf->df", normed_low, grad_hidden, preferred_element_type=jnp.float32)
    grad_up_bias = jnp.sum(grad_hidden.astype(jnp.float32), axis=0)
    grad_normed = grad_resid_two + jnp.einsum(
        "tf,df->td", grad_hidden, up_weight, preferred_element_type=jnp.float32
    )
    norm_pull_one = jax.vjp(
        layer_norm, resid_one, gain_one.astype(jnp.float32), shift_one.astype(jnp.float32)
    )[1]
    grad_resid_one, grad_gain_one, grad_shift_one = norm_pull_one(grad_normed)
    grad_attn = grad_resid_one.astype(jnp.bfloat16)
    grad_out_weight = jnp.einsum(
        "td,te->de", attn_in, grad_attn, preferred_element_type=jnp.float32
    )
    grad_out_bias = jnp.sum(grad_attn.astype(jnp.float32), axis=0)
    grad_mixed = jnp.einsum(
        "te,de->td", grad_attn, out_weight, preferred_element_type=jnp.float32
    ).astype(jnp.bfloat16)
    grad_heads = grad_mixed.reshape(head_shape)
    row_delta = jnp.einsum("sqhd,shqd->shq", grad_heads.astype(jnp.float32), mixed_out)
    shard_kv = (
        lax.all_gather(key_send, "ctx", axis=1, tiled=True),
        lax.all_gather(value_send, "ctx", axis=1, tiled=True),
    )
    key_part = shard_kv[0].reshape(seq_local, -1, HEADS, HEAD_DIM)
    value_part = shard_kv[1].reshape(seq_local, -1, HEADS, HEAD_DIM)
    key_count = key_part.shape[1]
    scores = (
        jnp.einsum("sqhd,skhd->shqk", query_heads, key_part, preferred_element_type=jnp.float32)
        * score_scale
    )
    attn_prob = jnp.exp(scores - log_total[..., None])
    grad_prob = jnp.einsum(
        "sqhd,skhd->shqk", grad_heads, value_part, preferred_element_type=jnp.float32
    )
    grad_score = (attn_prob * (grad_prob - row_delta[..., None])).astype(jnp.bfloat16)
    block_grad_query = (
        jnp.einsum("shqk,skhd->sqhd", grad_score, key_part, preferred_element_type=jnp.float32)
        * score_scale
    )
    grad_key = (
        jnp.einsum("shqk,sqhd->kshd", grad_score, query_heads, preferred_element_type=jnp.float32)
        * score_scale
    )
    grad_value = jnp.einsum(
        "shqk,sqhd->kshd",
        attn_prob.astype(jnp.bfloat16),
        grad_heads,
        preferred_element_type=jnp.float32,
    )
    stacked = jnp.stack(
        (
            grad_key.reshape(key_count, seq_local, width),
            grad_value.reshape(key_count, seq_local, width),
        ),
        axis=2,
    )
    grad_query, stacked = (block_grad_query, stacked)
    key_terms = stacked
    grad_query, key_terms = (grad_query, key_terms)
    own_terms = lax.psum_scatter(
        key_terms.astype(jnp.bfloat16), "ctx", scatter_dimension=0, tiled=True
    ).astype(jnp.float32)
    grad_keys = own_terms[:, :, 0].transpose(1, 0, 2).reshape(row_count, width).astype(jnp.bfloat16)
    grad_values = (
        own_terms[:, :, 1].transpose(1, 0, 2).reshape(row_count, width).astype(jnp.bfloat16)
    )
    grad_queries = grad_query.reshape(row_count, width).astype(jnp.bfloat16)
    grad_proj = jnp.concatenate((grad_queries, grad_keys, grad_values), axis=1)
    grad_input_proj = jnp.einsum(
        "td,te->de", tok_rows, grad_proj, preferred_element_type=jnp.float32
    )
    grad_query_bias = jnp.sum(grad_queries.astype(jnp.float32), axis=0)
    grad_value_bias = jnp.sum(grad_values.astype(jnp.float32), axis=0)
    d_tokens = grad_resid_one + jnp.einsum(
        "te,de->td", grad_proj, input_proj, preferred_element_type=jnp.float32
    )
    owned = (
        lax.psum_scatter(
            grad_input_proj.astype(jnp.bfloat16), "fsdp", scatter_dimension=0, tiled=True
        ).astype(jnp.float32),
        lax.psum_scatter(
            grad_query_bias.astype(jnp.bfloat16), "fsdp", scatter_dimension=0, tiled=True
        ).astype(jnp.float32),
        lax.psum_scatter(
            grad_value_bias.astype(jnp.bfloat16), "fsdp", scatter_dimension=0, tiled=True
        ).astype(jnp.float32),
        lax.psum_scatter(
            grad_out_weight.astype(jnp.bfloat16), "fsdp", scatter_dimension=0, tiled=True
        ).astype(jnp.float32),
        lax.psum_scatter(
            grad_out_bias.astype(jnp.bfloat16), "fsdp", scatter_dimension=0, tiled=True
        ).astype(jnp.float32),
        lax.psum_scatter(
            grad_gain_one.astype(jnp.bfloat16), "fsdp", scatter_dimension=0, tiled=True
        ).astype(jnp.float32),
        lax.psum_scatter(
            grad_shift_one.astype(jnp.bfloat16), "fsdp", scatter_dimension=0, tiled=True
        ).astype(jnp.float32),
        lax.psum_scatter(
            grad_up.astype(jnp.bfloat16), "fsdp", scatter_dimension=0, tiled=True
        ).astype(jnp.float32),
        lax.psum_scatter(
            grad_up_bias.astype(jnp.bfloat16), "fsdp", scatter_dimension=0, tiled=True
        ).astype(jnp.float32),
        lax.psum_scatter(
            grad_down.astype(jnp.bfloat16), "fsdp", scatter_dimension=0, tiled=True
        ).astype(jnp.float32),
        lax.psum_scatter(
            grad_down_bias.astype(jnp.bfloat16), "fsdp", scatter_dimension=0, tiled=True
        ).astype(jnp.float32),
        lax.psum_scatter(
            grad_gain_two.astype(jnp.bfloat16), "fsdp", scatter_dimension=0, tiled=True
        ).astype(jnp.float32),
        lax.psum_scatter(
            grad_shift_two.astype(jnp.bfloat16), "fsdp", scatter_dimension=0, tiled=True
        ).astype(jnp.float32),
    )
    summed = (
        lax.psum(owned[0].astype(jnp.bfloat16), "ctx").astype(jnp.float32),
        lax.psum(owned[1].astype(jnp.bfloat16), "ctx").astype(jnp.float32),
        lax.psum(owned[2].astype(jnp.bfloat16), "ctx").astype(jnp.float32),
        lax.psum(owned[3].astype(jnp.bfloat16), "ctx").astype(jnp.float32),
        lax.psum(owned[4].astype(jnp.bfloat16), "ctx").astype(jnp.float32),
        lax.psum(owned[5].astype(jnp.bfloat16), "ctx").astype(jnp.float32),
        lax.psum(owned[6].astype(jnp.bfloat16), "ctx").astype(jnp.float32),
        lax.psum(owned[7].astype(jnp.bfloat16), "ctx").astype(jnp.float32),
        lax.psum(owned[8].astype(jnp.bfloat16), "ctx").astype(jnp.float32),
        lax.psum(owned[9].astype(jnp.bfloat16), "ctx").astype(jnp.float32),
        lax.psum(owned[10].astype(jnp.bfloat16), "ctx").astype(jnp.float32),
        lax.psum(owned[11].astype(jnp.bfloat16), "ctx").astype(jnp.float32),
        lax.psum(owned[12].astype(jnp.bfloat16), "ctx").astype(jnp.float32),
    )
    return (
        output,
        d_tokens.reshape(seq_local, block_rows, width),
        summed[0],
        summed[1],
        summed[2],
        summed[3],
        summed[4],
        summed[5],
        summed[6],
        summed[7],
        summed[8],
        summed[9],
        summed[10],
        summed[11],
        summed[12],
    )


def solution(mesh):
    placed = (
        P("fsdp", "ctx", None),
        P("fsdp", None),
        P("fsdp"),
        P("fsdp"),
        P("fsdp", None),
        P("fsdp"),
        P("fsdp"),
        P("fsdp"),
        P("fsdp", None),
        P("fsdp"),
        P("fsdp", None),
        P("fsdp"),
        P("fsdp"),
        P("fsdp"),
        P("fsdp", "ctx", None),
    )
    return jax.shard_map(
        per_device,
        mesh=mesh,
        in_specs=placed,
        out_specs=(
            P("fsdp", "ctx", None),
            P("fsdp", "ctx", None),
            P("fsdp", None),
            P("fsdp"),
            P("fsdp"),
            P("fsdp", None),
            P("fsdp"),
            P("fsdp"),
            P("fsdp"),
            P("fsdp", None),
            P("fsdp"),
            P("fsdp", None),
            P("fsdp"),
            P("fsdp"),
            P("fsdp"),
        ),
        check_vma=False,
    )
```

profile of v0, /device:TPU:0, one launch (start us, length us, event | category | flops | bytes accessed | tf_op | source)
XLA Modules:
  0.0 843.5 jit_solution(4623592050887938171)
XLA Ops:
  7.2 0.7 all-gather.18.cloned.1.call-update
  8.0 10.3 %all-gather.2 = bf16[8,1,128]{2,1,0:T(2,128)(2,1)S(1)} all-gather(bf16[1,1,128]{2,1,0:T(2,128)(2,1)} %bitcast.128), channel_id=1, replica_groups=mesh['ctx'=4,'fsdp'=8] {'fsdp'}, dimensions={0}, use_global_device_ids=true | all-gather | bytes 2304 | tf_op jit(solution)/shard_map/all_gather | solution.py:42
  18.3 8.6 %all-gather.3 = bf16[8,1,128]{2,1,0:T(2,128)(2,1)S(1)} all-gather(bf16[1,1,128]{2,1,0:T(2,128)(2,1)} %bitcast.129), channel_id=1, replica_groups=mesh['ctx'=4,'fsdp'=8] {'fsdp'}, dimensions={0}, use_global_device_ids=true | all-gather | bytes 2304 | tf_op jit(solution)/shard_map/all_gather | solution.py:43
  26.9 31.3 %all-gather.18.cloned.1.call-done = bf16[1024,3072]{1,0:T(8,128)(2,1)} async-done(((bf16[128,3072]{1,0:T(8,128)(2,1)}), bf16[1024,3072]{1,0:T(8,128)(2,1)}) %all-gather.18.cloned.1.call-update) | async-done | bytes 6291472 | tf_op jit(solution)/shard_map/all_gather | solution.py:41
  58.2 4.8 fusion.37
  63.0 1.2 fusion.29
  64.3 0.9 slice.38
  67.0 8.7 %all-gather.4 = bf16[8,1,128]{2,1,0:T(2,128)(2,1)S(1)} all-gather(bf16[1,1,128]{2,1,0:T(2,128)(2,1)S(1)} %bitcast.130), channel_id=1, replica_groups=mesh['ctx'=4,'fsdp'=8] {'fsdp'}, dimensions={0}, use_global_device_ids=true | all-gather | bytes 2304 | tf_op jit(solution)/shard_map/all_gather | solution.py:45
  75.7 7.8 all-gather.5
  83.5 8.7 %all-gather.6 = bf16[8,1,128]{2,1,0:T(2,128)(2,1)S(1)} all-gather(bf16[1,1,128]{2,1,0:T(2,128)(2,1)S(1)} %bitcast.132), channel_id=1, replica_groups=mesh['ctx'=4,'fsdp'=8] {'fsdp'}, dimensions={0}, use_global_device_ids=true | all-gather | bytes 2304 | tf_op jit(solution)/shard_map/all_gather | solution.py:47
  92.2 7.8 all-gather.8
  100.0 8.7 %all-gather.9 = bf16[8,1,128]{2,1,0:T(2,128)(2,1)S(1)} all-gather(bf16[1,1,128]{2,1,0:T(2,128)(2,1)S(1)} %bitcast.134), channel_id=1, replica_groups=mesh['ctx'=4,'fsdp'=8] {'fsdp'}, dimensions={0}, use_global_device_ids=true | all-gather | bytes 2304 | tf_op jit(solution)/shard_map/all_gather | solution.py:52
  108.7 7.8 all-gather.10
  116.5 9.0 %all-gather.7 = bf16[8,1,512]{2,1,0:T(2,128)(2,1)S(1)} all-gather(bf16[1,1,512]{2,1,0:T(2,128)(2,1)S(1)} %reshape.286), channel_id=1, replica_groups=mesh['ctx'=4,'fsdp'=8] {'fsdp'}, dimensions={0}, use_global_device_ids=true | all-gather | bytes 9216 | tf_op jit(solution)/shard_map/all_gather | solution.py:49
  125.5 1.2 copy.44
  126.8 4.1 copy.46
  130.9 26.3 %all-gather.26.cloned.1.call-done = bf16[1024,1024]{1,0:T(8,128)(2,1)} async-done(((bf16[256,1024]{1,0:T(8,128)(2,1)}), bf16[1024,1024]{1,0:T(8,128)(2,1)}) %all-gather.26.cloned.1.call-update) | async-done | bytes 2097168 | tf_op jit(solution)/shard_map/all_gather | solution.py:84
  157.2 2.9 copy.45
  160.1 2.5 multiply_reduce_fusion
  162.6 3.5 fusion
  166.0 2.9 copy-done
  169.0 4.5 fusion.53
  173.4 12.1 %all-gather.20.cloned.1.call-done = bf16[1024,1024]{1,0:T(8,128)(2,1)} async-done(((bf16[128,1024]{1,0:T(8,128)(2,1)}), bf16[1024,1024]{1,0:T(8,128)(2,1)}) %all-gather.20.cloned.1.call-update) | async-done | bytes 2097168 | tf_op jit(solution)/shard_map/all_gather | solution.py:44
  185.5 2.6 fusion.54
  188.5 53.2 %all-gather.22.cloned.1.call-done = bf16[1024,4096]{1,0:T(8,128)(2,1)} async-done(((bf16[128,4096]{1,0:T(8,128)(2,1)}), bf16[1024,4096]{1,0:T(8,128)(2,1)}) %all-gather.22.cloned.1.call-update) | async-done | bytes 8388624 | tf_op jit(solution)/shard_map/all_gather | solution.py:48
  241.7 16.4 %multiply_convert_fusion.2 = (bf16[256,4096]{1,0:T(8,128)(2,1)}, f32[256,4096]{1,0:T(8,128)}, f32[256,4096]{1,0:T(8,128)}) fusion(f32[4096]{0:T(1024)S(1)} %bitcast.126, bf16[1024,4096]{1,0:T(8,128)(2,1)} %all-gather.22.cloned.1.call-done, f32[256,1024]{1,0:T(8,128)S(1)} %get-tuple-element.110, f32[1024]{0:T(1024)S(1)} %bitcast.117, ...), kind=kOutput, calls=%fused_computation.22 | convolution fusion | flops 2218000384 | bytes 19949568 | tf_op jit(solution)/shard_map/dot_general | solution.py:113
  258.1 39.8 %all-gather.24.cloned.1.call-done = bf16[4096,1024]{1,0:T(8,128)(2,1)} async-done(((bf16[512,1024]{1,0:T(8,128)(2,1)}), bf16[4096,1024]{1,0:T(8,128)(2,1)}) %all-gather.24.cloned.1.call-update) | async-done | bytes 8388624 | tf_op jit(solution)/shard_map/all_gather | solution.py:50
  297.8 6.6 fusion.55
  305.2 1.3 fusion.51
  306.7 6.5 fusion.48
  313.2 6.9 multiply_reduce_fusion.1
  320.6 1.0 copy-done.9
  321.7 0.8 copy-done.17
  322.5 1.5 convolution_convert_fusion.3
  324.1 2.0 copy.47
  326.1 1.5 fusion.30
  327.7 9.1 %fusion.17 = bf16[16,64,1024]{2,1,0:T(8,128)(2,1)S(1)} fusion(bf16[256,16,64]{0,2,1:T(8,128)(2,1)} %bitcast.101, f32[16,256,1024]{2,1,0:T(8,128)} %copy-done, f32[16,256]{1,0:T(8,128)S(1)} %log_add_fusion), kind=kOutput, calls=%fused_computation.36 | convolution fusion | flops 550502400 | bytes 19415040 | tf_op jit(solution)/shard_map/shqk,sqhd->kshd/dot_general | solution.py:184
  336.8 8.4 multiply_convert_fusion
  345.3 1.6 multiply_convert_fusion.1
  346.8 1.7 copy-done.1
  348.5 2.3 pad_maximum_fusion
  351.1 6.8 fusion.56
  357.9 69.9 %reduce-scatter.8.cloned.1.call-done = bf16[256,1,2,1024]{0,3,2,1:T(8,128)(2,1)} async-done(((bf16[1024,1,2,1024]{0,3,2,1:T(8,128)(2,1)}), bf16[256,1,2,1024]{0,3,2,1:T(8,128)(2,1)}) %reduce-scatter.8.cloned.1.call-update) | async-done | bytes 1048592 | tf_op jit(solution)/shard_map/reduce_scatter | solution.py:200
  427.8 1.4 slice_reduce_fusion
  429.2 0.8 copy-done.20
  430.2 5.6 convert_bitcast_fusion
  435.8 8.6 %copy.56 = bf16[1024,3072]{1,0:T(8,128)(2,1)} copy(bf16[1024,3072]{0,1:T(8,128)(2,1)} %convert_bitcast_fusion) | data formatting | bytes 12582912
  444.5 3.4 convolution_convert_fusion.2
  448.0 6.2 convolution_convert_fusion.1
  454.2 1.8 copy-done.11
  456.2 5.6 convolution_convert_fusion
  462.0 44.9 %reduce-scatter.16.cloned.1.call-done = bf16[128,3072]{1,0:T(8,128)(2,1)} async-done(((bf16[1024,3072]{1,0:T(8,128)(2,1)}), bf16[128,3072]{1,0:T(8,128)(2,1)}) %reduce-scatter.16.cloned.1.call-update) | async-done | bytes 786448
  506.9 2.3 copy.57
  509.2 42.8 %reduce-scatter.10.cloned.1.call-done = bf16[128,1024]{1,0:T(8,128)(2,1)} async-done(((bf16[1024,1024]{1,0:T(8,128)(2,1)}), bf16[128,1024]{1,0:T(8,128)(2,1)}) %reduce-scatter.10.cloned.1.call-update) | async-done | bytes 262160 | tf_op jit(solution)/shard_map/reduce_scatter | solution.py:227
  552.0 75.0 %reduce-scatter.12.cloned.1.call-done = bf16[128,4096]{1,0:T(8,128)(2,1)} async-done(((bf16[1024,4096]{1,0:T(8,128)(2,1)}), bf16[128,4096]{1,0:T(8,128)(2,1)}) %reduce-scatter.12.cloned.1.call-update) | async-done | bytes 1048592 | tf_op jit(solution)/shard_map/reduce_scatter | solution.py:239
  627.0 74.8 %reduce-scatter.14.cloned.1.call-done = bf16[512,1024]{1,0:T(8,128)(2,1)} async-done(((bf16[4096,1024]{1,0:T(8,128)(2,1)}), bf16[512,1024]{1,0:T(8,128)(2,1)}) %reduce-scatter.14.cloned.1.call-update) | async-done | bytes 1048592 | tf_op jit(solution)/shard_map/reduce_scatter | solution.py:245
  703.9 23.9 %all-reduce.9 = (bf16[1024]{0:T(1024)(128)(2,1)S(1)}, bf16[1024]{0:T(1024)(128)(2,1)S(1)}, bf16[1024]{0:T(1024)(128)(2,1)S(1)}, bf16[1024]{0:T(1024)(128)(2,1)S(...) all-reduce(bf16[1024]{0:T(1024)(128)(2,1)S(1)} %reduce_sum.240, ...), channel_id=6, replica_groups=mesh['ctx'=4,'fsdp'=8] {'fsdp'}, use_global_device_ids=true, to_apply=%region_14.0.clone | all-reduce | flops 12288 | bytes 49152
  728.5 13.4 %all-reduce.10 = (bf16[128]{0:T(256)(128)(2,1)S(1)}, bf16[128]{0:T(256)(128)(2,1)S(1)}, bf16[128]{0:T(256)(128)(2,1)S(1)}, bf16[128]{0:T(256)(128)(2,1)S(1)}, bf...) all-reduce(bf16[128]{0:T(256)(128)(2,1)S(1)} %dynamic-slice.1, ...), channel_id=1, replica_groups=mesh['ctx'=4,'fsdp'=8] {'ctx'}, use_global_device_ids=true, to_apply=%region_15.0 | all-reduce | flops 1536 | bytes 6144 | tf_op jit(solution)/shard_map/psum | solution.py:260
  746.6 5.6 fusion.21
  752.2 75.4 %all-reduce.14.cloned.1.call-done = (bf16[128,3072]{0,1:T(8,128)(2,1)}, bf16[128,1024]{1,0:T(8,128)(2,1)}, bf16[128,4096]{1,0:T(8,128)(2,1)}, bf16[512,1024]{1,0:T(8,128)(2,1)}) async-done(((bf16[128,3072]{0,1:T(8,128)(2,1)}, bf16[128,1024]{1,0:T(8,128)(2,1)}, bf16[128,4096]{1,0:T(8,128)(2,1)}, bf16[512,1024]{1,0:T(8,128)(2,1)}), (bf16[128,3072]{0,1:T(8,128)(2,1)}, bf16[128,1024]{1,0:T(8,128)(2,1)}, ...) | async-done | bytes 3145744 | tf_op jit(solution)/shard_map/psum | solution.py:259
  827.6 1.9 convert_element_type.264
  829.5 2.5 copy.48
  832.1 2.8 convert_element_type.271
  834.8 1.6 convert_element_type.274
  (134 shorter events, 10.8 us)
Async XLA Ops:
  7.2 51.0 %all-gather.18.cloned.1.call-start = ((), (), s32[]{:S(2)}) async-start(), calls=%async_computation.5 | async-start | bytes 7077888 | tf_op jit(solution)/shard_map/all_gather | solution.py:41
  7.9 118.9 %all-gather.28.cloned.1.call-start = ((), (), s32[]{:S(2)}) async-start(), calls=%async_computation.14 | async-start | bytes 2621440 | tf_op jit(solution)/shard_map/all_gather | solution.py:85
  62.9 4.1 copy-start.24
  62.9 4.1 copy-start.25
  62.9 12.8 %copy-start.26 = (bf16[128]{0:T(256)(128)(2,1)S(1)}, bf16[128]{0:T(256)(128)(2,1)}, u32[]{:S(2)}) copy-start(bf16[128]{0:T(256)(128)(2,1)} %param.21) | copy-start | bytes 772
  63.0 20.6 %copy-start.27 = (bf16[128]{0:T(256)(128)(2,1)S(1)}, bf16[128]{0:T(256)(128)(2,1)}, u32[]{:S(2)}) copy-start(bf16[128]{0:T(256)(128)(2,1)} %param.22) | copy-start | bytes 772
  63.0 29.2 %copy-start.28 = (bf16[128]{0:T(256)(128)(2,1)S(1)}, bf16[128]{0:T(256)(128)(2,1)}, u32[]{:S(2)}) copy-start(bf16[128]{0:T(256)(128)(2,1)} %param.26) | copy-start | bytes 772
  63.0 37.0 %copy-start.29 = (bf16[128]{0:T(256)(128)(2,1)S(1)}, bf16[128]{0:T(256)(128)(2,1)}, u32[]{:S(2)}) copy-start(bf16[128]{0:T(256)(128)(2,1)} %param.27) | copy-start | bytes 772
  63.0 45.7 %copy-start.30 = (bf16[128]{0:T(256)(128)(2,1)S(1)}, bf16[128]{0:T(256)(128)(2,1)}, u32[]{:S(2)}) copy-start(bf16[128]{0:T(256)(128)(2,1)} %param.28) | copy-start | bytes 772
  64.3 92.9 %all-gather.26.cloned.1.call-start = ((), (), s32[]{:S(2)}) async-start(), calls=%async_computation.13 | async-start | bytes 2621440 | tf_op jit(solution)/shard_map/all_gather | solution.py:84
  65.2 120.3 %all-gather.20.cloned.1.call-start = ((), (), s32[]{:S(2)}) async-start(), calls=%async_computation.6 | async-start | bytes 2359296 | tf_op jit(solution)/shard_map/all_gather | solution.py:44
  65.8 175.9 %all-gather.22.cloned.1.call-start = ((), (), s32[]{:S(2)}) async-start(), calls=%async_computation.7 | async-start | bytes 9437184 | tf_op jit(solution)/shard_map/all_gather | solution.py:48
  66.4 231.5 %all-gather.24.cloned.1.call-start = ((), (), s32[]{:S(2)}) async-start(), calls=%async_computation.8 | async-start | bytes 9437184 | tf_op jit(solution)/shard_map/all_gather | solution.py:50
  66.9 360.8 %reduce-scatter.8.cloned.1.call-start = ((), (), s32[]{:S(2)}) async-start(), calls=%async_computation.9 | async-start | bytes 5242880 | tf_op jit(solution)/shard_map/reduce_scatter | solution.py:200
  126.8 33.3 %copy-start.5 = (bf16[256,1024]{0,1:T(8,128)(2,1)}, bf16[256,1024]{0,1:T(8,128)(2,1)S(1)}, u32[]{:S(2)}) copy-start(bf16[256,1024]{0,1:T(8,128)(2,1)S(1)} %copy.44) | copy-start | bytes 1572868
  162.5 6.4 copy-start
  162.5 6.4 copy-start.3
  297.8 8.9 %slice-start = ((s8[8388608]{0:T(1024)(128)(4,1)}), s8[4194304]{0:T(1024)(128)(4,1)S(1)}, s32[]{:S(2)}) async-start(s8[8388608]{0:T(1024)(128)(4,1)} %bitcast.136), calls=%async_computation.17 | async-start | bytes 8388608
  297.8 6.9 copy-start.7
  297.8 8.9 %slice-start.1 = ((s8[8388608]{0:T(1024)(128)(4,1)}), s8[4194304]{0:T(1024)(128)(4,1)S(1)}, s32[]{:S(2)}) async-start(s8[8388608]{0:T(1024)(128)(4,1)} %bitcast.136), calls=%async_computation.18 | async-start | bytes 8388608
  306.7 6.5 copy-start.12
  313.2 6.9 copy-start.14
  320.1 2.4 copy-start.16
  320.6 1.0 copy-start.9
  321.7 0.8 copy-start.17
  327.6 9.2 %copy-start.2 = (bf16[256,1024]{0,1:T(8,128)(2,1)S(1)}, bf16[256,1024]{0,1:T(8,128)(2,1)}, u32[]{:S(2)}) copy-start(bf16[256,1024]{0,1:T(8,128)(2,1)} %copy.47) | copy-start | bytes 1572868
  327.6 9.2 %copy-start.4 = (bf16[1024,1024]{0,1:T(8,128)(2,1)S(1)}, bf16[1024,1024]{0,1:T(8,128)(2,1)}, u32[]{:S(2)}) copy-start(bf16[1024,1024]{0,1:T(8,128)(2,1)} %copy.46) | copy-start | bytes 6291460
  336.8 8.4 copy-start.6
  345.3 3.2 copy-start.1
  350.8 156.1 %reduce-scatter.16.cloned.1.call-start = ((), (), s32[]{:S(2)}) async-start(), calls=%async_computation.15 | async-start | bytes 7077888
  429.2 0.8 copy-start.20
  429.2 1.0 copy-start.22
  444.4 3.5 copy-start.15
  444.4 107.5 %reduce-scatter.10.cloned.1.call-start = ((), (), s32[]{:S(2)}) async-start(), calls=%async_computation.10 | async-start | bytes 2359296 | tf_op jit(solution)/shard_map/reduce_scatter | solution.py:227
  447.9 179.1 %reduce-scatter.12.cloned.1.call-start = ((), (), s32[]{:S(2)}) async-start(), calls=%async_computation.11 | async-start | bytes 9437184 | tf_op jit(solution)/shard_map/reduce_scatter | solution.py:239
  454.2 1.9 copy-start.11
  454.2 2.1 copy-start.13
  454.2 247.6 %reduce-scatter.14.cloned.1.call-start = ((), (), s32[]{:S(2)}) async-start(), calls=%async_computation.12 | async-start | bytes 9437184 | tf_op jit(solution)/shard_map/reduce_scatter | solution.py:245
  461.8 240.0 %copy-start.31 = (u32[32]{0:T(128)S(1)}, u32[32]{0:T(128)}, u32[]{:S(2)}) copy-start(u32[32]{0:T(128)} %constant.97) | copy-start | bytes 388
  461.9 241.9 %copy-start.8 = (bf16[1,256,1024]{2,1,0:T(8,128)(2,1)S(1)}, bf16[1,256,1024]{2,1,0:T(8,128)(2,1)}, u32[]{:S(2)}) copy-start(bf16[1,256,1024]{2,1,0:T(8,128)(2,1)} %param.29) | copy-start | bytes 1572868
  461.9 284.7 %copy-start.10 = (f32[256,1024]{1,0:T(8,128)S(1)}, f32[256,1024]{1,0:T(8,128)}, u32[]{:S(2)}) copy-start(f32[256,1024]{1,0:T(8,128)} %copy-done.9) | copy-start | bytes 3145732
  461.9 284.7 %copy-start.19 = (bf16[16,64,256]{2,1,0:T(8,128)(2,1)S(1)}, bf16[16,64,256]{2,1,0:T(8,128)(2,1)}, u32[]{:S(2)}) copy-start(bf16[16,64,256]{2,1,0:T(8,128)(2,1)} %get-tuple-element.116) | copy-start | bytes 1572868
  461.9 284.7 %copy-start.21 = (bf16[256,1024]{0,1:T(8,128)(2,1)S(1)}, bf16[256,1024]{0,1:T(8,128)(2,1)}, u32[]{:S(2)}) copy-start(bf16[256,1024]{0,1:T(8,128)(2,1)} %copy-done.20) | copy-start | bytes 1572868
  461.9 284.7 %copy-start.23 = (bf16[256,1024]{0,1:T(8,128)(2,1)S(1)}, bf16[256,1024]{0,1:T(8,128)(2,1)}, u32[]{:S(2)}) copy-start(bf16[256,1024]{0,1:T(8,128)(2,1)} %copy-done.22) | copy-start | bytes 1572868
  461.9 365.7 %all-reduce.14.cloned.1.call-start = ((), (), s32[]{:S(2)}) async-start(), calls=%async_computation.16 | async-start | bytes 6291456 | tf_op jit(solution)/shard_map/psum | solution.py:259
  827.6 7.2 copy-start.18
Sparse Core Ops, SparseCore 0:
  9.9 48.2 all-gather.17
  64.4 45.9 all-gather.27
  112.5 44.6 all-gather.25
  158.9 26.5 all-gather.19
  187.3 54.3 all-gather.21
  243.4 54.3 all-gather.23
  351.0 76.7 reduce-scatter.7
  444.6 62.3 reduce-scatter.15
  510.8 41.1 reduce-scatter.9
  555.7 71.2 reduce-scatter.11
  630.5 71.2 reduce-scatter.13
  705.0 122.5 all-reduce.13
where the time goes:
time: 848 us; the launch traced here: 843 us
  waiting for transfers between devices  548 us (65%)
  blocking collectives  115 us (14%)
  matrix products  105 us (12%)
  local copies, waits for them, and re-layouts  35.4 us (4%)
  other arithmetic  24 us (3%)
  between operations  16.3 us (2%)
    psum x1, waiting for transfers between devices, per_device(): lax.psum(owned[0].astype(jnp.bfloat16), 'ctx').astype(jnp.float32)  75.4 us
    reduce_scatter x1, waiting for transfers between devices, per_device(): lax.psum_scatter(grad_up.astype(jnp.bfloat16), 'fsdp', scatter_dimension=...  75 us
    reduce_scatter x1, waiting for transfers between devices, per_device(): lax.psum_scatter(grad_down.astype(jnp.bfloat16), 'fsdp', scatter_dimensio...  74.8 us
    reduce_scatter x1, waiting for transfers between devices, per_device(): lax.psum_scatter(key_terms.astype(jnp.bfloat16), 'ctx', scatter_dimension...  69.9 us
    all_gather x1, waiting for transfers between devices, per_device(): lax.all_gather(w_up, 'fsdp', axis=0, tiled=True)  53.2 us
    unnamed x13, waiting for transfers between devices  47.3 us
    reduce_scatter x1, waiting for transfers between devices, per_device(): lax.psum_scatter(grad_out_weight.astype(jnp.bfloat16), 'fsdp', scatter_di...  42.8 us
    all_gather x1, waiting for transfers between devices, per_device(): lax.all_gather(w_down, 'fsdp', axis=0, tiled=True)  39.8 us
  transfers between devices with their start and end apart: 12, of which 11 were waited for; matrix products, arithmetic and copies ran while one was open for 9% of the time, Pallas kernels for 0%

commit v1 on v0

v1 whole, which is shorter than its diff:
```python
import jax
import jax.numpy as jnp
from jax import lax
from jax.sharding import PartitionSpec as P

HEADS = 16
HEAD_DIM = 64


norm_eps = 1e-05


def layer_norm(inputs, gain, shift):
    center = inputs - jnp.mean(inputs, axis=-1, keepdims=True)
    variance = jnp.mean(center * center, axis=-1, keepdims=True)
    return center * lax.rsqrt(variance + norm_eps) * gain + shift


def gelu_exact(hidden):
    return jax.nn.gelu(hidden, approximate=False)


def swap(value, axis, mask):
    size = lax.axis_size(axis)
    return lax.ppermute(value, axis, [(at, at ^ mask) for at in range(size)])


def add(first, second):
    return (first.astype(jnp.float32) + second.astype(jnp.float32)).astype(jnp.bfloat16)


def bits_of(axis):
    return lax.axis_size(axis).bit_length() - 1


def two_ways(bits):
    outer = list(range(1, bits))
    return (outer + [0], outer[::-1] + [0])


def gather_half(shard, order):
    held, done = shard[None], []
    for bit in order:
        other = swap(held, "fsdp", 1 << bit)
        done.append(bit)
        lower = sum(1 for at in done if at < bit)
        rest = held.shape[1:]
        inner = 1 << lower
        split = (held.shape[0] // inner, 1, inner) + rest
        held = jnp.concatenate((held.reshape(split), other.reshape(split)), axis=1)
        held = held.reshape((-1,) + rest)
    return held


def gather(shard):
    half = shard.shape[1] // 2
    first, second = two_ways(bits_of("fsdp"))
    whole = jnp.concatenate(
        (gather_half(shard[:, :half], first), gather_half(shard[:, half:], second)), axis=2
    )
    return whole.reshape(-1, shard.shape[1])


def ctx_total(value):
    me = lax.axis_index("ctx")
    gray = me ^ (me >> 1)
    bits = bits_of("ctx")
    for at in range(bits):
        half = value.shape[0] // 2
        mine = (gray >> at) & 1
        keep = lax.dynamic_slice_in_dim(value, mine * half, half, 0)
        send = lax.dynamic_slice_in_dim(value, (1 - mine) * half, half, 0)
        value = add(keep, swap(send, "ctx", (2 << at) - 1))
    for at in reversed(range(bits)):
        other = swap(value, "ctx", (2 << at) - 1)
        upper = ((gray >> at) & 1) == 1
        value = jnp.concatenate(
            (jnp.where(upper, other, value), jnp.where(upper, value, other)), axis=0
        )
    return value.astype(jnp.float32)


def reduce_grad(grad):
    count = lax.axis_size("fsdp")
    columns = grad.shape[1]
    half = columns // 2
    blocks = grad.astype(jnp.bfloat16).reshape(count, -1, columns)
    pairs = blocks.reshape(count // 2, 2, -1, columns)
    blocks = add(pairs[:, 0], swap(pairs[:, 1], "fsdp", 1))
    first, second = two_ways(bits_of("fsdp"))
    first = [bit - 1 for bit in first[:-1]]
    second = [bit - 1 for bit in second[:-1]]
    return jnp.concatenate(
        (
            ctx_total(scatter_outer(blocks[:, :, :half], first)),
            ctx_total(scatter_outer(blocks[:, :, half:], second)),
        ),
        axis=1,
    )


def scatter_outer(blocks, order):
    left = sorted(order)
    for bit in order:
        inner = 1 << left.index(bit)
        left.remove(bit)
        rest = blocks.shape[1:]
        parts = blocks.reshape((blocks.shape[0] // (2 * inner), 2, inner) + rest)
        came = swap(parts[:, 1], "fsdp", 2 << bit)
        blocks = add(parts[:, 0], came).reshape((-1,) + rest)
    return blocks[0]


def gray_mask(index):
    mask, at = 0, 0
    while index >> at:
        if (index >> at) & 1:
            mask ^= (2 << at) - 1
        at += 1
    return mask


def gather_tokens(rows):
    held = rows[None]
    for at in reversed(range(bits_of("ctx"))):
        other = swap(held, "ctx", (2 << at) - 1)
        held = interleave(held, other)
    return held


def interleave(held, other):
    rest = held.shape[1:]
    return jnp.stack((held, other), axis=1).reshape((-1,) + rest)


def scatter_tokens(blocks):
    while blocks.shape[0] > 1:
        at = bits_of("ctx") - (blocks.shape[0].bit_length() - 1)
        parts = blocks.reshape((-1, 2) + blocks.shape[1:])
        blocks = add(parts[:, 0], swap(parts[:, 1], "ctx", (2 << at) - 1))
    return blocks[0]


def reorder(value, count):
    me = lax.axis_index("fsdp")
    width = value.shape[1] // count
    return jnp.concatenate(
        [lax.dynamic_slice_in_dim(value, (me ^ at) * width, width, 1) for at in range(count)],
        axis=1,
    )


def dot(first, second):
    return jnp.dot(first, second, preferred_element_type=jnp.float32)


def dot_rows(first, second):
    return lax.dot_general(
        first, second, (((0,), (0,)), ((), ())), preferred_element_type=jnp.float32
    )


def dot_back(first, second):
    return lax.dot_general(
        first, second, (((1,), (1,)), ((), ())), preferred_element_type=jnp.float32
    )


def per_device(
    tokens,
    w_qkv,
    b_query,
    b_value,
    w_attn_out,
    b_attn_out,
    norm1_gain,
    norm1_shift,
    w_up,
    b_up,
    w_down,
    b_down,
    norm2_gain,
    norm2_shift,
    d_out,
):
    count = lax.axis_size("fsdp")
    seq_local, block_rows, width = tokens.shape
    row_count = seq_local * block_rows
    tok_rows = tokens.reshape(row_count, width)
    vectors = (
        b_query,
        b_value,
        b_attn_out,
        norm1_gain,
        norm1_shift,
        b_up,
        b_down,
        norm2_gain,
        norm2_shift,
    )
    packed = lax.all_gather(jnp.concatenate(vectors), "fsdp", axis=0, tiled=False)
    spread, start = [], 0
    for item in vectors:
        size = item.shape[0]
        spread.append(packed[:, start : start + size].reshape(-1).astype(jnp.float32))
        start += size
    (
        query_bias,
        value_bias,
        out_bias,
        gain_one,
        shift_one,
        up_bias,
        down_bias,
        gain_two,
        shift_two,
    ) = spread
    input_proj = gather(w_qkv)
    token_blocks = gather_tokens(tok_rows)
    out_weight = gather(w_attn_out)
    up_weight = gather(w_up)
    down_weight = gather(w_down)
    ctx_count = token_blocks.shape[0]
    score_scale = HEAD_DIM ** (-0.5)
    all_rows = reorder(token_blocks.reshape(ctx_count * row_count, width), count)
    own_rows = all_rows[:row_count]
    key_rows = ctx_count * block_rows

    def by_sequence(value):
        parts = value.reshape(ctx_count, seq_local, block_rows, HEADS, HEAD_DIM)
        return parts.transpose(1, 3, 0, 2, 4).reshape(seq_local, HEADS, key_rows, HEAD_DIM)

    def by_block(value):
        parts = value.reshape(seq_local, HEADS, ctx_count, block_rows, HEAD_DIM)
        return parts.transpose(2, 0, 3, 1, 4).reshape(ctx_count * row_count, width)

    def heads(value):
        return value.reshape(seq_local, block_rows, HEADS, HEAD_DIM).transpose(0, 2, 1, 3)

    def joined(value):
        return value.transpose(0, 2, 1, 3).reshape(row_count, width)

    queries = heads((dot(own_rows, input_proj[:, :width]) + query_bias).astype(jnp.bfloat16))
    kv_all = dot(all_rows, input_proj[:, width:])
    key_part = by_sequence(kv_all[:, :width].astype(jnp.bfloat16))
    value_part = by_sequence((kv_all[:, width:] + value_bias).astype(jnp.bfloat16))
    scores = (
        jnp.einsum("shqd,shkd->shqk", queries, key_part, preferred_element_type=jnp.float32)
        * score_scale
    )
    attn_prob = jax.nn.softmax(scores, axis=-1).astype(jnp.bfloat16)
    mixed_out = jnp.einsum(
        "shqk,shkd->shqd", attn_prob, value_part, preferred_element_type=jnp.float32
    )
    mixed_rows = joined(mixed_out)
    attn_in = reorder(mixed_rows.astype(jnp.bfloat16), count)
    attn_out = dot(attn_in, out_weight) + out_bias
    resid_one = tok_rows.astype(jnp.float32) + attn_out
    normed = layer_norm(resid_one, gain_one, shift_one)
    normed_low = reorder(normed.astype(jnp.bfloat16), count)
    hidden = dot(normed_low, up_weight) + up_bias
    activated = reorder(gelu_exact(hidden).astype(jnp.bfloat16), count)
    branch = dot(activated, down_weight) + down_bias
    resid_two = normed + branch
    result = layer_norm(resid_two, gain_two, shift_two)
    output = result.astype(jnp.bfloat16).reshape(seq_local, block_rows, width)
    cotangent = d_out.reshape(row_count, width).astype(jnp.float32)
    norm_pull = jax.vjp(layer_norm, resid_two, gain_two, shift_two)[1]
    grad_resid_two, grad_gain_two, grad_shift_two = norm_pull(cotangent)
    grad_branch = grad_resid_two.astype(jnp.bfloat16)
    sum_down = reduce_grad(dot_rows(activated, grad_branch))
    grad_down_bias = jnp.sum(grad_branch.astype(jnp.float32), axis=0)
    grad_act = reorder(dot_back(grad_branch, down_weight), count)
    grad_hidden = jax.vjp(gelu_exact, hidden)[1](grad_act)[0].astype(jnp.bfloat16)
    sum_up = reduce_grad(dot_rows(normed_low, grad_hidden))
    grad_up_bias = jnp.sum(grad_hidden.astype(jnp.float32), axis=0)
    grad_normed = grad_resid_two + reorder(dot_back(grad_hidden, up_weight), count)
    norm_pull_one = jax.vjp(layer_norm, resid_one, gain_one, shift_one)[1]
    grad_resid_one, grad_gain_one, grad_shift_one = norm_pull_one(grad_normed)
    grad_attn = grad_resid_one.astype(jnp.bfloat16)
    sum_out = reduce_grad(dot_rows(attn_in, grad_attn))
    grad_out_bias = jnp.sum(grad_attn.astype(jnp.float32), axis=0)
    grad_mixed = reorder(dot_back(grad_attn, out_weight).astype(jnp.bfloat16), count)
    grad_heads = heads(grad_mixed)
    row_delta = jnp.sum(grad_heads.astype(jnp.float32) * mixed_out, axis=-1, keepdims=True)
    grad_prob = jnp.einsum(
        "shqd,shkd->shqk", grad_heads, value_part, preferred_element_type=jnp.float32
    )
    grad_score = (attn_prob.astype(jnp.float32) * (grad_prob - row_delta)).astype(jnp.bfloat16)
    grad_value = jnp.einsum(
        "shqk,shqd->shkd", attn_prob, grad_heads, preferred_element_type=jnp.float32
    )
    grad_key = (
        jnp.einsum("shqk,shqd->shkd", grad_score, queries, preferred_element_type=jnp.float32)
        * score_scale
    )
    grad_query = (
        jnp.einsum("shqk,shkd->shqd", grad_score, key_part, preferred_element_type=jnp.float32)
        * score_scale
    )
    grad_queries = joined(grad_query).astype(jnp.bfloat16)
    grad_keys = by_block(grad_key).astype(jnp.bfloat16)
    grad_values = by_block(grad_value).astype(jnp.bfloat16)
    grad_kv = jnp.concatenate((grad_keys, grad_values), axis=1)
    grad_input_proj = jnp.concatenate(
        (dot_rows(own_rows, grad_queries), dot_rows(all_rows, grad_kv)), axis=1
    )
    sum_input = reduce_grad(grad_input_proj)
    grad_query_bias = jnp.sum(grad_queries.astype(jnp.float32), axis=0)
    grad_value_bias = jnp.sum(grad_values.astype(jnp.float32), axis=0)
    from_kv = dot_back(grad_kv, input_proj[:, width:])
    from_query = dot_back(grad_queries, input_proj[:, :width])
    from_kv = scatter_tokens(from_kv.astype(jnp.bfloat16).reshape(ctx_count, row_count, width))
    d_tokens = grad_resid_one + reorder(from_query + from_kv.astype(jnp.float32), count)
    small = (
        grad_query_bias,
        grad_value_bias,
        grad_out_bias,
        grad_gain_one,
        grad_shift_one,
        grad_up_bias,
        grad_down_bias,
        grad_gain_two,
        grad_shift_two,
    )
    small_all = lax.psum(
        jnp.concatenate([item.reshape(count, -1) for item in small], axis=1), ("fsdp", "ctx")
    )
    small_own = lax.dynamic_index_in_dim(small_all, lax.axis_index("fsdp"), 0, keepdims=False)
    owned, start = [], 0
    for item in small:
        size = item.shape[0] // count
        owned.append(small_own[start : start + size])
        start += size
    return (
        output,
        d_tokens.reshape(seq_local, block_rows, width),
        sum_input,
        owned[0],
        owned[1],
        sum_out,
        owned[2],
        owned[3],
        owned[4],
        sum_up,
        owned[5],
        sum_down,
        owned[6],
        owned[7],
        owned[8],
    )


def solution(mesh):
    placed = (
        P("fsdp", "ctx", None),
        P("fsdp", None),
        P("fsdp"),
        P("fsdp"),
        P("fsdp", None),
        P("fsdp"),
        P("fsdp"),
        P("fsdp"),
        P("fsdp", None),
        P("fsdp"),
        P("fsdp", None),
        P("fsdp"),
        P("fsdp"),
        P("fsdp"),
        P("fsdp", "ctx", None),
    )
    return jax.shard_map(
        per_device,
        mesh=mesh,
        in_specs=placed,
        out_specs=(
            P("fsdp", "ctx", None),
            P("fsdp", "ctx", None),
            P("fsdp", None),
            P("fsdp"),
            P("fsdp"),
            P("fsdp", None),
            P("fsdp"),
            P("fsdp"),
            P("fsdp"),
            P("fsdp", None),
            P("fsdp"),
            P("fsdp", None),
            P("fsdp"),
            P("fsdp"),
            P("fsdp"),
        ),
        check_vma=False,
    )
```

time: 848 us -> 610 us (0.72)
  waiting for transfers between devices: 548 us -> 163 us
  starting transfers between devices: 0.66 us -> 108 us
  other arithmetic: 24 us -> 91.1 us
  blocking collectives: 115 us -> 49.9 us
  local copies, waits for them, and re-layouts: 35.4 us -> 100 us
  matrix products: 105 us -> 90.3 us
  between operations: 16.3 us -> 3.08 us
    reduce_scatter x4 -> x0, waiting for transfers between devices: 262 us -> none  [the longest x1 75 us: per_device(): lax.psum_scatter(grad_up.astype(jnp.bfloat16), 'fsdp', scatter_dimension=...]
    ppermute x0 -> x80, waiting for transfers between devices: none -> 163 us  [swap(): return lax.ppermute(value, axis, [(at, at ^ mask) for at in range(size)])]
    all_gather x6 -> x0, waiting for transfers between devices: 163 us -> none  [the longest x1 53.2 us: per_device(): lax.all_gather(w_up, 'fsdp', axis=0, tiled=True)]
    ppermute x0 -> x80, starting transfers between devices: none -> 108 us  [swap(): return lax.ppermute(value, axis, [(at, at ^ mask) for at in range(size)])]
    psum x1 -> x0, waiting for transfers between devices: 75.4 us -> none  [per_device(): lax.psum(owned[0].astype(jnp.bfloat16), 'ctx').astype(jnp.float32)]
    all_gather x9 -> x1, blocking collectives: 77.4 us -> 9.76 us  [per_device(): lax.all_gather(jnp.concatenate(vectors), 'fsdp', axis=0, tiled=False)]
    unnamed x13 -> x0, waiting for transfers between devices: 47.3 us -> none
    concatenate x0 -> x28, other arithmetic: none -> 34.3 us  [the longest x16 28.9 us: gather_half(): held = jnp.concatenate((held.reshape(split), other.reshape(split)), axis=1)]
  transfers between devices with their start and end apart: 12 -> 80, of which waited for: 11 -> 40; matrix products, arithmetic and copies ran while one was open for 9% -> 29% of each run, Pallas kernels for 0% -> 0%
where the time goes in v1:
time: 610 us; the launch traced here: 606 us
  waiting for transfers between devices  163 us (27%)
  starting transfers between devices  108 us (18%)
  local copies, waits for them, and re-layouts  100 us (16%)
  other arithmetic  91.1 us (15%)
  matrix products  90.3 us (15%)
  blocking collectives  49.9 us (8%)
    ppermute x80, waiting for transfers between devices, swap(): return lax.ppermute(value, axis, [(at, at ^ mask) for at in range(size)])  163 us
    ppermute x80, starting transfers between devices, swap(): return lax.ppermute(value, axis, [(at, at ^ mask) for at in range(size)])  108 us
    psum x1, blocking collectives, per_device(): lax.psum(jnp.concatenate([item.reshape(count, -1) for item in small], axi...  40.2 us
    unnamed x208, local copies, waits for them, and re-layouts  36.4 us
    concatenate x16, other arithmetic, gather_half(): held = jnp.concatenate((held.reshape(split), other.reshape(split)), axis=1)  28.9 us
    dot_general x5, matrix products, dot(): return jnp.dot(first, second, preferred_element_type=jnp.float32)  24.3 us
    dot_general x5, matrix products, dot_rows(): lax.dot_general(first, second, (((0,), (0,)), ((), ())), preferred_elemen...  19.2 us
    dot_general x5, matrix products, dot_back(): lax.dot_general(first, second, (((1,), (1,)), ((), ())), preferred_elemen...  18 us
  transfers between devices with their start and end apart: 80, of which 40 were waited for; matrix products, arithmetic and copies ran while one was open for 29% of the time, Pallas kernels for 0%

profile of v1, /device:TPU:0, one launch (start us, length us, event | category | flops | bytes accessed | tf_op | source)
XLA Modules:
  0.0 605.8 jit_solution(9726957013842913960)
XLA Ops:
  2.8 2.9 collective-permute-start.2
  5.7 3.6 collective-permute-start
  21.1 9.8 %all-gather.1 = bf16[8,1,1536]{2,1,0:T(2,128)(2,1)S(1)} all-gather(bf16[1,1,1536]{2,1,0:T(2,128)(2,1)S(1)} %reshape.885), channel_id=2, replica_groups=mesh['ctx'=4,'fsdp'=8] {'fsdp'}, dimensions={0}, use_global_device_ids=true | all-gather | bytes 27648 | tf_op jit(solution)/shard_map/all_gather | solution.py:201
  42.5 4.4 collective-permute-done.12
  55.9 6.2 %collective-permute-done.17 = bf16[1,128,2048]{2,1,0:T(8,128)(2,1)S(1)} collective-permute-done((bf16[1,128,2048]{2,1,0:T(8,128)(2,1)}, bf16[1,128,2048]{2,1,0:T(8,128)(2,1)S(1)}, u32[]{:S(2)}, u32[]{:S(2)}) %collective-permute-start.17) | collective-permute-done | bytes 524320 | tf_op jit(solution)/shard_map/ppermute | solution.py:25
  63.1 8.9 %collective-permute-done.23 = bf16[1,512,512]{2,1,0:T(8,128)(2,1)S(1)} collective-permute-done((bf16[1,512,512]{2,1,0:T(8,128)(2,1)}, bf16[1,512,512]{2,1,0:T(8,128)(2,1)S(1)}, u32[]{:S(2)}, u32[]{:S(2)}) %collective-permute-start.23) | collective-permute-done | bytes 524320 | tf_op jit(solution)/shard_map/ppermute | solution.py:25
  82.8 9.7 %collective-permute-done.3 = bf16[2,128,1536]{2,1,0:T(8,128)(2,1)S(1)} collective-permute-done((bf16[2,128,1536]{2,1,0:T(8,128)(2,1)S(1)}, bf16[2,128,1536]{2,1,0:T(8,128)(2,1)S(1)}, u32[]{:S(2)}, u32[]{:S(2)}) %collective-permute-start.3) | collective-permute-done | bytes 786464 | tf_op jit(solution)/shard_map/ppermute | solution.py:25
  96.2 4.3 collective-permute-done.1
  101.7 16.0 %collective-permute-done.18 = bf16[2,128,2048]{2,1,0:T(8,128)(2,1)S(1)} collective-permute-done((bf16[2,128,2048]{2,1,0:T(8,128)(2,1)S(1)}, bf16[2,128,2048]{2,1,0:T(8,128)(2,1)S(1)}, u32[]{:S(2)}, u32[]{:S(2)}) %collective-permute-start.18) | collective-permute-done | bytes 1048608 | tf_op jit(solution)/shard_map/ppermute | solution.py:25
  121.5 3.2 pad_maximum_fusion.19
  125.2 2.9 pad_maximum_fusion.18
  128.1 9.4 %collective-permute-done.24 = bf16[2,512,512]{2,1,0:T(8,128)(2,1)} collective-permute-done((bf16[2,512,512]{2,1,0:T(8,128)(2,1)}, bf16[2,512,512]{2,1,0:T(8,128)(2,1)}, u32[]{:S(2)}, u32[]{:S(2)}) %collective-permute-start.24) | collective-permute-done | bytes 1048608 | tf_op jit(solution)/shard_map/ppermute | solution.py:25
  140.8 2.8 pad_maximum_fusion.20
  151.6 2.8 copy-done.21
  155.1 4.5 fusion.35
  159.6 3.3 copy-done.8
  164.6 3.0 copy.81
  167.6 2.8 reshape.787
  170.4 4.5 reshape.788
  174.8 4.1 fusion.14
  178.9 2.9 copy.82
  181.8 2.8 reshape.789
  184.6 3.2 reshape.790
  187.8 9.8 %fusion.140 = (f32[16,256]{1,0:T(8,128)S(1)}, f32[16,256,1024]{2,1,0:T(8,128)}) fusion(bf16[16,256,64]{1,2,0:T(8,128)(2,1)S(1)} %bitcast.663, bf16[16,1024,64]{1,2,0:T(8,128)(2,1)} %reshape.788), kind=kOutput, calls=%fused_computation.469 | convolution fusion | flops 549454848 | bytes 19415040 | tf_op jit(solution)/shard_map/sub | solution.py:251
  197.7 6.9 %divide_convert_fusion = bf16[16,256,1024]{2,1,0:T(8,128)(2,1)S(1)} fusion(f32[16,256,1024]{2,1,0:T(8,128)} %get-tuple-element.133, f32[16,256]{1,0:T(8,128)S(1)} %get-tuple-element.132), kind=kLoop, calls=%fused_computation.2 | loop fusion | flops 8388608 | bytes 25182208 | tf_op jit(solution)/shard_map/convert_element_type | solution.py:251
  204.7 3.6 fusion.141
  210.6 2.8 pad_maximum_fusion.10
  216.4 14.7 %multiply_convert_fusion.2 = (bf16[256,4096]{1,0:T(8,128)(2,1)S(1)}, f32[256,4096]{1,0:T(8,128)}, f32[256,4096]{1,0:T(8,128)}) fusion(f32[4096]{0:T(1024)S(1)} %bitcast.710, bf16[256,1024]{1,0:T(8,128)(2,1)S(1)} %constant_dynamic-update-slice_fusion.8, bf16[1024,2048]{1,0:T(8,128)(2,1)S(1)} %bitcast.655, bf16[1024,2048]{1,0:T(8,128)(2,1)S(1)} %bitcast.657), kind=kOutput, calls=%fused_computation.42 | convolution fusion | flops 2233466880 | bytes 19415040 | tf_op jit(solution)/shard_map/dot_general | solution.py:154
  234.3 3.4 pad_maximum_fusion.11
  242.4 6.8 %fusion.8 = f32[256,4096]{1,0:T(8,128)} fusion(bf16[256,1024]{1,0:T(8,128)(2,1)S(1)} %get-tuple-element.21, bf16[4096,512]{1,0:T(8,128)(2,1)S(1)} %bitcast.660, bf16[4096,512]{1,0:T(8,128)(2,1)} %bitcast.662), kind=kOutput, calls=%fused_computation.20 | convolution fusion | flops 2164260864 | bytes 13107200 | tf_op jit(solution)/shard_map/dot_general | solution.py:164
  254.5 3.5 convert_reduce_fusion
  270.8 5.7 multiply_convert_fusion
  276.5 5.2 convert_reduce_fusion.5
  283.9 2.9 convert_reduce_fusion.1
  299.8 7.1 %convolution_convert_fusion.6 = bf16[1024,1024]{1,0:T(8,128)(2,1)S(1)} fusion(bf16[1024,2048]{0,1:T(8,128)(2,1)} %constant_dynamic-update-slice_fusion.32, bf16[1024,1536]{1,0:T(8,128)(2,1)S(1)} %bitcast.670, bf16[1024,1536]{1,0:T(8,128)(2,1)S(1)} %bitcast.667), kind=kOutput, calls=%fused_computation.85 | convolution fusion | flops 4304404480 | bytes 12582912 | tf_op jit(solution)/shard_map/dot_general | solution.py:164
  307.0 5.0 convolution_convert_fusion.2
  315.2 5.7 convolution_convert_fusion.1
  320.9 5.7 convolution_convert_fusion
  333.3 4.6 slice_bitcast_fusion.2
  338.4 4.7 slice_bitcast_fusion
  343.2 40.2 %psum.7 = f32[8,1536]{1,0:T(8,128)S(1)} all-reduce(f32[8,1536]{1,0:T(8,128)S(1)} %constant_dynamic-update-slice_fusion.42), channel_id=1, replica_groups=mesh['ctx'=4,'fsdp'=8] {'fsdp','ctx'}, use_global_device_ids=true, to_apply=%region_20.21 | all-reduce | flops 12288 | bytes 98304 | tf_op jit(solution)/shard_map/psum | solution.py:326
  396.1 4.6 collective-permute-done.42
  402.8 2.9 collective-permute-done.49
  407.8 2.9 collective-permute-done.43
  421.8 3.1 collective-permute-done.51
  427.6 3.2 collective-permute-done.45
  441.3 2.8 fusion.7
  449.0 13.1 %collective-permute-done.35 = bf16[1,2,128,1536]{3,2,1,0:T(8,128)(2,1)S(1)} collective-permute-done((bf16[1,2,128,1536]{3,2,1,0:T(8,128)(2,1)S(1)}, bf16[1,2,128,1536]{3,2,1,0:T(8,128)(2,1)S(1)}, u32[]{:S(2)}, u32[]{:S(2)}) %collective-permute-start.35) | collective-permute-done | bytes 786464 | tf_op jit(solution)/shard_map/ppermute | solution.py:25
  468.5 3.9 fusion.5
  476.1 4.3 fusion.4
  485.9 4.8 collective-permute-done.37
  491.5 5.5 collective-permute-done.31
  497.0 3.2 collective-permute-start.38
  500.2 3.2 collective-permute-done.38
  503.4 3.2 collective-permute-start.32
  506.6 3.2 collective-permute-done.32
  509.8 3.2 collective-permute-start.39
  513.1 3.3 collective-permute-done.39
  516.4 3.2 collective-permute-start.33
  519.6 4.3 collective-permute-done.33
  523.9 7.8 %collective-permute-done.40 = bf16[64,1536]{1,0:T(8,128)(2,1)S(1)} collective-permute-done((bf16[64,1536]{1,0:T(8,128)(2,1)S(1)}, bf16[64,1536]{1,0:T(8,128)(2,1)S(1)}, u32[]{:S(2)}, u32[]{:S(2)}) %collective-permute-start.40) | collective-permute-done | bytes 196640 | tf_op jit(solution)/shard_map/ppermute | solution.py:25
  531.8 9.5 %collective-permute-done.34 = bf16[64,1536]{1,0:T(8,128)(2,1)S(1)} collective-permute-done((bf16[64,1536]{1,0:T(8,128)(2,1)S(1)}, bf16[64,1536]{1,0:T(8,128)(2,1)S(1)}, u32[]{:S(2)}, u32[]{:S(2)}) %collective-permute-start.34) | collective-permute-done | bytes 196640 | tf_op jit(solution)/shard_map/ppermute | solution.py:25
  562.0 6.7 %collective-permute-start.64 = (bf16[32,2048]{1,0:T(8,128)(2,1)S(1)}, bf16[32,2048]{1,0:T(8,128)(2,1)S(1)}, u32[]{:S(2)}, u32[]{:S(2)}) collective-permute-start(bf16[32,2048]{1,0:T(8,128)(2,1)S(1)} %constant_dynamic-slice_fusion.3), channel_id=1, source_target_pairs={{0,24},{8,16},{16,8},{24,0},{1,25},{9,17},{17,9},{25,1},{2,26},{10... | collective-permute-start | bytes 393224 | tf_op jit(solution)/shard_map/ppermute | solution.py:25
  584.6 6.5 %collective-permute-start.66 = (bf16[64,2048]{1,0:T(8,128)(2,1)S(1)}, bf16[64,2048]{1,0:T(8,128)(2,1)S(1)}, u32[]{:S(2)}, u32[]{:S(2)}) collective-permute-start(bf16[64,2048]{1,0:T(8,128)(2,1)S(1)} %pad_maximum_fusion.48), channel_id=1, source_target_pairs={{0,8},{8,0},{16,24},{24,16},{1,9},{9,1},{17,25},{25,17},{2,10},{10... | collective-permute-start | bytes 786440 | tf_op jit(solution)/shard_map/ppermute | solution.py:25
  (526 shorter events, 238.2 us)
Async XLA Ops:
  2.8 47.4 %collective-permute-start.2 = (bf16[1,128,1536]{2,1,0:T(8,128)(2,1)}, bf16[1,128,1536]{2,1,0:T(8,128)(2,1)}, u32[]{:S(2)}, u32[]{:S(2)}) collective-permute-start(bf16[1,128,1536]{2,1,0:T(8,128)(2,1)} %get-tuple-element.71), channel_id=1, source_target_pairs={{0,2},{1,3},{2,0},{3,1},{4,6},{5,7},{6,4},{7,5},{8,10},{9,11},{10,... | collective-permute-start | bytes 1179656 | tf_op jit(solution)/shard_map/ppermute | solution.py:25
  5.7 48.9 %collective-permute-start = (bf16[1,256,1024]{2,1,0:T(8,128)(2,1)}, bf16[1,256,1024]{2,1,0:T(8,128)(2,1)}, u32[]{:S(2)}, u32[]{:S(2)}) collective-permute-start(bf16[1,256,1024]{2,1,0:T(8,128)(2,1)} %param.15), channel_id=1, source_target_pairs={{0,24},{8,16},{16,8},{24,0},{1,25},{9,17},{17,9},{25,1},{2,26},{10... | collective-permute-start | bytes 1572872 | tf_op jit(solution)/shard_map/ppermute | solution.py:25
  9.3 43.7 %collective-permute-start.5 = (bf16[1,128,1536]{2,1,0:T(8,128)(2,1)}, bf16[1,128,1536]{2,1,0:T(8,128)(2,1)}, u32[]{:S(2)}, u32[]{:S(2)}) collective-permute-start(bf16[1,128,1536]{2,1,0:T(8,128)(2,1)} %get-tuple-element.72), channel_id=1, source_target_pairs={{0,4},{1,5},{2,6},{3,7},{4,0},{5,1},{6,2},{7,3},{8,12},{9,13},{10,... | collective-permute-start | bytes 1179656 | tf_op jit(solution)/shard_map/ppermute | solution.py:25
  12.5 23.7 %collective-permute-start.11 = (bf16[1,128,512]{2,1,0:T(8,128)(2,1)}, bf16[1,128,512]{2,1,0:T(8,128)(2,1)}, u32[]{:S(2)}, u32[]{:S(2)}) collective-permute-start(bf16[1,128,512]{2,1,0:T(8,128)(2,1)} %get-tuple-element.100), channel_id=1, source_target_pairs={{0,4},{1,5},{2,6},{3,7},{4,0},{5,1},{6,2},{7,3},{8,12},{9,13},{10,... | collective-permute-start | bytes 393224 | tf_op jit(solution)/shard_map/ppermute | solution.py:25
  13.1 27.2 %collective-permute-start.8 = (bf16[1,128,512]{2,1,0:T(8,128)(2,1)}, bf16[1,128,512]{2,1,0:T(8,128)(2,1)}, u32[]{:S(2)}, u32[]{:S(2)}) collective-permute-start(bf16[1,128,512]{2,1,0:T(8,128)(2,1)} %get-tuple-element.99), channel_id=1, source_target_pairs={{0,2},{1,3},{2,0},{3,1},{4,6},{5,7},{6,4},{7,5},{8,10},{9,11},{10,... | collective-permute-start | bytes 393224 | tf_op jit(solution)/shard_map/ppermute | solution.py:25
  38.1 8.9 %collective-permute-start.12 = (bf16[2,128,512]{2,1,0:T(8,128)(2,1)}, bf16[2,128,512]{2,1,0:T(8,128)(2,1)}, u32[]{:S(2)}, u32[]{:S(2)}) collective-permute-start(bf16[2,128,512]{2,1,0:T(8,128)(2,1)} %get-tuple-element.103), channel_id=1, source_target_pairs={{0,2},{1,3},{2,0},{3,1},{4,6},{5,7},{6,4},{7,5},{8,10},{9,11},{10,... | collective-permute-start | bytes 786440 | tf_op jit(solution)/shard_map/ppermute | solution.py:25
  41.2 8.5 %collective-permute-start.9 = (bf16[2,128,512]{2,1,0:T(8,128)(2,1)S(1)}, bf16[2,128,512]{2,1,0:T(8,128)(2,1)S(1)}, u32[]{:S(2)}, u32[]{:S(2)}) collective-permute-start(bf16[2,128,512]{2,1,0:T(8,128)(2,1)S(1)} %get-tuple-element.97), channel_id=1, source_target_pairs={{0,4},{1,5},{2,6},{3,7},{4,0},{5,1},{6,2},{7,3},{8,12},{9,13},{10,... | collective-permute-start | bytes 786440 | tf_op jit(solution)/shard_map/ppermute | solution.py:25
  47.0 15.1 %collective-permute-start.17 = (bf16[1,128,2048]{2,1,0:T(8,128)(2,1)}, bf16[1,128,2048]{2,1,0:T(8,128)(2,1)S(1)}, u32[]{:S(2)}, u32[]{:S(2)}) collective-permute-start(bf16[1,128,2048]{2,1,0:T(8,128)(2,1)} %get-tuple-element.60), channel_id=1, source_target_pairs={{0,4},{1,5},{2,6},{3,7},{4,0},{5,1},{6,2},{7,3},{8,12},{9,13},{10,... | collective-permute-start | bytes 1572872 | tf_op jit(solution)/shard_map/ppermute | solution.py:25
  49.8 27.3 %collective-permute-start.14 = (bf16[1,128,2048]{2,1,0:T(8,128)(2,1)}, bf16[1,128,2048]{2,1,0:T(8,128)(2,1)S(1)}, u32[]{:S(2)}, u32[]{:S(2)}) collective-permute-start(bf16[1,128,2048]{2,1,0:T(8,128)(2,1)} %get-tuple-element.59), channel_id=1, source_target_pairs={{0,2},{1,3},{2,0},{3,1},{4,6},{5,7},{6,4},{7,5},{8,10},{9,11},{10,... | collective-permute-start | bytes 1572872 | tf_op jit(solution)/shard_map/ppermute | solution.py:25
  50.2 21.8 %collective-permute-start.23 = (bf16[1,512,512]{2,1,0:T(8,128)(2,1)}, bf16[1,512,512]{2,1,0:T(8,128)(2,1)S(1)}, u32[]{:S(2)}, u32[]{:S(2)}) collective-permute-start(bf16[1,512,512]{2,1,0:T(8,128)(2,1)} %get-tuple-element.52), channel_id=1, source_target_pairs={{0,4},{1,5},{2,6},{3,7},{4,0},{5,1},{6,2},{7,3},{8,12},{9,13},{10,... | collective-permute-start | bytes 1572872 | tf_op jit(solution)/shard_map/ppermute | solution.py:25
  53.0 21.7 %collective-permute-start.20 = (bf16[1,512,512]{2,1,0:T(8,128)(2,1)S(1)}, bf16[1,512,512]{2,1,0:T(8,128)(2,1)S(1)}, u32[]{:S(2)}, u32[]{:S(2)}) collective-permute-start(bf16[1,512,512]{2,1,0:T(8,128)(2,1)S(1)} %copy-done.43), channel_id=1, source_target_pairs={{0,2},{1,3},{2,0},{3,1},{4,6},{5,7},{6,4},{7,5},{8,10},{9,11},{10,... | collective-permute-start | bytes 1572872 | tf_op jit(solution)/shard_map/ppermute | solution.py:25
  54.6 24.0 %collective-permute-start.13 = (bf16[4,128,512]{2,1,0:T(8,128)(2,1)S(1)}, bf16[4,128,512]{2,1,0:T(8,128)(2,1)S(1)}, u32[]{:S(2)}, u32[]{:S(2)}) collective-permute-start(bf16[4,128,512]{2,1,0:T(8,128)(2,1)S(1)} %bitcast.684), channel_id=1, source_target_pairs={{0,1},{1,0},{2,3},{3,2},{4,5},{5,4},{6,7},{7,6},{8,9},{9,8},{10,11... | collective-permute-start | bytes 1572872 | tf_op jit(solution)/shard_map/ppermute | solution.py:25
  62.0 18.9 %collective-permute-start.10 = (bf16[4,128,512]{2,1,0:T(8,128)(2,1)S(1)}, bf16[4,128,512]{2,1,0:T(8,128)(2,1)S(1)}, u32[]{:S(2)}, u32[]{:S(2)}) collective-permute-start(bf16[4,128,512]{2,1,0:T(8,128)(2,1)S(1)} %bitcast.686), channel_id=1, source_target_pairs={{0,1},{1,0},{2,3},{3,2},{4,5},{5,4},{6,7},{7,6},{8,9},{9,8},{10,11... | collective-permute-start | bytes 1572872 | tf_op jit(solution)/shard_map/ppermute | solution.py:25
  72.0 20.5 %collective-permute-start.3 = (bf16[2,128,1536]{2,1,0:T(8,128)(2,1)S(1)}, bf16[2,128,1536]{2,1,0:T(8,128)(2,1)S(1)}, u32[]{:S(2)}, u32[]{:S(2)}) collective-permute-start(bf16[2,128,1536]{2,1,0:T(8,128)(2,1)S(1)} %get-tuple-element.75), channel_id=1, source_target_pairs={{0,4},{1,5},{2,6},{3,7},{4,0},{5,1},{6,2},{7,3},{8,12},{9,13},{10,... | collective-permute-start | bytes 2359304 | tf_op jit(solution)/shard_map/ppermute | solution.py:25
  74.7 20.5 %collective-permute-start.6 = (bf16[2,128,1536]{2,1,0:T(8,128)(2,1)S(1)}, bf16[2,128,1536]{2,1,0:T(8,128)(2,1)S(1)}, u32[]{:S(2)}, u32[]{:S(2)}) collective-permute-start(bf16[2,128,1536]{2,1,0:T(8,128)(2,1)S(1)} %get-tuple-element.69), channel_id=1, source_target_pairs={{0,2},{1,3},{2,0},{3,1},{4,6},{5,7},{6,4},{7,5},{8,10},{9,11},{10,... | collective-permute-start | bytes 2359304 | tf_op jit(solution)/shard_map/ppermute | solution.py:25
  77.0 23.4 %collective-permute-start.1 = (bf16[2,256,1024]{2,1,0:T(8,128)(2,1)S(1)}, bf16[2,256,1024]{2,1,0:T(8,128)(2,1)S(1)}, u32[]{:S(2)}, u32[]{:S(2)}) collective-permute-start(bf16[2,256,1024]{2,1,0:T(8,128)(2,1)S(1)} %get-tuple-element.65), channel_id=1, source_target_pairs={{0,8},{8,0},{16,24},{24,16},{1,9},{9,1},{17,25},{25,17},{2,10},{10... | collective-permute-start | bytes 3145736 | tf_op jit(solution)/shard_map/ppermute | solution.py:25
  78.5 39.1 %collective-permute-start.18 = (bf16[2,128,2048]{2,1,0:T(8,128)(2,1)S(1)}, bf16[2,128,2048]{2,1,0:T(8,128)(2,1)S(1)}, u32[]{:S(2)}, u32[]{:S(2)}) collective-permute-start(bf16[2,128,2048]{2,1,0:T(8,128)(2,1)S(1)} %get-tuple-element.63), channel_id=1, source_target_pairs={{0,2},{1,3},{2,0},{3,1},{4,6},{5,7},{6,4},{7,5},{8,10},{9,11},{10,... | collective-permute-start | bytes 3145736 | tf_op jit(solution)/shard_map/ppermute | solution.py:25
  80.9 43.8 %collective-permute-start.15 = (bf16[2,128,2048]{2,1,0:T(8,128)(2,1)}, bf16[2,128,2048]{2,1,0:T(8,128)(2,1)}, u32[]{:S(2)}, u32[]{:S(2)}) collective-permute-start(bf16[2,128,2048]{2,1,0:T(8,128)(2,1)} %get-tuple-element.57), channel_id=1, source_target_pairs={{0,4},{1,5},{2,6},{3,7},{4,0},{5,1},{6,2},{7,3},{8,12},{9,13},{10,... | collective-permute-start | bytes 3145736 | tf_op jit(solution)/shard_map/ppermute | solution.py:25
  92.5 45.0 %collective-permute-start.24 = (bf16[2,512,512]{2,1,0:T(8,128)(2,1)}, bf16[2,512,512]{2,1,0:T(8,128)(2,1)}, u32[]{:S(2)}, u32[]{:S(2)}) collective-permute-start(bf16[2,512,512]{2,1,0:T(8,128)(2,1)} %get-tuple-element.55), channel_id=1, source_target_pairs={{0,2},{1,3},{2,0},{3,1},{4,6},{5,7},{6,4},{7,5},{8,10},{9,11},{10,... | collective-permute-start | bytes 3145736 | tf_op jit(solution)/shard_map/ppermute | solution.py:25
  95.2 45.1 %collective-permute-start.21 = (bf16[2,512,512]{2,1,0:T(8,128)(2,1)}, bf16[2,512,512]{2,1,0:T(8,128)(2,1)}, u32[]{:S(2)}, u32[]{:S(2)}) collective-permute-start(bf16[2,512,512]{2,1,0:T(8,128)(2,1)} %get-tuple-element.49), channel_id=1, source_target_pairs={{0,4},{1,5},{2,6},{3,7},{4,0},{5,1},{6,2},{7,3},{8,12},{9,13},{10,... | collective-permute-start | bytes 3145736 | tf_op jit(solution)/shard_map/ppermute | solution.py:25
  100.4 43.2 %collective-permute-start.4 = (bf16[4,128,1536]{2,1,0:T(8,128)(2,1)S(1)}, bf16[4,128,1536]{2,1,0:T(8,128)(2,1)}, u32[]{:S(2)}, u32[]{:S(2)}) collective-permute-start(bf16[4,128,1536]{2,1,0:T(8,128)(2,1)S(1)} %bitcast.647), channel_id=1, source_target_pairs={{0,1},{1,0},{2,3},{3,2},{4,5},{5,4},{6,7},{7,6},{8,9},{9,8},{10,11... | collective-permute-start | bytes 4718600 | tf_op jit(solution)/shard_map/ppermute | solution.py:25
  118.6 31.1 %collective-permute-start.7 = (bf16[4,128,1536]{2,1,0:T(8,128)(2,1)S(1)}, bf16[4,128,1536]{2,1,0:T(8,128)(2,1)}, u32[]{:S(2)}, u32[]{:S(2)}) collective-permute-start(bf16[4,128,1536]{2,1,0:T(8,128)(2,1)S(1)} %bitcast.649), channel_id=1, source_target_pairs={{0,1},{1,0},{2,3},{3,2},{4,5},{5,4},{6,7},{7,6},{8,9},{9,8},{10,11... | collective-permute-start | bytes 4718600 | tf_op jit(solution)/shard_map/ppermute | solution.py:25
  124.7 85.8 %collective-permute-start.19 = (bf16[4,128,2048]{2,1,0:T(8,128)(2,1)}, bf16[4,128,2048]{2,1,0:T(8,128)(2,1)}, u32[]{:S(2)}, u32[]{:S(2)}) collective-permute-start(bf16[4,128,2048]{2,1,0:T(8,128)(2,1)} %bitcast.85), channel_id=1, source_target_pairs={{0,1},{1,0},{2,3},{3,2},{4,5},{5,4},{6,7},{7,6},{8,9},{9,8},{10,11... | collective-permute-start | bytes 6291464 | tf_op jit(solution)/shard_map/ppermute | solution.py:25
  137.5 76.2 %collective-permute-start.16 = (bf16[4,128,2048]{2,1,0:T(8,128)(2,1)}, bf16[4,128,2048]{2,1,0:T(8,128)(2,1)}, u32[]{:S(2)}, u32[]{:S(2)}) collective-permute-start(bf16[4,128,2048]{2,1,0:T(8,128)(2,1)} %bitcast.73), channel_id=1, source_target_pairs={{0,1},{1,0},{2,3},{3,2},{4,5},{5,4},{6,7},{7,6},{8,9},{9,8},{10,11... | collective-permute-start | bytes 6291464 | tf_op jit(solution)/shard_map/ppermute | solution.py:25
  140.3 90.8 %collective-permute-start.25 = (bf16[4,512,512]{2,1,0:T(8,128)(2,1)}, bf16[4,512,512]{2,1,0:T(8,128)(2,1)}, u32[]{:S(2)}, u32[]{:S(2)}) collective-permute-start(bf16[4,512,512]{2,1,0:T(8,128)(2,1)} %bitcast.107), channel_id=1, source_target_pairs={{0,1},{1,0},{2,3},{3,2},{4,5},{5,4},{6,7},{7,6},{8,9},{9,8},{10,11... | collective-permute-start | bytes 6291464 | tf_op jit(solution)/shard_map/ppermute | solution.py:25
  143.6 90.7 %collective-permute-start.22 = (bf16[4,512,512]{2,1,0:T(8,128)(2,1)}, bf16[4,512,512]{2,1,0:T(8,128)(2,1)}, u32[]{:S(2)}, u32[]{:S(2)}) collective-permute-start(bf16[4,512,512]{2,1,0:T(8,128)(2,1)} %bitcast.95), channel_id=1, source_target_pairs={{0,1},{1,0},{2,3},{3,2},{4,5},{5,4},{6,7},{7,6},{8,9},{9,8},{10,11... | collective-permute-start | bytes 6291464 | tf_op jit(solution)/shard_map/ppermute | solution.py:25
  327.7 61.4 %collective-permute-start.26 = (bf16[2,256,1024]{2,1,0:T(8,128)(2,1)}, bf16[2,256,1024]{2,1,0:T(8,128)(2,1)S(1)}, u32[]{:S(2)}, u32[]{:S(2)}) collective-permute-start(bf16[2,256,1024]{2,1,0:T(8,128)(2,1)} %slice_bitcast_fusion.14), channel_id=1, source_target_pairs={{0,8},{8,0},{16,24},{24,16},{1,9},{9,1},{17,25},{25,17},{2,10},{10... | collective-permute-start | bytes 3145736 | tf_op jit(solution)/shard_map/ppermute | solution.py:25
  330.3 111.0 %collective-permute-start.28 = (bf16[4,128,3072]{2,1,0:T(8,128)(2,1)}, bf16[4,128,3072]{2,1,0:T(8,128)(2,1)}, u32[]{:S(2)}, u32[]{:S(2)}) collective-permute-start(bf16[4,128,3072]{2,1,0:T(8,128)(2,1)} %fusion.22), channel_id=1, source_target_pairs={{0,1},{1,0},{2,3},{3,2},{4,5},{5,4},{6,7},{7,6},{8,9},{9,8},{10,11... | collective-permute-start | bytes 9437192 | tf_op jit(solution)/shard_map/ppermute | solution.py:25
  333.2 51.4 %collective-permute-start.41 = (bf16[4,128,1024]{2,1,0:T(8,128)(2,1)}, bf16[4,128,1024]{2,1,0:T(8,128)(2,1)}, u32[]{:S(2)}, u32[]{:S(2)}) collective-permute-start(bf16[4,128,1024]{2,1,0:T(8,128)(2,1)} %slice_bitcast_fusion.12), channel_id=1, source_target_pairs={{0,1},{1,0},{2,3},{3,2},{4,5},{5,4},{6,7},{7,6},{8,9},{9,8},{10,11... | collective-permute-start | bytes 3145736 | tf_op jit(solution)/shard_map/ppermute | solution.py:25
  337.9 130.6 %collective-permute-start.54 = (bf16[4,128,4096]{2,1,0:T(8,128)(2,1)}, bf16[4,128,4096]{2,1,0:T(8,128)(2,1)}, u32[]{:S(2)}, u32[]{:S(2)}) collective-permute-start(bf16[4,128,4096]{2,1,0:T(8,128)(2,1)} %slice_bitcast_fusion.2), channel_id=1, source_target_pairs={{0,1},{1,0},{2,3},{3,2},{4,5},{5,4},{6,7},{7,6},{8,9},{9,8},{10,11... | collective-permute-start | bytes 12582920 | tf_op jit(solution)/shard_map/ppermute | solution.py:25
  343.1 133.0 %collective-permute-start.67 = (bf16[4,512,1024]{2,1,0:T(8,128)(2,1)}, bf16[4,512,1024]{2,1,0:T(8,128)(2,1)}, u32[]{:S(2)}, u32[]{:S(2)}) collective-permute-start(bf16[4,512,1024]{2,1,0:T(8,128)(2,1)} %slice_bitcast_fusion), channel_id=1, source_target_pairs={{0,1},{1,0},{2,3},{3,2},{4,5},{5,4},{6,7},{7,6},{8,9},{9,8},{10,11... | collective-permute-start | bytes 12582920 | tf_op jit(solution)/shard_map/ppermute | solution.py:25
  386.7 7.6 %collective-permute-start.48 = (bf16[1,2,128,512]{3,2,1,0:T(8,128)(2,1)S(1)}, bf16[1,2,128,512]{3,2,1,0:T(8,128)(2,1)S(1)}, u32[]{:S(2)}, u32[]{:S(2)}) collective-permute-start(bf16[1,2,128,512]{3,2,1,0:T(8,128)(2,1)S(1)} %slice_bitcast_fusion.47), channel_id=1, source_target_pairs={{0,4},{1,5},{2,6},{3,7},{4,0},{5,1},{6,2},{7,3},{8,12},{9,13},{10,... | collective-permute-start | bytes 786440 | tf_op jit(solution)/shard_map/ppermute | solution.py:25
  389.5 44.0 %collective-permute-start.27 = (bf16[1,256,1024]{2,1,0:T(8,128)(2,1)S(1)}, bf16[1,256,1024]{2,1,0:T(8,128)(2,1)S(1)}, u32[]{:S(2)}, u32[]{:S(2)}) collective-permute-start(bf16[1,256,1024]{2,1,0:T(8,128)(2,1)S(1)} %slice_bitcast_fusion.28), channel_id=1, source_target_pairs={{0,24},{8,16},{16,8},{24,0},{1,25},{9,17},{17,9},{25,1},{2,26},{10... | collective-permute-start | bytes 1572872 | tf_op jit(solution)/shard_map/ppermute | solution.py:25
  439.3 7.6 %collective-permute-start.47 = (bf16[64,512]{1,0:T(8,128)(2,1)S(1)}, bf16[64,512]{1,0:T(8,128)(2,1)S(1)}, u32[]{:S(2)}, u32[]{:S(2)}) collective-permute-start(bf16[64,512]{1,0:T(8,128)(2,1)S(1)} %pad_maximum_fusion.53), channel_id=1, source_target_pairs={{0,8},{8,0},{16,24},{24,16},{1,9},{9,1},{17,25},{25,17},{2,10},{10... | collective-permute-start | bytes 196616 | tf_op jit(solution)/shard_map/ppermute | solution.py:25
  444.5 17.6 %collective-permute-start.35 = (bf16[1,2,128,1536]{3,2,1,0:T(8,128)(2,1)S(1)}, bf16[1,2,128,1536]{3,2,1,0:T(8,128)(2,1)S(1)}, u32[]{:S(2)}, u32[]{:S(2)}) collective-permute-start(bf16[1,2,128,1536]{3,2,1,0:T(8,128)(2,1)S(1)} %slice_bitcast_fusion.16), channel_id=1, source_target_pairs={{0,4},{1,5},{2,6},{3,7},{4,0},{5,1},{6,2},{7,3},{8,12},{9,13},{10,... | collective-permute-start | bytes 2359304 | tf_op jit(solution)/shard_map/ppermute | solution.py:25
  447.8 17.6 %collective-permute-start.29 = (bf16[2,1,128,1536]{3,2,0,1:T(8,128)(2,1)S(1)}, bf16[2,1,128,1536]{3,2,0,1:T(8,128)(2,1)S(1)}, u32[]{:S(2)}, u32[]{:S(2)}) collective-permute-start(bf16[2,1,128,1536]{3,2,0,1:T(8,128)(2,1)S(1)} %slice_bitcast_fusion.18), channel_id=1, source_target_pairs={{0,2},{1,3},{2,0},{3,1},{4,6},{5,7},{6,4},{7,5},{8,10},{9,11},{10,... | collective-permute-start | bytes 2359304 | tf_op jit(solution)/shard_map/ppermute | solution.py:25
  463.1 19.4 %collective-permute-start.36 = (bf16[1,1,128,1536]{3,2,1,0:T(8,128)(2,1)}, bf16[1,1,128,1536]{3,2,1,0:T(8,128)(2,1)}, u32[]{:S(2)}, u32[]{:S(2)}) collective-permute-start(bf16[1,1,128,1536]{3,2,1,0:T(8,128)(2,1)} %slice_bitcast_fusion.39), channel_id=1, source_target_pairs={{0,2},{1,3},{2,0},{3,1},{4,6},{5,7},{6,4},{7,5},{8,10},{9,11},{10,... | collective-permute-start | bytes 1179656 | tf_op jit(solution)/shard_map/ppermute | solution.py:25
  466.4 18.0 %collective-permute-start.30 = (bf16[1,1,128,1536]{3,2,1,0:T(8,128)(2,1)}, bf16[1,1,128,1536]{3,2,1,0:T(8,128)(2,1)}, u32[]{:S(2)}, u32[]{:S(2)}) collective-permute-start(bf16[1,1,128,1536]{3,2,1,0:T(8,128)(2,1)} %slice_bitcast_fusion.41), channel_id=1, source_target_pairs={{0,4},{1,5},{2,6},{3,7},{4,0},{5,1},{6,2},{7,3},{8,12},{9,13},{10,... | collective-permute-start | bytes 1179656 | tf_op jit(solution)/shard_map/ppermute | solution.py:25
  474.0 68.7 %collective-permute-start.61 = (bf16[1,2,128,2048]{3,2,1,0:T(8,128)(2,1)}, bf16[1,2,128,2048]{3,2,1,0:T(8,128)(2,1)S(1)}, u32[]{:S(2)}, u32[]{:S(2)}) collective-permute-start(bf16[1,2,128,2048]{3,2,1,0:T(8,128)(2,1)} %slice_bitcast_fusion.8), channel_id=1, source_target_pairs={{0,4},{1,5},{2,6},{3,7},{4,0},{5,1},{6,2},{7,3},{8,12},{9,13},{10,... | collective-permute-start | bytes 3145736 | tf_op jit(solution)/shard_map/ppermute | solution.py:25
  474.1 70.1 %collective-permute-start.55 = (bf16[2,1,128,2048]{3,2,0,1:T(8,128)(2,1)S(1)}, bf16[2,1,128,2048]{3,2,0,1:T(8,128)(2,1)}, u32[]{:S(2)}, u32[]{:S(2)}) collective-permute-start(bf16[2,1,128,2048]{3,2,0,1:T(8,128)(2,1)S(1)} %slice_bitcast_fusion.10), channel_id=1, source_target_pairs={{0,2},{1,3},{2,0},{3,1},{4,6},{5,7},{6,4},{7,5},{8,10},{9,11},{10,... | collective-permute-start | bytes 3145736 | tf_op jit(solution)/shard_map/ppermute | solution.py:25
  480.9 65.6 %collective-permute-start.74 = (bf16[1,2,512,512]{3,2,1,0:T(8,128)(2,1)S(1)}, bf16[1,2,512,512]{3,2,1,0:T(8,128)(2,1)S(1)}, u32[]{:S(2)}, u32[]{:S(2)}) collective-permute-start(bf16[1,2,512,512]{3,2,1,0:T(8,128)(2,1)S(1)} %slice_bitcast_fusion.4), channel_id=1, source_target_pairs={{0,4},{1,5},{2,6},{3,7},{4,0},{5,1},{6,2},{7,3},{8,12},{9,13},{10,... | collective-permute-start | bytes 3145736 | tf_op jit(solution)/shard_map/ppermute | solution.py:25
  482.5 66.4 %collective-permute-start.68 = (bf16[2,1,512,512]{3,2,0,1:T(8,128)(2,1)S(1)}, bf16[2,1,512,512]{3,2,0,1:T(8,128)(2,1)S(1)}, u32[]{:S(2)}, u32[]{:S(2)}) collective-permute-start(bf16[2,1,512,512]{3,2,0,1:T(8,128)(2,1)S(1)} %slice_bitcast_fusion.6), channel_id=1, source_target_pairs={{0,2},{1,3},{2,0},{3,1},{4,6},{5,7},{6,4},{7,5},{8,10},{9,11},{10,... | collective-permute-start | bytes 3145736 | tf_op jit(solution)/shard_map/ppermute | solution.py:25
  516.4 7.5 %collective-permute-start.33 = (bf16[32,1536]{1,0:T(8,128)(2,1)S(1)}, bf16[32,1536]{1,0:T(8,128)(2,1)S(1)}, u32[]{:S(2)}, u32[]{:S(2)}) collective-permute-start(bf16[32,1536]{1,0:T(8,128)(2,1)S(1)} %add_convert_fusion.9), channel_id=1, source_target_pairs={{0,24},{8,16},{16,8},{24,0},{1,25},{9,17},{17,9},{25,1},{2,26},{10... | collective-permute-start | bytes 294920 | tf_op jit(solution)/shard_map/ppermute | solution.py:25
  523.9 7.8 %collective-permute-start.40 = (bf16[64,1536]{1,0:T(8,128)(2,1)S(1)}, bf16[64,1536]{1,0:T(8,128)(2,1)S(1)}, u32[]{:S(2)}, u32[]{:S(2)}) collective-permute-start(bf16[64,1536]{1,0:T(8,128)(2,1)S(1)} %pad_maximum_fusion.52), channel_id=1, source_target_pairs={{0,8},{8,0},{16,24},{24,16},{1,9},{9,1},{17,25},{25,17},{2,10},{10... | collective-permute-start | bytes 589832 | tf_op jit(solution)/shard_map/ppermute | solution.py:25
  531.7 9.6 %collective-permute-start.34 = (bf16[64,1536]{1,0:T(8,128)(2,1)S(1)}, bf16[64,1536]{1,0:T(8,128)(2,1)S(1)}, u32[]{:S(2)}, u32[]{:S(2)}) collective-permute-start(bf16[64,1536]{1,0:T(8,128)(2,1)S(1)} %pad_maximum_fusion.51), channel_id=1, source_target_pairs={{0,8},{8,0},{16,24},{24,16},{1,9},{9,1},{17,25},{25,17},{2,10},{10... | collective-permute-start | bytes 589832 | tf_op jit(solution)/shard_map/ppermute | solution.py:25
  543.1 9.2 %collective-permute-start.62 = (bf16[1,1,128,2048]{3,2,1,0:T(8,128)(2,1)S(1)}, bf16[1,1,128,2048]{3,2,1,0:T(8,128)(2,1)S(1)}, u32[]{:S(2)}, u32[]{:S(2)}) collective-permute-start(bf16[1,1,128,2048]{3,2,1,0:T(8,128)(2,1)S(1)} %slice_bitcast_fusion.24), channel_id=1, source_target_pairs={{0,2},{1,3},{2,0},{3,1},{4,6},{5,7},{6,4},{7,5},{8,10},{9,11},{10,... | collective-permute-start | bytes 1572872 | tf_op jit(solution)/shard_map/ppermute | solution.py:25
  546.0 9.2 %collective-permute-start.56 = (bf16[1,1,128,2048]{3,2,1,0:T(8,128)(2,1)S(1)}, bf16[1,1,128,2048]{3,2,1,0:T(8,128)(2,1)S(1)}, u32[]{:S(2)}, u32[]{:S(2)}) collective-permute-start(bf16[1,1,128,2048]{3,2,1,0:T(8,128)(2,1)S(1)} %slice_bitcast_fusion.26), channel_id=1, source_target_pairs={{0,4},{1,5},{2,6},{3,7},{4,0},{5,1},{6,2},{7,3},{8,12},{9,13},{10,... | collective-permute-start | bytes 1572872 | tf_op jit(solution)/shard_map/ppermute | solution.py:25
  546.9 11.1 %collective-permute-start.75 = (bf16[1,1,512,512]{3,2,1,0:T(8,128)(2,1)S(1)}, bf16[1,1,512,512]{3,2,1,0:T(8,128)(2,1)S(1)}, u32[]{:S(2)}, u32[]{:S(2)}) collective-permute-start(bf16[1,1,512,512]{3,2,1,0:T(8,128)(2,1)S(1)} %slice_bitcast_fusion.20), channel_id=1, source_target_pairs={{0,2},{1,3},{2,0},{3,1},{4,6},{5,7},{6,4},{7,5},{8,10},{9,11},{10,... | collective-permute-start | bytes 1572872 | tf_op jit(solution)/shard_map/ppermute | solution.py:25
  549.3 11.6 %collective-permute-start.69 = (bf16[1,1,512,512]{3,2,1,0:T(8,128)(2,1)S(1)}, bf16[1,1,512,512]{3,2,1,0:T(8,128)(2,1)S(1)}, u32[]{:S(2)}, u32[]{:S(2)}) collective-permute-start(bf16[1,1,512,512]{3,2,1,0:T(8,128)(2,1)S(1)} %slice_bitcast_fusion.22), channel_id=1, source_target_pairs={{0,4},{1,5},{2,6},{3,7},{4,0},{5,1},{6,2},{7,3},{8,12},{9,13},{10,... | collective-permute-start | bytes 1572872 | tf_op jit(solution)/shard_map/ppermute | solution.py:25
  552.5 9.3 %collective-permute-start.63 = (bf16[64,2048]{1,0:T(8,128)(2,1)S(1)}, bf16[64,2048]{1,0:T(8,128)(2,1)S(1)}, u32[]{:S(2)}, u32[]{:S(2)}) collective-permute-start(bf16[64,2048]{1,0:T(8,128)(2,1)S(1)} %dynamic-slice_bitcast_fusion.2), channel_id=1, source_target_pairs={{0,8},{8,0},{16,24},{24,16},{1,9},{9,1},{17,25},{25,17},{2,10},{10... | collective-permute-start | bytes 786440 | tf_op jit(solution)/shard_map/ppermute | solution.py:25
  555.4 13.2 %collective-permute-start.57 = (bf16[64,2048]{1,0:T(8,128)(2,1)S(1)}, bf16[64,2048]{1,0:T(8,128)(2,1)S(1)}, u32[]{:S(2)}, u32[]{:S(2)}) collective-permute-start(bf16[64,2048]{1,0:T(8,128)(2,1)S(1)} %dynamic-slice_bitcast_fusion.3), channel_id=1, source_target_pairs={{0,8},{8,0},{16,24},{24,16},{1,9},{9,1},{17,25},{25,17},{2,10},{10... | collective-permute-start | bytes 786440 | tf_op jit(solution)/shard_map/ppermute | solution.py:25
  558.2 12.7 %collective-permute-start.76 = (bf16[256,512]{1,0:T(8,128)(2,1)S(1)}, bf16[256,512]{1,0:T(8,128)(2,1)S(1)}, u32[]{:S(2)}, u32[]{:S(2)}) collective-permute-start(bf16[256,512]{1,0:T(8,128)(2,1)S(1)} %dynamic-slice_bitcast_fusion), channel_id=1, source_target_pairs={{0,8},{8,0},{16,24},{24,16},{1,9},{9,1},{17,25},{25,17},{2,10},{10... | collective-permute-start | bytes 786440 | tf_op jit(solution)/shard_map/ppermute | solution.py:25
  561.1 12.6 %collective-permute-start.70 = (bf16[256,512]{1,0:T(8,128)(2,1)S(1)}, bf16[256,512]{1,0:T(8,128)(2,1)S(1)}, u32[]{:S(2)}, u32[]{:S(2)}) collective-permute-start(bf16[256,512]{1,0:T(8,128)(2,1)S(1)} %dynamic-slice_bitcast_fusion.1), channel_id=1, source_target_pairs={{0,8},{8,0},{16,24},{24,16},{1,9},{9,1},{17,25},{25,17},{2,10},{10... | collective-permute-start | bytes 786440 | tf_op jit(solution)/shard_map/ppermute | solution.py:25
  562.0 14.5 %collective-permute-start.64 = (bf16[32,2048]{1,0:T(8,128)(2,1)S(1)}, bf16[32,2048]{1,0:T(8,128)(2,1)S(1)}, u32[]{:S(2)}, u32[]{:S(2)}) collective-permute-start(bf16[32,2048]{1,0:T(8,128)(2,1)S(1)} %constant_dynamic-slice_fusion.3), channel_id=1, source_target_pairs={{0,24},{8,16},{16,8},{24,0},{1,25},{9,17},{17,9},{25,1},{2,26},{10... | collective-permute-start | bytes 393224 | tf_op jit(solution)/shard_map/ppermute | solution.py:25
  568.7 10.1 %collective-permute-start.58 = (bf16[32,2048]{1,0:T(8,128)(2,1)S(1)}, bf16[32,2048]{1,0:T(8,128)(2,1)S(1)}, u32[]{:S(2)}, u32[]{:S(2)}) collective-permute-start(bf16[32,2048]{1,0:T(8,128)(2,1)S(1)} %constant_dynamic-slice_fusion.4), channel_id=1, source_target_pairs={{0,24},{8,16},{16,8},{24,0},{1,25},{9,17},{17,9},{25,1},{2,26},{10... | collective-permute-start | bytes 393224 | tf_op jit(solution)/shard_map/ppermute | solution.py:25
  570.9 9.5 %collective-permute-start.77 = (bf16[128,512]{1,0:T(8,128)(2,1)S(1)}, bf16[128,512]{1,0:T(8,128)(2,1)S(1)}, u32[]{:S(2)}, u32[]{:S(2)}) collective-permute-start(bf16[128,512]{1,0:T(8,128)(2,1)S(1)} %constant_dynamic-slice_fusion.1), channel_id=1, source_target_pairs={{0,24},{8,16},{16,8},{24,0},{1,25},{9,17},{17,9},{25,1},{2,26},{10... | collective-permute-start | bytes 393224 | tf_op jit(solution)/shard_map/ppermute | solution.py:25
  573.7 9.1 %collective-permute-start.71 = (bf16[128,512]{1,0:T(8,128)(2,1)S(1)}, bf16[128,512]{1,0:T(8,128)(2,1)S(1)}, u32[]{:S(2)}, u32[]{:S(2)}) collective-permute-start(bf16[128,512]{1,0:T(8,128)(2,1)S(1)} %constant_dynamic-slice_fusion.2), channel_id=1, source_target_pairs={{0,24},{8,16},{16,8},{24,0},{1,25},{9,17},{17,9},{25,1},{2,26},{10... | collective-permute-start | bytes 393224 | tf_op jit(solution)/shard_map/ppermute | solution.py:25
  576.5 8.0 %collective-permute-start.65 = (bf16[32,2048]{1,0:T(8,128)(2,1)S(1)}, bf16[32,2048]{1,0:T(8,128)(2,1)S(1)}, u32[]{:S(2)}, u32[]{:S(2)}) collective-permute-start(bf16[32,2048]{1,0:T(8,128)(2,1)S(1)} %add_convert_fusion.6), channel_id=1, source_target_pairs={{0,24},{8,16},{16,8},{24,0},{1,25},{9,17},{17,9},{25,1},{2,26},{10... | collective-permute-start | bytes 393224 | tf_op jit(solution)/shard_map/ppermute | solution.py:25
  578.8 12.3 %collective-permute-start.59 = (bf16[32,2048]{1,0:T(8,128)(2,1)S(1)}, bf16[32,2048]{1,0:T(8,128)(2,1)S(1)}, u32[]{:S(2)}, u32[]{:S(2)}) collective-permute-start(bf16[32,2048]{1,0:T(8,128)(2,1)S(1)} %add_convert_fusion.7), channel_id=1, source_target_pairs={{0,24},{8,16},{16,8},{24,0},{1,25},{9,17},{17,9},{25,1},{2,26},{10... | collective-permute-start | bytes 393224 | tf_op jit(solution)/shard_map/ppermute | solution.py:25
  580.5 12.0 %collective-permute-start.78 = (bf16[128,512]{1,0:T(8,128)(2,1)S(1)}, bf16[128,512]{1,0:T(8,128)(2,1)S(1)}, u32[]{:S(2)}, u32[]{:S(2)}) collective-permute-start(bf16[128,512]{1,0:T(8,128)(2,1)S(1)} %add_convert_fusion.4), channel_id=1, source_target_pairs={{0,24},{8,16},{16,8},{24,0},{1,25},{9,17},{17,9},{25,1},{2,26},{10... | collective-permute-start | bytes 393224 | tf_op jit(solution)/shard_map/ppermute | solution.py:25
  582.9 11.0 %collective-permute-start.72 = (bf16[128,512]{1,0:T(8,128)(2,1)S(1)}, bf16[128,512]{1,0:T(8,128)(2,1)S(1)}, u32[]{:S(2)}, u32[]{:S(2)}) collective-permute-start(bf16[128,512]{1,0:T(8,128)(2,1)S(1)} %add_convert_fusion.5), channel_id=1, source_target_pairs={{0,24},{8,16},{16,8},{24,0},{1,25},{9,17},{17,9},{25,1},{2,26},{10... | collective-permute-start | bytes 393224 | tf_op jit(solution)/shard_map/ppermute | solution.py:25
  584.6 10.9 %collective-permute-start.66 = (bf16[64,2048]{1,0:T(8,128)(2,1)S(1)}, bf16[64,2048]{1,0:T(8,128)(2,1)S(1)}, u32[]{:S(2)}, u32[]{:S(2)}) collective-permute-start(bf16[64,2048]{1,0:T(8,128)(2,1)S(1)} %pad_maximum_fusion.48), channel_id=1, source_target_pairs={{0,8},{8,0},{16,24},{24,16},{1,9},{9,1},{17,25},{25,17},{2,10},{10... | collective-permute-start | bytes 786440 | tf_op jit(solution)/shard_map/ppermute | solution.py:25
  592.6 8.5 %collective-permute-start.79 = (bf16[256,512]{1,0:T(8,128)(2,1)S(1)}, bf16[256,512]{1,0:T(8,128)(2,1)S(1)}, u32[]{:S(2)}, u32[]{:S(2)}) collective-permute-start(bf16[256,512]{1,0:T(8,128)(2,1)S(1)} %pad_maximum_fusion.50), channel_id=1, source_target_pairs={{0,8},{8,0},{16,24},{24,16},{1,9},{9,1},{17,25},{25,17},{2,10},{10... | collective-permute-start | bytes 786440 | tf_op jit(solution)/shard_map/ppermute | solution.py:25
  594.0 9.9 %collective-permute-start.73 = (bf16[256,512]{1,0:T(8,128)(2,1)S(1)}, bf16[256,512]{1,0:T(8,128)(2,1)S(1)}, u32[]{:S(2)}, u32[]{:S(2)}) collective-permute-start(bf16[256,512]{1,0:T(8,128)(2,1)S(1)} %pad_maximum_fusion.49), channel_id=1, source_target_pairs={{0,8},{8,0},{16,24},{24,16},{1,9},{9,1},{17,25},{25,17},{2,10},{10... | collective-permute-start | bytes 786440 | tf_op jit(solution)/shard_map/ppermute | solution.py:25
  (81 other events, 620.3 us)

commit v2 on v1

--- a/solution.py
+++ b/solution.py
@@ -38,77 +38,91 @@
     return (outer + [0], outer[::-1] + [0])
 
 
-def gather_half(shard, order):
-    held, done = shard[None], []
-    for bit in order:
-        other = swap(held, "fsdp", 1 << bit)
-        done.append(bit)
-        lower = sum(1 for at in done if at < bit)
-        rest = held.shape[1:]
-        inner = 1 << lower
-        split = (held.shape[0] // inner, 1, inner) + rest
-        held = jnp.concatenate((held.reshape(split), other.reshape(split)), axis=1)
-        held = held.reshape((-1,) + rest)
-    return held
-
-
-def gather(shard):
-    half = shard.shape[1] // 2
-    first, second = two_ways(bits_of("fsdp"))
-    whole = jnp.concatenate(
-        (gather_half(shard[:, :half], first), gather_half(shard[:, half:], second)), axis=2
-    )
-    return whole.reshape(-1, shard.shape[1])
-
-
-def ctx_total(value):
+def tie(*values):
+    return lax.optimization_barrier(values)
+
+
+def halves(value):
+    middle = value.shape[-1] // 256 * 128
+    return value[..., :middle], value[..., middle:]
+
+
+def gather_hop(held, bit, done):
+    other = swap(held, "fsdp", 1 << bit)
+    inner = 1 << sum(1 for at in done if at < bit)
+    rest = held.shape[1:]
+    split = (held.shape[0] // inner, 1, inner) + rest
+    held = jnp.concatenate((held.reshape(split), other.reshape(split)), axis=1)
+    return held.reshape((-1,) + rest)
+
+
+def gather_hops(pair, first, last):
+    moved = []
+    for held, order in zip(pair, two_ways(bits_of("fsdp"))):
+        for at in range(first, last):
+            held = gather_hop(held, order[at], order[:at])
+        moved.append(held)
+    return tuple(moved)
+
+
+def whole(pair):
+    joined = jnp.concatenate(pair, axis=2)
+    return joined.reshape(-1, joined.shape[2])
+
+
+def ctx_hops(value, first, last):
     me = lax.axis_index("ctx")
     gray = me ^ (me >> 1)
     bits = bits_of("ctx")
-    for at in range(bits):
-        half = value.shape[0] // 2
-        mine = (gray >> at) & 1
-        keep = lax.dynamic_slice_in_dim(value, mine * half, half, 0)
-        send = lax.dynamic_slice_in_dim(value, (1 - mine) * half, half, 0)
-        value = add(keep, swap(send, "ctx", (2 << at) - 1))
-    for at in reversed(range(bits)):
-        other = swap(value, "ctx", (2 << at) - 1)
-        upper = ((gray >> at) & 1) == 1
-        value = jnp.concatenate(
-            (jnp.where(upper, other, value), jnp.where(upper, value, other)), axis=0
-        )
-    return value.astype(jnp.float32)
-
-
-def reduce_grad(grad):
-    count = lax.axis_size("fsdp")
-    columns = grad.shape[1]
-    half = columns // 2
-    blocks = grad.astype(jnp.bfloat16).reshape(count, -1, columns)
-    pairs = blocks.reshape(count // 2, 2, -1, columns)
-    blocks = add(pairs[:, 0], swap(pairs[:, 1], "fsdp", 1))
-    first, second = two_ways(bits_of("fsdp"))
-    first = [bit - 1 for bit in first[:-1]]
-    second = [bit - 1 for bit in second[:-1]]
+    for hop in range(first, last):
+        if hop < bits:
+            half = value.shape[1] // 2
+            mine = (gray >> hop) & 1
+            keep = lax.dynamic_slice_in_dim(value, mine * half, half, 1)
+            send = lax.dynamic_slice_in_dim(value, (1 - mine) * half, half, 1)
+            value = add(keep, swap(send, "ctx", (2 << hop) - 1))
+        else:
+            at = 2 * bits - 1 - hop
+            other = swap(value, "ctx", (2 << at) - 1)
+            upper = ((gray >> at) & 1) == 1
+            value = jnp.concatenate(
+                (jnp.where(upper, other, value), jnp.where(upper, value, other)), axis=1
+            )
+    return value
+
+
+def as_blocks(grad):
+    return grad.astype(jnp.bfloat16).reshape(lax.axis_size("fsdp"), -1, grad.shape[1])
+
+
+def scatter_core(blocks):
+    pairs = blocks.reshape((-1, 2) + blocks.shape[1:])
+    return halves(add(pairs[:, 0], swap(pairs[:, 1], "fsdp", 1)))
+
+
+def scatter_hops(pair, first, last):
+    moved = []
+    for blocks, order in zip(pair, two_ways(bits_of("fsdp"))):
+        for at in range(first, last):
+            inner = 1 << sorted(order[at:-1]).index(order[at])
+            rest = blocks.shape[1:]
+            parts = blocks.reshape((blocks.shape[0] // (2 * inner), 2, inner) + rest)
+            came = swap(parts[:, 1], "fsdp", 1 << order[at])
+            blocks = add(parts[:, 0], came).reshape((-1,) + rest)
+        moved.append(blocks)
+    return tuple(moved)
+
+
+def fold(value, width):
     return jnp.concatenate(
-        (
-            ctx_total(scatter_outer(blocks[:, :, :half], first)),
-            ctx_total(scatter_outer(blocks[:, :, half:], second)),
-        ),
-        axis=1,
-    )
-
-
-def scatter_outer(blocks, order):
-    left = sorted(order)
-    for bit in order:
-        inner = 1 << left.index(bit)
-        left.remove(bit)
-        rest = blocks.shape[1:]
-        parts = blocks.reshape((blocks.shape[0] // (2 * inner), 2, inner) + rest)
-        came = swap(parts[:, 1], "fsdp", 2 << bit)
-        blocks = add(parts[:, 0], came).reshape((-1,) + rest)
-    return blocks[0]
+        [value[:, at : at + width] for at in range(0, value.shape[1], width)], axis=0
+    )
+
+
+def unfold(value, rows):
+    return jnp.concatenate(
+        [value[at : at + rows] for at in range(0, value.shape[0], rows)], axis=1
+    )
 
 
 def gray_mask(index):
@@ -215,11 +229,16 @@
         gain_two,
         shift_two,
     ) = spread
-    input_proj = gather(w_qkv)
+    bits = bits_of("fsdp")
+    outer = bits - 1
+    input_half = gather_hops(halves(w_qkv[None]), 0, outer)
+    input_half, up_half, down_half = tie(
+        input_half, halves(jnp.concatenate((w_attn_out, w_up), axis=1)[None]), halves(w_down[None])
+    )
+    input_proj = whole(gather_hops(input_half, outer, bits))
     token_blocks = gather_tokens(tok_rows)
-    out_weight = gather(w_attn_out)
-    up_weight = gather(w_up)
-    down_weight = gather(w_down)
+    up_half = gather_hops(up_half, 0, outer)
+    down_half = gather_hops(down_half, 0, outer)
     ctx_count = token_blocks.shape[0]
     score_scale = HEAD_DIM ** (-0.5)
     all_rows = reorder(token_blocks.reshape(ctx_count * row_count, width), count)
@@ -249,6 +268,10 @@
         * score_scale
     )
     attn_prob = jax.nn.softmax(scores, axis=-1).astype(jnp.bfloat16)
+    up_half, down_half, attn_prob = tie(up_half, down_half, attn_prob)
+    out_up = whole(gather_hops(up_half, outer, bits))
+    down_weight = whole(gather_hops(down_half, outer, bits))
+    out_weight, up_weight = out_up[:, :width], out_up[:, width:]
     mixed_out = jnp.einsum(
         "shqk,shkd->shqd", attn_prob, value_part, preferred_element_type=jnp.float32
     )
@@ -268,17 +291,23 @@
     norm_pull = jax.vjp(layer_norm, resid_two, gain_two, shift_two)[1]
     grad_resid_two, grad_gain_two, grad_shift_two = norm_pull(cotangent)
     grad_branch = grad_resid_two.astype(jnp.bfloat16)
-    sum_down = reduce_grad(dot_rows(activated, grad_branch))
+    down_blocks, grad_branch = tie(as_blocks(dot_rows(activated, grad_branch)), grad_branch)
+    down_pair = scatter_core(down_blocks)
     grad_down_bias = jnp.sum(grad_branch.astype(jnp.float32), axis=0)
     grad_act = reorder(dot_back(grad_branch, down_weight), count)
     grad_hidden = jax.vjp(gelu_exact, hidden)[1](grad_act)[0].astype(jnp.bfloat16)
-    sum_up = reduce_grad(dot_rows(normed_low, grad_hidden))
+    up_blocks, grad_hidden = tie(as_blocks(dot_rows(normed_low, grad_hidden)), grad_hidden)
+    up_pair = scatter_core(up_blocks)
     grad_up_bias = jnp.sum(grad_hidden.astype(jnp.float32), axis=0)
+    down_pair, grad_hidden = tie(down_pair, grad_hidden)
+    down_pair = scatter_hops(down_pair, 0, 1)
     grad_normed = grad_resid_two + reorder(dot_back(grad_hidden, up_weight), count)
     norm_pull_one = jax.vjp(layer_norm, resid_one, gain_one, shift_one)[1]
     grad_resid_one, grad_gain_one, grad_shift_one = norm_pull_one(grad_normed)
     grad_attn = grad_resid_one.astype(jnp.bfloat16)
-    sum_out = reduce_grad(dot_rows(attn_in, grad_attn))
+    grad_out_weight = dot_rows(attn_in, grad_attn)
+    up_pair, grad_attn = tie(up_pair, grad_attn)
+    up_pair = scatter_hops(up_pair, 0, 1)
     grad_out_bias = jnp.sum(grad_attn.astype(jnp.float32), axis=0)
     grad_mixed = reorder(dot_back(grad_attn, out_weight).astype(jnp.bfloat16), count)
     grad_heads = heads(grad_mixed)
@@ -287,6 +316,8 @@
         "shqd,shkd->shqk", grad_heads, value_part, preferred_element_type=jnp.float32
     )
     grad_score = (attn_prob.astype(jnp.float32) * (grad_prob - row_delta)).astype(jnp.bfloat16)
+    down_pair, grad_score = tie(down_pair, grad_score)
+    down_pair = scatter_hops(down_pair, 1, outer)
     grad_value = jnp.einsum(
         "shqk,shqd->shkd", attn_prob, grad_heads, preferred_element_type=jnp.float32
     )
@@ -302,16 +333,13 @@
     grad_keys = by_block(grad_key).astype(jnp.bfloat16)
     grad_values = by_block(grad_value).astype(jnp.bfloat16)
     grad_kv = jnp.concatenate((grad_keys, grad_values), axis=1)
+    up_pair, grad_kv = tie(up_pair, grad_kv)
+    up_pair = scatter_hops(up_pair, 1, outer)
     grad_input_proj = jnp.concatenate(
         (dot_rows(own_rows, grad_queries), dot_rows(all_rows, grad_kv)), axis=1
     )
-    sum_input = reduce_grad(grad_input_proj)
     grad_query_bias = jnp.sum(grad_queries.astype(jnp.float32), axis=0)
     grad_value_bias = jnp.sum(grad_values.astype(jnp.float32), axis=0)
-    from_kv = dot_back(grad_kv, input_proj[:, width:])
-    from_query = dot_back(grad_queries, input_proj[:, :width])
-    from_kv = scatter_tokens(from_kv.astype(jnp.bfloat16).reshape(ctx_count, row_count, width))
-    d_tokens = grad_resid_one + reorder(from_query + from_kv.astype(jnp.float32), count)
     small = (
         grad_query_bias,
         grad_value_bias,
@@ -323,10 +351,54 @@
         grad_gain_two,
         grad_shift_two,
     )
-    small_all = lax.psum(
-        jnp.concatenate([item.reshape(count, -1) for item in small], axis=1), ("fsdp", "ctx")
-    )
-    small_own = lax.dynamic_index_in_dim(small_all, lax.axis_index("fsdp"), 0, keepdims=False)
+    small_rows = jnp.concatenate([item.reshape(count, -1) for item in small], axis=1)
+    small_size = small_rows.shape[1]
+    me = lax.axis_index("fsdp")
+    small_rows = jnp.concatenate(
+        [lax.dynamic_slice_in_dim(small_rows, me ^ at, 1, 0) for at in range(count)], axis=0
+    )
+    own_width = width // count
+    small_lines = -(-small_size // 128)
+    small_rows = jnp.pad(small_rows, ((0, 0), (0, small_lines * 128 - small_size)))
+    small_rows = small_rows.reshape(count, small_lines, 128).astype(jnp.bfloat16)
+    small_rows = jnp.pad(small_rows, ((0, 0), (0, own_width - small_lines), (0, 0)))
+    input_blocks = jnp.concatenate(
+        (as_blocks(grad_input_proj), as_blocks(grad_out_weight), small_rows), axis=2
+    )
+    input_blocks, grad_kv = tie(input_blocks, grad_kv)
+    input_pair = scatter_core(input_blocks)
+    from_kv = dot_back(grad_kv, input_proj[:, width:])
+    from_query = dot_back(grad_queries, input_proj[:, :width])
+    input_pair, from_kv = tie(input_pair, from_kv)
+    input_pair = scatter_hops(input_pair, 0, 1)
+    from_kv = scatter_tokens(from_kv.astype(jnp.bfloat16).reshape(ctx_count, row_count, width))
+    d_tokens = grad_resid_one + reorder(from_query + from_kv.astype(jnp.float32), count)
+    down_own = jnp.concatenate(down_pair, axis=2)[0]
+    up_own = jnp.concatenate(up_pair, axis=2)[0]
+    first_group = jnp.concatenate((down_own, fold(up_own, width)), axis=0)
+    ctx_steps = 2 * bits_of("ctx")
+    first_group = ctx_hops(first_group, 0, 1)
+    input_pair, first_group = tie(input_pair, first_group)
+    input_pair = scatter_hops(input_pair, 1, outer)
+    first_group = ctx_hops(first_group, 1, 2)
+    input_pair, first_group = tie(input_pair, first_group)
+    input_own = jnp.concatenate(input_pair, axis=2)[0]
+    extra = input_own[:small_lines, 4 * width :].reshape(-1)
+    extra = jnp.pad(extra, (0, -extra.shape[0] % (16 * width))).reshape(-1, width)
+    second_group = jnp.concatenate((fold(input_own[:, : 4 * width], width), extra), axis=0)
+    for step in range(2, ctx_steps):
+        second_group = ctx_hops(second_group, step - 2, step - 1)
+        first_group = ctx_hops(first_group, step, step + 1)
+        first_group, second_group = tie(first_group, second_group)
+    second_group = ctx_hops(second_group, ctx_steps - 2, ctx_steps)
+    first_group = first_group.astype(jnp.float32)
+    second_group = second_group.astype(jnp.float32)
+    down_rows = down_own.shape[0]
+    sum_down = first_group[:down_rows]
+    sum_up = unfold(first_group[down_rows:], own_width)
+    sum_input = unfold(second_group[: 3 * own_width], own_width)
+    sum_out = second_group[3 * own_width : 4 * own_width]
+    small_own = second_group[4 * own_width :].reshape(-1)
     owned, start = [], 0
     for item in small:
         size = item.shape[0] // count

time: 610 us -> 564 us (0.925); the launches traced: 606 us -> 554 us
  blocking collectives: 49.9 us -> 15.9 us
  starting transfers between devices: 108 us -> 81.8 us
  waiting for transfers between devices: 163 us -> 141 us
  matrix products: 90.3 us -> 109 us
  local copies, waits for them, and re-layouts: 100 us -> 107 us
    psum x1 -> x0, blocking collectives: 40.2 us -> none  [per_device(): lax.psum(jnp.concatenate([item.reshape(count, -1) for item in small], axi...]
    ppermute x80 -> x45, starting transfers between devices: 108 us -> 81.8 us  [swap(): return lax.ppermute(value, axis, [(at, at ^ mask) for at in range(size)])]
    ppermute x80 -> x45, waiting for transfers between devices: 163 us -> 141 us  [swap(): return lax.ppermute(value, axis, [(at, at ^ mask) for at in range(size)])]
    reshape x0 -> x12, other arithmetic: none -> 15.3 us  [scatter_hops(): blocks = add(parts[:, 0], came).reshape((-1,) + rest)]
    sub x1 -> x0, matrix products: 9.83 us -> none  [per_device(): attn_prob = jax.nn.softmax(scores, axis=-1).astype(jnp.bfloat16)]
    dot_general x5, matrix products: 18 us -> 27.2 us  [dot_back(): lax.dot_general(first, second, (((1,), (1,)), ((), ())), preferred_elemen...]
    div x0 -> x1, matrix products: none -> 9.15 us  [per_device(): attn_prob = jax.nn.softmax(scores, axis=-1).astype(jnp.bfloat16)]
    another operation x6 -> x3, local copies, waits for them, and re-layouts: 16.3 us -> 7.95 us  [the longest x4 8.6 us: gather_half(): held = jnp.concatenate((held.reshape(split), other.reshape(split)), axis=1)]
  transfers between devices with their start and end apart: 80 -> 45, of which waited for: 40 -> 15; matrix products, arithmetic and copies ran while one was open for 29% -> 38% of each run, Pallas kernels for 0% -> 0%
where the time goes in v2:
time: 564 us; the launch traced here: 554 us
  waiting for transfers between devices  141 us (25%)
  matrix products  109 us (19%)
  local copies, waits for them, and re-layouts  107 us (19%)
  other arithmetic  96.9 us (17%)
  starting transfers between devices  81.8 us (15%)
  blocking collectives  15.9 us (3%)
    ppermute x45, waiting for transfers between devices, swap(): return lax.ppermute(value, axis, [(at, at ^ mask) for at in range(size)])  141 us
    ppermute x45, starting transfers between devices, swap(): return lax.ppermute(value, axis, [(at, at ^ mask) for at in range(size)])  81.8 us
    unnamed x216, local copies, waits for them, and re-layouts  40.6 us
    concatenate x12, other arithmetic, gather_hop(): held = jnp.concatenate((held.reshape(split), other.reshape(split)), axis=1)  30.2 us
    dot_general x5, matrix products, dot(): return jnp.dot(first, second, preferred_element_type=jnp.float32)  27.9 us
    dot_general x5, matrix products, dot_back(): lax.dot_general(first, second, (((1,), (1,)), ((), ())), preferred_elemen...  27.2 us
    dot_general x5, matrix products, dot_rows(): lax.dot_general(first, second, (((0,), (0,)), ((), ())), preferred_elemen...  16.1 us
    all_gather x1, blocking collectives, per_device(): lax.all_gather(jnp.concatenate(vectors), 'fsdp', axis=0, tiled=False)  15.9 us
  transfers between devices with their start and end apart: 45, of which 15 were waited for; matrix products, arithmetic and copies ran while one was open for 38% of the time, Pallas kernels for 0%

profile of v2, /device:TPU:0, one launch (start us, length us, event | category | flops | bytes accessed | tf_op | source)
XLA Modules:
  0.0 553.7 jit_solution(5779816062788197203)
XLA Ops:
  0.6 5.1 collective-permute-start.12
  14.4 3.3 collective-permute-done.2
  28.5 2.7 collective-permute-start.13
  31.3 15.9 %all-gather.1 = bf16[8,1,1536]{2,1,0:T(2,128)(2,1)S(1)} all-gather(bf16[1,1,1536]{2,1,0:T(2,128)(2,1)S(1)} %reshape.876), channel_id=2, replica_groups=mesh['ctx'=4,'fsdp'=8] {'fsdp'}, dimensions={0}, use_global_device_ids=true | all-gather | bytes 27648 | tf_op jit(solution)/shard_map/all_gather | solution.py:215
  57.9 8.5 %collective-permute-done.10 = bf16[1,512,512]{2,1,0:T(8,128)(2,1)S(1)} collective-permute-done((bf16[1,512,512]{2,1,0:T(8,128)(2,1)S(1)}, bf16[1,512,512]{2,1,0:T(8,128)(2,1)S(1)}, u32[]{:S(2)}, u32[]{:S(2)}) %collective-permute-start.10) | collective-permute-done | bytes 524320 | tf_op jit(solution)/shard_map/ppermute | solution.py:25
  71.5 8.4 %collective-permute-done.6 = bf16[1,128,2560]{2,1,0:T(8,128)(2,1)S(1)} collective-permute-done((bf16[1,128,2560]{2,1,0:T(8,128)(2,1)S(1)}, bf16[1,128,2560]{2,1,0:T(8,128)(2,1)S(1)}, u32[]{:S(2)}, u32[]{:S(2)}) %collective-permute-start.6) | collective-permute-done | bytes 655392 | tf_op jit(solution)/shard_map/ppermute | solution.py:25
  81.7 2.5 collective-permute-done.4
  84.8 2.8 fusion.109
  91.3 4.5 fusion.53
  95.8 3.3 copy-done.22
  100.7 3.0 copy.110
  103.8 2.8 reshape.786
  106.5 4.4 reshape.787
  111.0 3.3 fusion.83
  116.4 2.8 pad_maximum_fusion.17
  119.2 2.8 pad_maximum_fusion.16
  122.0 9.1 %fusion.22 = bf16[1,16,256,1024]{3,2,1,0:T(8,128)(2,1)} fusion(bf16[16,256,64]{1,2,0:T(8,128)(2,1)S(1)} %bitcast.566, bf16[16,1024,64]{1,2,0:T(8,128)(2,1)} %reshape.787), kind=kOutput, calls=%fused_computation.33 | convolution fusion | flops 553658368 | bytes 11010048 | tf_op jit(solution)/shard_map/div | solution.py:270
  132.9 3.1 pad_maximum_fusion.15
  136.0 3.1 pad_maximum_fusion.14
  140.9 4.1 fusion.25
  145.0 2.9 copy.111
  147.8 2.8 reshape.789
  150.6 3.4 reshape.790
  154.1 7.8 %fusion.164 = (bf16[1,16,256,64]{2,3,1,0:T(8,128)(2,1)S(1)}, f32[1,16,256,64]{2,3,1,0:T(8,128)}) fusion(bf16[16,1024,64]{1,2,0:T(8,128)(2,1)S(1)} %reshape.790, bf16[1,16,256,1024]{3,2,1,0:T(8,128)(2,1)} %fusion.22), kind=kOutput, calls=%fused_computation.398 | convolution fusion | flops 537133056 | bytes 12058624 | tf_op jit(solution)/shard_map/shqk,shkd->shqd/dot_general | solution.py:275
  162.0 2.8 pad_maximum_fusion.10
  164.8 2.5 copy.115
  167.3 4.6 pad_maximum_fusion.9
  171.9 3.0 pad_maximum_fusion.5
  175.3 4.9 pad_maximum_fusion.4
  182.6 14.5 %multiply_convert_fusion.1 = (bf16[256,4096]{1,0:T(8,128)(2,1)}, f32[256,4096]{1,0:T(8,128)S(1)}, f32[256,4096]{1,0:T(8,128)S(1)}) fusion(f32[4096]{0:T(1024)S(1)} %bitcast.606, bf16[256,1024]{1,0:T(8,128)(2,1)S(1)} %constant_dynamic-update-slice_fusion.8, bf16[1024,2560]{1,0:T(8,128)(2,1)S(1)} %bitcast.547, bf16[1024,2560]{1,0:T(8,128)(2,1)S(1)} %bitcast.513), kind=kOutput, calls=%fused_computation.56 | convolution fusion | flops 2233466880 | bytes 21512192 | tf_op jit(solution)/shard_map/dot_general | solution.py:168
  205.4 4.7 fusion.166
  213.2 2.4 convolution_convert_fusion.1
  215.6 10.8 %fusion.20 = f32[256,4096]{1,0:T(8,128)} fusion(bf16[256,1024]{1,0:T(8,128)(2,1)S(1)} %add_convert_fusion.6, bf16[4096,512]{1,0:T(8,128)(2,1)} %bitcast.561, bf16[4096,512]{1,0:T(8,128)(2,1)} %bitcast.564), kind=kOutput, calls=%fused_computation.31 | convolution fusion | flops 2164260864 | bytes 13107200 | tf_op jit(solution)/shard_map/dot_general | solution.py:178
  228.6 2.6 slice_bitcast_fusion.4
  234.9 2.4 convolution_convert_fusion
  237.3 2.5 slice_bitcast_fusion.2
  247.4 5.6 %fusion.10 = bf16[4,512,1024]{2,1,0:T(8,128)(2,1)S(1)} fusion(bf16[4,512,1024]{2,1,0:T(8,128)(2,1)} %collective-permute-done.20, bf16[4,2,512,1024]{3,2,1,0:T(8,128)(2,1)} %bitcast.502), kind=kLoop, calls=%fused_computation.18 | loop fusion | flops 8388608 | bytes 12582912 | tf_op jit(solution)/shard_map/convert_element_type | solution.py:29
  252.9 2.5 fusion.158
  255.4 5.3 fusion.23
  262.1 4.1 fusion.9
  283.0 5.0 convert_reduce_fusion.1
  288.0 2.8 convert_element_type.668
  290.8 3.5 copy.146
  299.9 3.1 convolution_convert_fusion.3
  303.0 5.4 fusion.3
  308.4 3.4 fusion.93
  312.6 2.7 fusion.92
  316.9 11.4 %collective-permute-done.25 = bf16[1,2,128,2048]{3,2,1,0:T(8,128)(2,1)} collective-permute-done((bf16[1,2,128,2048]{3,2,1,0:T(8,128)(2,1)}, bf16[1,2,128,2048]{3,2,1,0:T(8,128)(2,1)}, u32[]{:S(2)}, u32[]{:S(2)}) %collective-permute-start.25) | collective-permute-done | bytes 1048608 | tf_op jit(solution)/shard_map/ppermute | solution.py:25
  329.9 2.9 convert_element_type.664
  336.7 8.4 %convert_reduce_fusion.5 = (bf16[16,64]{1,0:T(8,128)(2,1)S(1)}, bf16[16,256,64]{1,2,0:T(8,128)(2,1)}) fusion(bf16[16,1024,64]{1,2,0:T(8,128)(2,1)S(1)} %copy-done.46, bf16[1,16,256,1024]{3,2,1,0:T(8,128)(2,1)} %copy-done), kind=kOutput, calls=%fused_computation.186 | convolution fusion | flops 537918464 | bytes 11012096 | tf_op jit(solution)/shard_map/shqk,shkd->shqd/dot_general | solution.py:329
  354.4 6.2 %convolution_convert_fusion.2 = bf16[1024,2048]{1,0:T(8,128)(2,1)} fusion(bf16[1024,1024]{1,0:T(8,128)(2,1)S(1)} %copy-done.52, bf16[1024,2048]{0,1:T(8,128)(2,1)S(1)} %pad_maximum_fusion.11), kind=kOutput, calls=%fused_computation.70 | convolution fusion | flops 4297064448 | bytes 10485760 | tf_op jit(solution)/shard_map/dot_general | solution.py:172
  363.1 3.2 fusion.7
  369.4 7.9 %fusion.54 = bf16[1024,1024]{1,0:T(8,128)(2,1)} fusion(bf16[1024,2048]{0,1:T(8,128)(2,1)S(1)} %copy-done.31, bf16[1024,1536]{1,0:T(8,128)(2,1)} %bitcast.573, bf16[1024,1536]{1,0:T(8,128)(2,1)S(1)} %bitcast.570), kind=kOutput, calls=%fused_computation.108 | convolution fusion | flops 4303355904 | bytes 12582912 | tf_op jit(solution)/shard_map/dot_general | solution.py:178
  390.1 18.8 %collective-permute-done.35 = bf16[1024,512]{1,0:T(8,128)(2,1)S(1)} collective-permute-done((bf16[1024,512]{1,0:T(8,128)(2,1)S(1)}, bf16[1024,512]{1,0:T(8,128)(2,1)S(1)}, u32[]{:S(2)}, u32[]{:S(2)}) %collective-permute-start.35) | collective-permute-done | bytes 1048608 | tf_op jit(solution)/shard_map/ppermute | solution.py:25
  409.3 19.6 %collective-permute-done.27 = bf16[2,256,1024]{2,1,0:T(8,128)(2,1)S(1)} collective-permute-done((bf16[2,256,1024]{2,1,0:T(8,128)(2,1)S(1)}, bf16[2,256,1024]{2,1,0:T(8,128)(2,1)S(1)}, u32[]{:S(2)}, u32[]{:S(2)}) %collective-permute-start.27) | collective-permute-done | bytes 1048608 | tf_op jit(solution)/shard_map/ppermute | solution.py:25
  430.6 3.5 collective-permute-start.38
  436.4 9.8 %collective-permute-done.28 = bf16[1,256,1024]{2,1,0:T(8,128)(2,1)S(1)} collective-permute-done((bf16[1,256,1024]{2,1,0:T(8,128)(2,1)S(1)}, bf16[1,256,1024]{2,1,0:T(8,128)(2,1)S(1)}, u32[]{:S(2)}, u32[]{:S(2)}) %collective-permute-start.28) | collective-permute-done | bytes 524320 | tf_op jit(solution)/shard_map/ppermute | solution.py:25
  447.0 7.1 %collective-permute-done.38 = bf16[1024,256]{1,0:T(8,128)(2,1)S(1)} collective-permute-done((bf16[1024,256]{1,0:T(8,128)(2,1)S(1)}, bf16[1024,256]{1,0:T(8,128)(2,1)S(1)}, u32[]{:S(2)}, u32[]{:S(2)}) %collective-permute-start.38) | collective-permute-done | bytes 524320 | tf_op jit(solution)/shard_map/ppermute | solution.py:25
  455.3 32.3 %collective-permute-start.40 = (bf16[528,512]{1,0:T(8,128)(2,1)S(1)}, bf16[528,512]{1,0:T(8,128)(2,1)S(1)}, u32[]{:S(2)}, u32[]{:S(2)}) collective-permute-start(bf16[528,512]{1,0:T(8,128)(2,1)S(1)} %constant_dynamic-slice_fusion.1), channel_id=1, source_target_pairs={{0,8},{8,0},{16,24},{24,16},{1,9},{9,1},{17,25},{25,17},{2,10},{10... | collective-permute-start | bytes 1622024 | tf_op jit(solution)/shard_map/ppermute | solution.py:25
  487.9 10.9 %collective-permute-done.40 = bf16[528,512]{1,0:T(8,128)(2,1)S(1)} collective-permute-done((bf16[528,512]{1,0:T(8,128)(2,1)S(1)}, bf16[528,512]{1,0:T(8,128)(2,1)S(1)}, u32[]{:S(2)}, u32[]{:S(2)}) %collective-permute-start.40) | collective-permute-done | bytes 540704 | tf_op jit(solution)/shard_map/ppermute | solution.py:25
  503.0 25.7 %collective-permute-done.42 = bf16[528,256]{1,0:T(8,128)(2,1)S(1)} collective-permute-done((bf16[528,256]{1,0:T(8,128)(2,1)S(1)}, bf16[528,256]{1,0:T(8,128)(2,1)S(1)}, u32[]{:S(2)}, u32[]{:S(2)}) %collective-permute-start.42) | collective-permute-done | bytes 270368 | tf_op jit(solution)/shard_map/ppermute | solution.py:25
  529.3 2.6 collective-permute-start.43
  533.0 5.6 %collective-permute-done.43 = bf16[528,256]{1,0:T(8,128)(2,1)S(1)} collective-permute-done((bf16[528,256]{1,0:T(8,128)(2,1)S(1)}, bf16[528,256]{1,0:T(8,128)(2,1)S(1)}, u32[]{:S(2)}, u32[]{:S(2)}) %collective-permute-start.43) | collective-permute-done | bytes 270368 | tf_op jit(solution)/shard_map/ppermute | solution.py:25
  542.1 7.2 %collective-permute-done.44 = bf16[528,512]{1,0:T(8,128)(2,1)S(1)} collective-permute-done((bf16[528,512]{1,0:T(8,128)(2,1)S(1)}, bf16[528,512]{1,0:T(8,128)(2,1)S(1)}, u32[]{:S(2)}, u32[]{:S(2)}) %collective-permute-start.44) | collective-permute-done | bytes 540704 | tf_op jit(solution)/shard_map/ppermute | solution.py:25
  (420 shorter events, 154.1 us)
Async XLA Ops:
  0.6 25.6 %collective-permute-start.12 = (bf16[1,256,1024]{2,1,0:T(8,128)(2,1)}, bf16[1,256,1024]{2,1,0:T(8,128)(2,1)}, u32[]{:S(2)}, u32[]{:S(2)}) collective-permute-start(bf16[1,256,1024]{2,1,0:T(8,128)(2,1)} %param.15), channel_id=1, source_target_pairs={{0,24},{8,16},{16,8},{24,0},{1,25},{9,17},{17,9},{25,1},{2,26},{10... | collective-permute-start | bytes 1572872 | tf_op jit(solution)/shard_map/ppermute | solution.py:25
  7.1 10.6 %collective-permute-start.2 = (bf16[1,128,1536]{2,1,0:T(8,128)(2,1)S(1)}, bf16[1,128,1536]{2,1,0:T(8,128)(2,1)S(1)}, u32[]{:S(2)}, u32[]{:S(2)}) collective-permute-start(bf16[1,128,1536]{2,1,0:T(8,128)(2,1)S(1)} %get-tuple-element.147), channel_id=1, source_target_pairs={{0,4},{1,5},{2,6},{3,7},{4,0},{5,1},{6,2},{7,3},{8,12},{9,13},{10,... | collective-permute-start | bytes 1179656 | tf_op jit(solution)/shard_map/ppermute | solution.py:25
  8.7 13.3 %collective-permute-start = (bf16[1,128,1536]{2,1,0:T(8,128)(2,1)S(1)}, bf16[1,128,1536]{2,1,0:T(8,128)(2,1)S(1)}, u32[]{:S(2)}, u32[]{:S(2)}) collective-permute-start(bf16[1,128,1536]{2,1,0:T(8,128)(2,1)S(1)} %get-tuple-element.148), channel_id=1, source_target_pairs={{0,2},{1,3},{2,0},{3,1},{4,6},{5,7},{6,4},{7,5},{8,10},{9,11},{10,... | collective-permute-start | bytes 1179656 | tf_op jit(solution)/shard_map/ppermute | solution.py:25
  12.5 41.6 %copy-start.42 = (bf16[1,128,2560]{2,1,0:T(8,128)(2,1)}, bf16[1,128,2560]{2,1,0:T(8,128)(2,1)S(1)}, u32[]{:S(2)}) copy-start(bf16[1,128,2560]{2,1,0:T(8,128)(2,1)S(1)} %get-tuple-element.58) | copy-start | bytes 1966084
  20.5 28.0 %collective-permute-start.3 = (bf16[2,128,1536]{2,1,0:T(8,128)(2,1)}, bf16[2,128,1536]{2,1,0:T(8,128)(2,1)}, u32[]{:S(2)}, u32[]{:S(2)}) collective-permute-start(bf16[2,128,1536]{2,1,0:T(8,128)(2,1)} %get-tuple-element.144), channel_id=1, source_target_pairs={{0,2},{1,3},{2,0},{3,1},{4,6},{5,7},{6,4},{7,5},{8,10},{9,11},{10,... | collective-permute-start | bytes 2359304 | tf_op jit(solution)/shard_map/ppermute | solution.py:25
  24.7 25.1 %collective-permute-start.1 = (bf16[2,128,1536]{2,1,0:T(8,128)(2,1)}, bf16[2,128,1536]{2,1,0:T(8,128)(2,1)}, u32[]{:S(2)}, u32[]{:S(2)}) collective-permute-start(bf16[2,128,1536]{2,1,0:T(8,128)(2,1)} %get-tuple-element.150), channel_id=1, source_target_pairs={{0,4},{1,5},{2,6},{3,7},{4,0},{5,1},{6,2},{7,3},{8,12},{9,13},{10,... | collective-permute-start | bytes 2359304 | tf_op jit(solution)/shard_map/ppermute | solution.py:25
  28.5 25.5 %collective-permute-start.13 = (bf16[2,256,1024]{2,1,0:T(8,128)(2,1)}, bf16[2,256,1024]{2,1,0:T(8,128)(2,1)}, u32[]{:S(2)}, u32[]{:S(2)}) collective-permute-start(bf16[2,256,1024]{2,1,0:T(8,128)(2,1)} %get-tuple-element.142), channel_id=1, source_target_pairs={{0,8},{8,0},{16,24},{24,16},{1,9},{9,1},{17,25},{25,17},{2,10},{10... | collective-permute-start | bytes 3145736 | tf_op jit(solution)/shard_map/ppermute | solution.py:25
  51.0 38.6 %collective-permute-start.14 = (bf16[4,128,1536]{2,1,0:T(8,128)(2,1)S(1)}, bf16[4,128,1536]{2,1,0:T(8,128)(2,1)S(1)}, u32[]{:S(2)}, u32[]{:S(2)}) collective-permute-start(bf16[4,128,1536]{2,1,0:T(8,128)(2,1)S(1)} %bitcast.545), channel_id=1, source_target_pairs={{0,1},{1,0},{2,3},{3,2},{4,5},{5,4},{6,7},{7,6},{8,9},{9,8},{10,11... | collective-permute-start | bytes 4718600 | tf_op jit(solution)/shard_map/ppermute | solution.py:25
  51.5 36.1 %collective-permute-start.15 = (bf16[4,128,1536]{2,1,0:T(8,128)(2,1)S(1)}, bf16[4,128,1536]{2,1,0:T(8,128)(2,1)S(1)}, u32[]{:S(2)}, u32[]{:S(2)}) collective-permute-start(bf16[4,128,1536]{2,1,0:T(8,128)(2,1)S(1)} %bitcast.543), channel_id=1, source_target_pairs={{0,1},{1,0},{2,3},{3,2},{4,5},{5,4},{6,7},{7,6},{8,9},{9,8},{10,11... | collective-permute-start | bytes 4718600 | tf_op jit(solution)/shard_map/ppermute | solution.py:25
  51.6 14.8 %collective-permute-start.10 = (bf16[1,512,512]{2,1,0:T(8,128)(2,1)S(1)}, bf16[1,512,512]{2,1,0:T(8,128)(2,1)S(1)}, u32[]{:S(2)}, u32[]{:S(2)}) collective-permute-start(bf16[1,512,512]{2,1,0:T(8,128)(2,1)S(1)} %get-tuple-element.60), channel_id=1, source_target_pairs={{0,4},{1,5},{2,6},{3,7},{4,0},{5,1},{6,2},{7,3},{8,12},{9,13},{10,... | collective-permute-start | bytes 1572872 | tf_op jit(solution)/shard_map/ppermute | solution.py:25
  52.2 16.3 %collective-permute-start.8 = (bf16[1,512,512]{2,1,0:T(8,128)(2,1)S(1)}, bf16[1,512,512]{2,1,0:T(8,128)(2,1)S(1)}, u32[]{:S(2)}, u32[]{:S(2)}) collective-permute-start(bf16[1,512,512]{2,1,0:T(8,128)(2,1)S(1)} %get-tuple-element.59), channel_id=1, source_target_pairs={{0,2},{1,3},{2,0},{3,1},{4,6},{5,7},{6,4},{7,5},{8,10},{9,11},{10,... | collective-permute-start | bytes 1572872 | tf_op jit(solution)/shard_map/ppermute | solution.py:25
  54.0 25.8 %collective-permute-start.6 = (bf16[1,128,2560]{2,1,0:T(8,128)(2,1)S(1)}, bf16[1,128,2560]{2,1,0:T(8,128)(2,1)S(1)}, u32[]{:S(2)}, u32[]{:S(2)}) collective-permute-start(bf16[1,128,2560]{2,1,0:T(8,128)(2,1)S(1)} %get-tuple-element.58), channel_id=1, source_target_pairs={{0,4},{1,5},{2,6},{3,7},{4,0},{5,1},{6,2},{7,3},{8,12},{9,13},{10,... | collective-permute-start | bytes 1966088 | tf_op jit(solution)/shard_map/ppermute | solution.py:25
  66.4 17.9 %collective-permute-start.4 = (bf16[1,128,2560]{2,1,0:T(8,128)(2,1)}, bf16[1,128,2560]{2,1,0:T(8,128)(2,1)S(1)}, u32[]{:S(2)}, u32[]{:S(2)}) collective-permute-start(bf16[1,128,2560]{2,1,0:T(8,128)(2,1)} %get-tuple-element.57), channel_id=1, source_target_pairs={{0,2},{1,3},{2,0},{3,1},{4,6},{5,7},{6,4},{7,5},{8,10},{9,11},{10,... | collective-permute-start | bytes 1966088 | tf_op jit(solution)/shard_map/ppermute | solution.py:25
  67.0 22.9 %copy-start.51 = (bf16[1024,1024]{1,0:T(8,128)(2,1)}, bf16[1024,1024]{1,0:T(8,128)(2,1)S(1)}, u32[]{:S(2)}) copy-start(bf16[1024,1024]{1,0:T(8,128)(2,1)S(1)} %dynamic-slice_dynamic-update-slice_fusion.16) | copy-start | bytes 6291460
  67.0 13.4 %copy-start.43 = (bf16[1,128,2560]{2,1,0:T(8,128)(2,1)S(1)}, bf16[1,128,2560]{2,1,0:T(8,128)(2,1)}, u32[]{:S(2)}) copy-start(bf16[1,128,2560]{2,1,0:T(8,128)(2,1)} %copy-done.42) | copy-start | bytes 1966084
  68.5 47.9 %collective-permute-start.11 = (bf16[2,512,512]{2,1,0:T(8,128)(2,1)}, bf16[2,512,512]{2,1,0:T(8,128)(2,1)}, u32[]{:S(2)}, u32[]{:S(2)}) collective-permute-start(bf16[2,512,512]{2,1,0:T(8,128)(2,1)} %get-tuple-element.136), channel_id=1, source_target_pairs={{0,2},{1,3},{2,0},{3,1},{4,6},{5,7},{6,4},{7,5},{8,10},{9,11},{10,... | collective-permute-start | bytes 3145736 | tf_op jit(solution)/shard_map/ppermute | solution.py:25
  79.9 39.3 %collective-permute-start.9 = (bf16[2,512,512]{2,1,0:T(8,128)(2,1)}, bf16[2,512,512]{2,1,0:T(8,128)(2,1)}, u32[]{:S(2)}, u32[]{:S(2)}) collective-permute-start(bf16[2,512,512]{2,1,0:T(8,128)(2,1)} %get-tuple-element.138), channel_id=1, source_target_pairs={{0,4},{1,5},{2,6},{3,7},{4,0},{5,1},{6,2},{7,3},{8,12},{9,13},{10,... | collective-permute-start | bytes 3145736 | tf_op jit(solution)/shard_map/ppermute | solution.py:25
  84.3 48.6 %collective-permute-start.7 = (bf16[2,128,2560]{2,1,0:T(8,128)(2,1)}, bf16[2,128,2560]{2,1,0:T(8,128)(2,1)}, u32[]{:S(2)}, u32[]{:S(2)}) collective-permute-start(bf16[2,128,2560]{2,1,0:T(8,128)(2,1)} %get-tuple-element.125), channel_id=1, source_target_pairs={{0,2},{1,3},{2,0},{3,1},{4,6},{5,7},{6,4},{7,5},{8,10},{9,11},{10,... | collective-permute-start | bytes 3932168 | tf_op jit(solution)/shard_map/ppermute | solution.py:25
  87.5 48.4 %collective-permute-start.5 = (bf16[2,128,2560]{2,1,0:T(8,128)(2,1)}, bf16[2,128,2560]{2,1,0:T(8,128)(2,1)}, u32[]{:S(2)}, u32[]{:S(2)}) collective-permute-start(bf16[2,128,2560]{2,1,0:T(8,128)(2,1)} %get-tuple-element.127), channel_id=1, source_target_pairs={{0,4},{1,5},{2,6},{3,7},{4,0},{5,1},{6,2},{7,3},{8,12},{9,13},{10,... | collective-permute-start | bytes 3932168 | tf_op jit(solution)/shard_map/ppermute | solution.py:25
  139.1 22.9 %collective-permute-start.19 = (bf16[4,512,512]{2,1,0:T(8,128)(2,1)}, bf16[4,512,512]{2,1,0:T(8,128)(2,1)}, u32[]{:S(2)}, u32[]{:S(2)}) collective-permute-start(bf16[4,512,512]{2,1,0:T(8,128)(2,1)} %bitcast.45), channel_id=1, source_target_pairs={{0,1},{1,0},{2,3},{3,2},{4,5},{5,4},{6,7},{7,6},{8,9},{9,8},{10,11... | collective-permute-start | bytes 6291464 | tf_op jit(solution)/shard_map/ppermute | solution.py:25
  139.1 32.8 %collective-permute-start.17 = (bf16[4,128,2560]{2,1,0:T(8,128)(2,1)}, bf16[4,128,2560]{2,1,0:T(8,128)(2,1)}, u32[]{:S(2)}, u32[]{:S(2)}) collective-permute-start(bf16[4,128,2560]{2,1,0:T(8,128)(2,1)} %bitcast.31), channel_id=1, source_target_pairs={{0,1},{1,0},{2,3},{3,2},{4,5},{5,4},{6,7},{7,6},{8,9},{9,8},{10,11... | collective-permute-start | bytes 7864328 | tf_op jit(solution)/shard_map/ppermute | solution.py:25
  140.4 26.9 %collective-permute-start.18 = (bf16[4,512,512]{2,1,0:T(8,128)(2,1)}, bf16[4,512,512]{2,1,0:T(8,128)(2,1)}, u32[]{:S(2)}, u32[]{:S(2)}) collective-permute-start(bf16[4,512,512]{2,1,0:T(8,128)(2,1)} %bitcast.37), channel_id=1, source_target_pairs={{0,1},{1,0},{2,3},{3,2},{4,5},{5,4},{6,7},{7,6},{8,9},{9,8},{10,11... | collective-permute-start | bytes 6291464 | tf_op jit(solution)/shard_map/ppermute | solution.py:25
  140.4 34.9 %collective-permute-start.16 = (bf16[4,128,2560]{2,1,0:T(8,128)(2,1)}, bf16[4,128,2560]{2,1,0:T(8,128)(2,1)}, u32[]{:S(2)}, u32[]{:S(2)}) collective-permute-start(bf16[4,128,2560]{2,1,0:T(8,128)(2,1)} %bitcast.23), channel_id=1, source_target_pairs={{0,1},{1,0},{2,3},{3,2},{4,5},{5,4},{6,7},{7,6},{8,9},{9,8},{10,11... | collective-permute-start | bytes 7864328 | tf_op jit(solution)/shard_map/ppermute | solution.py:25
  162.0 18.2 %copy-start.44 = (bf16[256,1024]{0,1:T(8,128)(2,1)}, bf16[256,1024]{0,1:T(8,128)(2,1)S(1)}, u32[]{:S(2)}) copy-start(bf16[256,1024]{0,1:T(8,128)(2,1)S(1)} %constant_dynamic-update-slice_fusion) | copy-start | bytes 1572868
  197.2 8.2 %copy-start.32 = (bf16[4,2,1,512,512]{4,3,1,0,2:T(8,128)(2,1)S(1)}, bf16[4,2,1,512,512]{4,3,1,0,2:T(8,128)(2,1)}, u32[]{:S(2)}) copy-start(bf16[4,2,1,512,512]{4,3,1,0,2:T(8,128)(2,1)} %copy.115) | copy-start | bytes 12582916
  215.6 13.0 %copy-start.1 = (bf16[4096,1024]{1,0:T(8,128)(2,1)}, bf16[4096,1024]{1,0:T(8,128)(2,1)S(1)}, u32[]{:S(2)}) copy-start(bf16[4096,1024]{1,0:T(8,128)(2,1)S(1)} %convolution_convert_fusion.1) | copy-start | bytes 25165828
  231.2 16.1 %collective-permute-start.20 = (bf16[4,512,1024]{2,1,0:T(8,128)(2,1)}, bf16[4,512,1024]{2,1,0:T(8,128)(2,1)}, u32[]{:S(2)}, u32[]{:S(2)}) collective-permute-start(bf16[4,512,1024]{2,1,0:T(8,128)(2,1)} %slice_bitcast_fusion.4), channel_id=1, source_target_pairs={{0,1},{1,0},{2,3},{3,2},{4,5},{5,4},{6,7},{7,6},{8,9},{9,8},{10,11... | collective-permute-start | bytes 12582920 | tf_op jit(solution)/shard_map/ppermute | solution.py:25
  241.9 20.2 %collective-permute-start.23 = (bf16[4,128,4096]{2,1,0:T(8,128)(2,1)}, bf16[4,128,4096]{2,1,0:T(8,128)(2,1)}, u32[]{:S(2)}, u32[]{:S(2)}) collective-permute-start(bf16[4,128,4096]{2,1,0:T(8,128)(2,1)} %slice_bitcast_fusion.2), channel_id=1, source_target_pairs={{0,1},{1,0},{2,3},{3,2},{4,5},{5,4},{6,7},{7,6},{8,9},{9,8},{10,11... | collective-permute-start | bytes 12582920 | tf_op jit(solution)/shard_map/ppermute | solution.py:25
  252.9 9.2 %slice-start = ((s8[8388608]{0:T(1024)(128)(4,1)}), s8[4194304]{0:T(1024)(128)(4,1)S(1)}, s32[]{:S(2)}) async-start(s8[8388608]{0:T(1024)(128)(4,1)} %bitcast.506), calls=%async_computation | async-start | bytes 8388608
  271.1 9.4 %copy-start.10 = (bf16[4,512,512]{2,1,0:T(8,128)(2,1)S(1)}, bf16[4,512,512]{2,1,0:T(8,128)(2,1)}, u32[]{:S(2)}) copy-start(bf16[4,512,512]{2,1,0:T(8,128)(2,1)} %get-tuple-element.72) | copy-start | bytes 6291460
  279.9 28.5 %collective-permute-start.22 = (bf16[1,2,512,512]{3,2,1,0:T(8,128)(2,1)}, bf16[1,2,512,512]{3,2,1,0:T(8,128)(2,1)}, u32[]{:S(2)}, u32[]{:S(2)}) collective-permute-start(bf16[1,2,512,512]{3,2,1,0:T(8,128)(2,1)} %slice_bitcast_fusion.16), channel_id=1, source_target_pairs={{0,4},{1,5},{2,6},{3,7},{4,0},{5,1},{6,2},{7,3},{8,12},{9,13},{10,... | collective-permute-start | bytes 3145736 | tf_op jit(solution)/shard_map/ppermute | solution.py:25
  281.5 30.3 %collective-permute-start.21 = (bf16[2,1,512,512]{3,2,0,1:T(8,128)(2,1)}, bf16[2,1,512,512]{3,2,0,1:T(8,128)(2,1)}, u32[]{:S(2)}, u32[]{:S(2)}) collective-permute-start(bf16[2,1,512,512]{3,2,0,1:T(8,128)(2,1)} %slice_bitcast_fusion.18), channel_id=1, source_target_pairs={{0,2},{1,3},{2,0},{3,1},{4,6},{5,7},{6,4},{7,5},{8,10},{9,11},{10,... | collective-permute-start | bytes 3145736 | tf_op jit(solution)/shard_map/ppermute | solution.py:25
  295.4 32.9 %collective-permute-start.25 = (bf16[1,2,128,2048]{3,2,1,0:T(8,128)(2,1)}, bf16[1,2,128,2048]{3,2,1,0:T(8,128)(2,1)}, u32[]{:S(2)}, u32[]{:S(2)}) collective-permute-start(bf16[1,2,128,2048]{3,2,1,0:T(8,128)(2,1)} %slice_bitcast_fusion.12), channel_id=1, source_target_pairs={{0,4},{1,5},{2,6},{3,7},{4,0},{5,1},{6,2},{7,3},{8,12},{9,13},{10,... | collective-permute-start | bytes 3145736 | tf_op jit(solution)/shard_map/ppermute | solution.py:25
  296.9 48.2 %collective-permute-start.24 = (bf16[2,1,128,2048]{3,2,0,1:T(8,128)(2,1)}, bf16[2,1,128,2048]{3,2,0,1:T(8,128)(2,1)}, u32[]{:S(2)}, u32[]{:S(2)}) collective-permute-start(bf16[2,1,128,2048]{3,2,0,1:T(8,128)(2,1)} %slice_bitcast_fusion.14), channel_id=1, source_target_pairs={{0,2},{1,3},{2,0},{3,1},{4,6},{5,7},{6,4},{7,5},{8,10},{9,11},{10,... | collective-permute-start | bytes 3145736 | tf_op jit(solution)/shard_map/ppermute | solution.py:25
  308.3 8.6 %copy-start = (bf16[1,16,256,1024]{3,2,1,0:T(8,128)(2,1)}, bf16[1,16,256,1024]{3,2,1,0:T(8,128)(2,1)S(1)}, u32[]{:S(2)}) copy-start(bf16[1,16,256,1024]{3,2,1,0:T(8,128)(2,1)S(1)} %fusion.3) | copy-start | bytes 25165828
  315.3 13.0 %copy-start.16 = (bf16[4,128,2048]{2,1,0:T(8,128)(2,1)S(1)}, bf16[4,128,2048]{2,1,0:T(8,128)(2,1)}, u32[]{:S(2)}) copy-start(bf16[4,128,2048]{2,1,0:T(8,128)(2,1)} %get-tuple-element.78) | copy-start | bytes 6291460
  336.7 17.7 %copy-start.30 = (bf16[1024,2048]{0,1:T(8,128)(2,1)}, bf16[1024,2048]{0,1:T(8,128)(2,1)S(1)}, u32[]{:S(2)}) copy-start(bf16[1024,2048]{0,1:T(8,128)(2,1)S(1)} %pad_maximum_fusion.11) | copy-start | bytes 12582916
  336.7 8.4 %copy-start.14 = (bf16[4,128,2048]{2,1,0:T(8,128)(2,1)S(1)}, bf16[4,128,2048]{2,1,0:T(8,128)(2,1)}, u32[]{:S(2)}) copy-start(bf16[4,128,2048]{2,1,0:T(8,128)(2,1)} %get-tuple-element.77) | copy-start | bytes 6291460
  345.1 9.3 %copy-start.52 = (bf16[1024,1024]{1,0:T(8,128)(2,1)S(1)}, bf16[1024,1024]{1,0:T(8,128)(2,1)}, u32[]{:S(2)}) copy-start(bf16[1024,1024]{1,0:T(8,128)(2,1)} %copy-done.51) | copy-start | bytes 6291460
  346.9 13.7 %copy-start.28 = (bf16[2,128,2048]{2,1,0:T(8,128)(2,1)}, bf16[2,128,2048]{2,1,0:T(8,128)(2,1)S(1)}, u32[]{:S(2)}) copy-start(bf16[2,128,2048]{2,1,0:T(8,128)(2,1)S(1)} %fusion.94) | copy-start | bytes 3145732
  347.8 32.2 %collective-permute-start.33 = (bf16[1,1,128,2048]{3,2,1,0:T(8,128)(2,1)}, bf16[1,1,128,2048]{3,2,1,0:T(8,128)(2,1)}, u32[]{:S(2)}, u32[]{:S(2)}) collective-permute-start(bf16[1,1,128,2048]{3,2,1,0:T(8,128)(2,1)} %slice_bitcast_fusion.26), channel_id=1, source_target_pairs={{0,4},{1,5},{2,6},{3,7},{4,0},{5,1},{6,2},{7,3},{8,12},{9,13},{10,... | collective-permute-start | bytes 1572872 | tf_op jit(solution)/shard_map/ppermute | solution.py:25
  349.2 32.0 %collective-permute-start.34 = (bf16[1,1,128,2048]{3,2,1,0:T(8,128)(2,1)}, bf16[1,1,128,2048]{3,2,1,0:T(8,128)(2,1)}, u32[]{:S(2)}, u32[]{:S(2)}) collective-permute-start(bf16[1,1,128,2048]{3,2,1,0:T(8,128)(2,1)} %slice_bitcast_fusion.24), channel_id=1, source_target_pairs={{0,2},{1,3},{2,0},{3,1},{4,6},{5,7},{6,4},{7,5},{8,10},{9,11},{10,... | collective-permute-start | bytes 1572872 | tf_op jit(solution)/shard_map/ppermute | solution.py:25
  351.6 27.1 %collective-permute-start.31 = (bf16[1,1,512,512]{3,2,1,0:T(8,128)(2,1)}, bf16[1,1,512,512]{3,2,1,0:T(8,128)(2,1)}, u32[]{:S(2)}, u32[]{:S(2)}) collective-permute-start(bf16[1,1,512,512]{3,2,1,0:T(8,128)(2,1)} %slice_bitcast_fusion.30), channel_id=1, source_target_pairs={{0,4},{1,5},{2,6},{3,7},{4,0},{5,1},{6,2},{7,3},{8,12},{9,13},{10,... | collective-permute-start | bytes 1572872 | tf_op jit(solution)/shard_map/ppermute | solution.py:25
  352.8 7.9 %copy-start.53 = (bf16[1024]{0:T(1024)(128)(2,1)S(1)}, bf16[1024]{0:T(1024)(128)(2,1)}, u32[]{:S(2)}) copy-start(bf16[1024]{0:T(1024)(128)(2,1)} %convert_reduce_fusion.2) | copy-start | bytes 6148
  352.8 24.6 %collective-permute-start.32 = (bf16[1,1,512,512]{3,2,1,0:T(8,128)(2,1)}, bf16[1,1,512,512]{3,2,1,0:T(8,128)(2,1)}, u32[]{:S(2)}, u32[]{:S(2)}) collective-permute-start(bf16[1,1,512,512]{3,2,1,0:T(8,128)(2,1)} %slice_bitcast_fusion.28), channel_id=1, source_target_pairs={{0,2},{1,3},{2,0},{3,1},{4,6},{5,7},{6,4},{7,5},{8,10},{9,11},{10,... | collective-permute-start | bytes 1572872 | tf_op jit(solution)/shard_map/ppermute | solution.py:25
  366.6 10.8 %copy-start.25 = (bf16[2,512,512]{2,1,0:T(8,128)(2,1)S(1)}, bf16[2,512,512]{2,1,0:T(8,128)(2,1)}, u32[]{:S(2)}) copy-start(bf16[2,512,512]{2,1,0:T(8,128)(2,1)} %fusion.93) | copy-start | bytes 3145732
  366.6 12.1 %copy-start.27 = (bf16[2,512,512]{2,1,0:T(8,128)(2,1)S(1)}, bf16[2,512,512]{2,1,0:T(8,128)(2,1)}, u32[]{:S(2)}) copy-start(bf16[2,512,512]{2,1,0:T(8,128)(2,1)} %fusion.92) | copy-start | bytes 3145732
  366.6 16.2 %collective-permute-start.26 = (bf16[4,128,4224]{2,1,0:T(8,128)(2,1)S(1)}, bf16[4,128,4224]{2,1,0:T(8,128)(2,1)S(1)}, u32[]{:S(2)}, u32[]{:S(2)}) collective-permute-start(bf16[4,128,4224]{2,1,0:T(8,128)(2,1)S(1)} %slice_bitcast_fusion), channel_id=1, source_target_pairs={{0,1},{1,0},{2,3},{3,2},{4,5},{5,4},{6,7},{7,6},{8,9},{9,8},{10,11... | collective-permute-start | bytes 12976136 | tf_op jit(solution)/shard_map/ppermute | solution.py:25
  382.7 26.2 %collective-permute-start.35 = (bf16[1024,512]{1,0:T(8,128)(2,1)S(1)}, bf16[1024,512]{1,0:T(8,128)(2,1)S(1)}, u32[]{:S(2)}, u32[]{:S(2)}) collective-permute-start(bf16[1024,512]{1,0:T(8,128)(2,1)S(1)} %constant_dynamic-slice_fusion.3), channel_id=1, source_target_pairs={{0,8},{8,0},{16,24},{24,16},{1,9},{9,1},{17,25},{25,17},{2,10},{10... | collective-permute-start | bytes 3145736 | tf_op jit(solution)/shard_map/ppermute | solution.py:25
  385.7 43.2 %collective-permute-start.27 = (bf16[2,256,1024]{2,1,0:T(8,128)(2,1)S(1)}, bf16[2,256,1024]{2,1,0:T(8,128)(2,1)S(1)}, u32[]{:S(2)}, u32[]{:S(2)}) collective-permute-start(bf16[2,256,1024]{2,1,0:T(8,128)(2,1)S(1)} %slice_bitcast_fusion.10), channel_id=1, source_target_pairs={{0,8},{8,0},{16,24},{24,16},{1,9},{9,1},{17,25},{25,17},{2,10},{10... | collective-permute-start | bytes 3145736 | tf_op jit(solution)/shard_map/ppermute | solution.py:25
  387.8 42.0 %collective-permute-start.29 = (bf16[2,1,128,2048]{3,2,0,1:T(8,128)(2,1)S(1)}, bf16[2,1,128,2048]{3,2,0,1:T(8,128)(2,1)S(1)}, u32[]{:S(2)}, u32[]{:S(2)}) collective-permute-start(bf16[2,1,128,2048]{3,2,0,1:T(8,128)(2,1)S(1)} %slice_bitcast_fusion.8), channel_id=1, source_target_pairs={{0,2},{1,3},{2,0},{3,1},{4,6},{5,7},{6,4},{7,5},{8,10},{9,11},{10,... | collective-permute-start | bytes 3145736 | tf_op jit(solution)/shard_map/ppermute | solution.py:25
  388.5 41.8 %collective-permute-start.30 = (bf16[1,2,128,2176]{3,2,1,0:T(8,128)(2,1)S(1)}, bf16[1,2,128,2176]{3,2,1,0:T(8,128)(2,1)S(1)}, u32[]{:S(2)}, u32[]{:S(2)}) collective-permute-start(bf16[1,2,128,2176]{3,2,1,0:T(8,128)(2,1)S(1)} %slice_bitcast_fusion.6), channel_id=1, source_target_pairs={{0,4},{1,5},{2,6},{3,7},{4,0},{5,1},{6,2},{7,3},{8,12},{9,13},{10,... | collective-permute-start | bytes 3342344 | tf_op jit(solution)/shard_map/ppermute | solution.py:25
  429.4 16.8 %collective-permute-start.28 = (bf16[1,256,1024]{2,1,0:T(8,128)(2,1)S(1)}, bf16[1,256,1024]{2,1,0:T(8,128)(2,1)S(1)}, u32[]{:S(2)}, u32[]{:S(2)}) collective-permute-start(bf16[1,256,1024]{2,1,0:T(8,128)(2,1)S(1)} %slice_bitcast_fusion.32), channel_id=1, source_target_pairs={{0,24},{8,16},{16,8},{24,0},{1,25},{9,17},{17,9},{25,1},{2,26},{10... | collective-permute-start | bytes 1572872 | tf_op jit(solution)/shard_map/ppermute | solution.py:25
  430.2 15.9 %copy-start.40 = (bf16[4,2,1,128,1536]{4,3,1,0,2:T(8,128)(2,1)S(1)}, bf16[4,2,1,128,1536]{4,3,1,0,2:T(8,128)(2,1)}, u32[]{:S(2)}) copy-start(bf16[4,2,1,128,1536]{4,3,1,0,2:T(8,128)(2,1)} %copy-done.38) | copy-start | bytes 9437188
  430.2 15.9 %copy-start.48 = (bf16[16,256,64]{1,2,0:T(8,128)(2,1)S(1)}, bf16[16,256,64]{1,2,0:T(8,128)(2,1)}, u32[]{:S(2)}) copy-start(bf16[16,256,64]{1,2,0:T(8,128)(2,1)} %get-tuple-element.185) | copy-start | bytes 1572868
  430.6 23.5 %collective-permute-start.38 = (bf16[1024,256]{1,0:T(8,128)(2,1)S(1)}, bf16[1024,256]{1,0:T(8,128)(2,1)S(1)}, u32[]{:S(2)}, u32[]{:S(2)}) collective-permute-start(bf16[1024,256]{1,0:T(8,128)(2,1)S(1)} %constant_dynamic-slice_fusion.2), channel_id=1, source_target_pairs={{0,24},{8,16},{16,8},{24,0},{1,25},{9,17},{17,9},{25,1},{2,26},{10... | collective-permute-start | bytes 1572872 | tf_op jit(solution)/shard_map/ppermute | solution.py:25
  434.1 20.3 %collective-permute-start.37 = (bf16[1,1,128,2176]{3,2,1,0:T(8,128)(2,1)S(1)}, bf16[1,1,128,2176]{3,2,1,0:T(8,128)(2,1)S(1)}, u32[]{:S(2)}, u32[]{:S(2)}) collective-permute-start(bf16[1,1,128,2176]{3,2,1,0:T(8,128)(2,1)S(1)} %slice_bitcast_fusion.20), channel_id=1, source_target_pairs={{0,2},{1,3},{2,0},{3,1},{4,6},{5,7},{6,4},{7,5},{8,10},{9,11},{10,... | collective-permute-start | bytes 1671176 | tf_op jit(solution)/shard_map/ppermute | solution.py:25
  434.7 19.5 %collective-permute-start.36 = (bf16[1,1,128,2048]{3,2,1,0:T(8,128)(2,1)S(1)}, bf16[1,1,128,2048]{3,2,1,0:T(8,128)(2,1)S(1)}, u32[]{:S(2)}, u32[]{:S(2)}) collective-permute-start(bf16[1,1,128,2048]{3,2,1,0:T(8,128)(2,1)S(1)} %slice_bitcast_fusion.22), channel_id=1, source_target_pairs={{0,4},{1,5},{2,6},{3,7},{4,0},{5,1},{6,2},{7,3},{8,12},{9,13},{10,... | collective-permute-start | bytes 1572872 | tf_op jit(solution)/shard_map/ppermute | solution.py:25
  454.8 32.9 %collective-permute-start.39 = (bf16[1024,256]{1,0:T(8,128)(2,1)S(1)}, bf16[1024,256]{1,0:T(8,128)(2,1)S(1)}, u32[]{:S(2)}, u32[]{:S(2)}) collective-permute-start(bf16[1024,256]{1,0:T(8,128)(2,1)S(1)} %add_convert_fusion.3), channel_id=1, source_target_pairs={{0,24},{8,16},{16,8},{24,0},{1,25},{9,17},{17,9},{25,1},{2,26},{10... | collective-permute-start | bytes 1572872 | tf_op jit(solution)/shard_map/ppermute | solution.py:25
  455.3 43.4 %collective-permute-start.40 = (bf16[528,512]{1,0:T(8,128)(2,1)S(1)}, bf16[528,512]{1,0:T(8,128)(2,1)S(1)}, u32[]{:S(2)}, u32[]{:S(2)}) collective-permute-start(bf16[528,512]{1,0:T(8,128)(2,1)S(1)} %constant_dynamic-slice_fusion.1), channel_id=1, source_target_pairs={{0,8},{8,0},{16,24},{24,16},{1,9},{9,1},{17,25},{25,17},{2,10},{10... | collective-permute-start | bytes 1622024 | tf_op jit(solution)/shard_map/ppermute | solution.py:25
  498.9 29.8 %collective-permute-start.41 = (bf16[1024,512]{1,0:T(8,128)(2,1)S(1)}, bf16[1024,512]{1,0:T(8,128)(2,1)S(1)}, u32[]{:S(2)}, u32[]{:S(2)}) collective-permute-start(bf16[1024,512]{1,0:T(8,128)(2,1)S(1)} %pad_maximum_fusion.35), channel_id=1, source_target_pairs={{0,8},{8,0},{16,24},{24,16},{1,9},{9,1},{17,25},{25,17},{2,10},{10... | collective-permute-start | bytes 3145736 | tf_op jit(solution)/shard_map/ppermute | solution.py:25
  500.9 27.8 %collective-permute-start.42 = (bf16[528,256]{1,0:T(8,128)(2,1)S(1)}, bf16[528,256]{1,0:T(8,128)(2,1)S(1)}, u32[]{:S(2)}, u32[]{:S(2)}) collective-permute-start(bf16[528,256]{1,0:T(8,128)(2,1)S(1)} %constant_dynamic-slice_fusion), channel_id=1, source_target_pairs={{0,24},{8,16},{16,8},{24,0},{1,25},{9,17},{17,9},{25,1},{2,26},{10... | collective-permute-start | bytes 811016 | tf_op jit(solution)/shard_map/ppermute | solution.py:25
  529.3 9.4 %collective-permute-start.43 = (bf16[528,256]{1,0:T(8,128)(2,1)S(1)}, bf16[528,256]{1,0:T(8,128)(2,1)S(1)}, u32[]{:S(2)}, u32[]{:S(2)}) collective-permute-start(bf16[528,256]{1,0:T(8,128)(2,1)S(1)} %add_convert_fusion.7), channel_id=1, source_target_pairs={{0,24},{8,16},{16,8},{24,0},{1,25},{9,17},{17,9},{25,1},{2,26},{10... | collective-permute-start | bytes 811016 | tf_op jit(solution)/shard_map/ppermute | solution.py:25
  538.7 10.5 %collective-permute-start.44 = (bf16[528,512]{1,0:T(8,128)(2,1)S(1)}, bf16[528,512]{1,0:T(8,128)(2,1)S(1)}, u32[]{:S(2)}, u32[]{:S(2)}) collective-permute-start(bf16[528,512]{1,0:T(8,128)(2,1)S(1)} %pad_maximum_fusion.38), channel_id=1, source_target_pairs={{0,8},{8,0},{16,24},{24,16},{1,9},{9,1},{17,25},{25,17},{2,10},{10... | collective-permute-start | bytes 1622024 | tf_op jit(solution)/shard_map/ppermute | solution.py:25
  (46 other events, 206.9 us)

commit v3 on v2

--- a/solution.py
+++ b/solution.py
@@ -1,6 +1,8 @@
 import jax
 import jax.numpy as jnp
 from jax import lax
+from jax.experimental import pallas as pl
+from jax.experimental.pallas import tpu as pltpu
 from jax.sharding import PartitionSpec as P
 
 HEADS = 16
@@ -178,6 +180,81 @@
     return lax.dot_general(
         first, second, (((1,), (1,)), ((), ())), preferred_element_type=jnp.float32
     )
+
+
+LANES = 128
+
+
+def head_mask(head):
+    lane = lax.broadcasted_iota(jnp.int32, (1, LANES), 1)
+    return jnp.where(lane // HEAD_DIM == head, 1.0, 0.0).astype(jnp.float32)
+
+
+def attend_kernel(q_ref, k_ref, v_ref, o_ref):
+    queries = q_ref[0].astype(jnp.float32) * HEAD_DIM ** (-0.5)
+    keys, values = k_ref[0], v_ref[0]
+    total = jnp.zeros(queries.shape, jnp.float32)
+    for head in range(LANES // HEAD_DIM):
+        mask = head_mask(head)
+        scores = dot_back((queries * mask).astype(jnp.bfloat16), keys)
+        exped = jnp.exp(scores - jnp.max(scores, axis=1, keepdims=True))
+        share = 1.0 / jnp.sum(exped, axis=1, keepdims=True)
+        total = total + dot(exped.astype(jnp.bfloat16), values) * share * mask
+    o_ref[0] = total
+
+
+def attend_back_kernel(q_ref, k_ref, v_ref, o_ref, g_ref, dq_ref, dk_ref, dv_ref):
+    scale = HEAD_DIM ** (-0.5)
+    queries = q_ref[0].astype(jnp.float32) * scale
+    grads = g_ref[0].astype(jnp.float32)
+    keys, values = k_ref[0], v_ref[0]
+    product = grads * o_ref[0]
+    grad_q = jnp.zeros(queries.shape, jnp.float32)
+    grad_k = jnp.zeros(keys.shape, jnp.float32)
+    grad_v = jnp.zeros(keys.shape, jnp.float32)
+    for head in range(LANES // HEAD_DIM):
+        mask = head_mask(head)
+        query = (queries * mask).astype(jnp.bfloat16)
+        grad = (grads * mask).astype(jnp.bfloat16)
+        scores = dot_back(keys, query)
+        exped = jnp.exp(scores - jnp.max(scores, axis=0, keepdims=True))
+        prob = exped * (1.0 / jnp.sum(exped, axis=0, keepdims=True))
+        delta = lax.dot_general(
+            jnp.broadcast_to(mask, (8, LANES)),
+            product,
+            (((1,), (1,)), ((), ())),
+            precision=lax.Precision.HIGHEST,
+            preferred_element_type=jnp.float32,
+        )[:1]
+        grad_score = (prob * (dot_back(values, grad) - delta)).astype(jnp.bfloat16)
+        grad_v = grad_v + dot(prob.astype(jnp.bfloat16), grad)
+        grad_k = grad_k + dot(grad_score, query)
+        grad_q = grad_q + dot_rows(grad_score, keys) * (mask * scale)
+    dq_ref[0] = grad_q.astype(jnp.bfloat16)
+    dk_ref[0] = grad_k.astype(jnp.bfloat16)
+    dv_ref[0] = grad_v.astype(jnp.bfloat16)
+
+
+def attention_call(kernel, inputs, outputs, products):
+    seqs, rows, width = inputs[0].shape
+    keys = inputs[1].shape[1]
+
+    def spec(array):
+        return pl.BlockSpec((1, array.shape[1], LANES), lambda seq, part: (seq, 0, part))
+
+    return pl.pallas_call(
+        kernel,
+        grid=(seqs, width // LANES),
+        in_specs=[spec(item) for item in inputs],
+        out_specs=[spec(item) for item in outputs],
+        out_shape=outputs,
+        compiler_params=pltpu.CompilerParams(vmem_limit_bytes=40 * 1024 * 1024),
+        cost_estimate=pl.CostEstimate(
+            flops=2 * products * seqs * rows * keys * width,
+            bytes_accessed=sum(item.size * item.dtype.itemsize for item in inputs),
+            transcendentals=seqs * rows * keys * width // HEAD_DIM,
+        ),
+    )(*inputs)
 
 
 def per_device(
@@ -246,37 +323,29 @@
     key_rows = ctx_count * block_rows
 
     def by_sequence(value):
-        parts = value.reshape(ctx_count, seq_local, block_rows, HEADS, HEAD_DIM)
-        return parts.transpose(1, 3, 0, 2, 4).reshape(seq_local, HEADS, key_rows, HEAD_DIM)
+        parts = value.reshape(ctx_count, seq_local, block_rows, width)
+        return parts.transpose(1, 0, 2, 3).reshape(seq_local, key_rows, width)
 
     def by_block(value):
-        parts = value.reshape(seq_local, HEADS, ctx_count, block_rows, HEAD_DIM)
-        return parts.transpose(2, 0, 3, 1, 4).reshape(ctx_count * row_count, width)
-
-    def heads(value):
-        return value.reshape(seq_local, block_rows, HEADS, HEAD_DIM).transpose(0, 2, 1, 3)
-
-    def joined(value):
-        return value.transpose(0, 2, 1, 3).reshape(row_count, width)
-
-    queries = heads((dot(own_rows, input_proj[:, :width]) + query_bias).astype(jnp.bfloat16))
-    kv_all = dot(all_rows, input_proj[:, width:])
-    key_part = by_sequence(kv_all[:, :width].astype(jnp.bfloat16))
-    value_part = by_sequence((kv_all[:, width:] + value_bias).astype(jnp.bfloat16))
-    scores = (
-        jnp.einsum("shqd,shkd->shqk", queries, key_part, preferred_element_type=jnp.float32)
-        * score_scale
-    )
-    attn_prob = jax.nn.softmax(scores, axis=-1).astype(jnp.bfloat16)
-    up_half, down_half, attn_prob = tie(up_half, down_half, attn_prob)
+        parts = value.reshape(seq_local, ctx_count, block_rows, width)
+        return parts.transpose(1, 0, 2, 3).reshape(ctx_count * row_count, width)
+
+    queries = (dot(own_rows, input_proj[:, :width]) + query_bias).astype(jnp.bfloat16)
+    queries = queries.reshape(seq_local, block_rows, width)
+    key_part = by_sequence(dot(all_rows, input_proj[:, width : 2 * width]).astype(jnp.bfloat16))
+    value_part = dot(all_rows, input_proj[:, 2 * width :]) + value_bias
+    value_part = by_sequence(value_part.astype(jnp.bfloat16))
+    mixed_out = attention_call(
+        attend_kernel,
+        (queries, key_part, value_part),
+        (jax.ShapeDtypeStruct(queries.shape, jnp.float32),),
+        2,
+    )[0]
+    up_half, down_half, mixed_out = tie(up_half, down_half, mixed_out)
     out_up = whole(gather_hops(up_half, outer, bits))
     down_weight = whole(gather_hops(down_half, outer, bits))
     out_weight, up_weight = out_up[:, :width], out_up[:, width:]
-    mixed_out = jnp.einsum(
-        "shqk,shkd->shqd", attn_prob, value_part, preferred_element_type=jnp.float32
-    )
-    mixed_rows = joined(mixed_out)
-    attn_in = reorder(mixed_rows.astype(jnp.bfloat16), count)
+    attn_in = reorder(mixed_out.reshape(row_count, width).astype(jnp.bfloat16), count)
     attn_out = dot(attn_in, out_weight) + out_bias
     resid_one = tok_rows.astype(jnp.float32) + attn_out
     normed = layer_norm(resid_one, gain_one, shift_one)
@@ -310,31 +379,26 @@
     up_pair = scatter_hops(up_pair, 0, 1)
     grad_out_bias = jnp.sum(grad_attn.astype(jnp.float32), axis=0)
     grad_mixed = reorder(dot_back(grad_attn, out_weight).astype(jnp.bfloat16), count)
-    grad_heads = heads(grad_mixed)
-    row_delta = jnp.sum(grad_heads.astype(jnp.float32) * mixed_out, axis=-1, keepdims=True)
-    grad_prob = jnp.einsum(
-        "shqd,shkd->shqk", grad_heads, value_part, preferred_element_type=jnp.float32
-    )
-    grad_score = (attn_prob.astype(jnp.float32) * (grad_prob - row_delta)).astype(jnp.bfloat16)
-    down_pair, grad_score = tie(down_pair, grad_score)
+    down_pair, grad_mixed = tie(down_pair, grad_mixed)
     down_pair = scatter_hops(down_pair, 1, outer)
-    grad_value = jnp.einsum(
-        "shqk,shqd->shkd", attn_prob, grad_heads, preferred_element_type=jnp.float32
-    )
-    grad_key = (
-        jnp.einsum("shqk,shqd->shkd", grad_score, queries, preferred_element_type=jnp.float32)
-        * score_scale
-    )
-    grad_query = (
-        jnp.einsum("shqk,shkd->shqd", grad_score, key_part, preferred_element_type=jnp.float32)
-        * score_scale
-    )
-    grad_queries = joined(grad_query).astype(jnp.bfloat16)
-    grad_keys = by_block(grad_key).astype(jnp.bfloat16)
-    grad_values = by_block(grad_value).astype(jnp.bfloat16)
+    grad_queries, grad_keys, grad_values = attention_call(
+        attend_back_kernel,
+        (queries, key_part, value_part, mixed_out, grad_mixed.reshape(queries.shape)),
+        (
+            jax.ShapeDtypeStruct(queries.shape, jnp.bfloat16),
+            jax.ShapeDtypeStruct(key_part.shape, jnp.bfloat16),
+            jax.ShapeDtypeStruct(key_part.shape, jnp.bfloat16),
+        ),
+        5,
+    )
+    up_pair, down_pair, grad_queries, grad_keys, grad_values = tie(
+        up_pair, down_pair, grad_queries, grad_keys, grad_values
+    )
+    up_pair = scatter_hops(up_pair, 1, outer)
+    down_own = ctx_hops(jnp.concatenate(down_pair, axis=2)[0], 0, 1)
+    grad_queries = grad_queries.reshape(row_count, width)
+    grad_keys, grad_values = by_block(grad_keys), by_block(grad_values)
     grad_kv = jnp.concatenate((grad_keys, grad_values), axis=1)
-    up_pair, grad_kv = tie(up_pair, grad_kv)
-    up_pair = scatter_hops(up_pair, 1, outer)
     grad_input_proj = jnp.concatenate(
         (dot_rows(own_rows, grad_queries), dot_rows(all_rows, grad_kv)), axis=1
     )
@@ -369,35 +433,35 @@
     input_pair = scatter_core(input_blocks)
     from_kv = dot_back(grad_kv, input_proj[:, width:])
     from_query = dot_back(grad_queries, input_proj[:, :width])
-    input_pair, from_kv = tie(input_pair, from_kv)
+    from_kv = from_kv.astype(jnp.bfloat16).reshape(ctx_count, row_count, width)
+    steps = 2 * bits_of("ctx")
+    input_pair, from_kv, down_own, up_pair = tie(input_pair, from_kv, down_own, up_pair)
     input_pair = scatter_hops(input_pair, 0, 1)
-    from_kv = scatter_tokens(from_kv.astype(jnp.bfloat16).reshape(ctx_count, row_count, width))
+    from_kv = scatter_tokens(from_kv)
     d_tokens = grad_resid_one + reorder(from_query + from_kv.astype(jnp.float32), count)
-    down_own = jnp.concatenate(down_pair, axis=2)[0]
-    up_own = jnp.concatenate(up_pair, axis=2)[0]
-    first_group = jnp.concatenate((down_own, fold(up_own, width)), axis=0)
-    ctx_steps = 2 * bits_of("ctx")
-    first_group = ctx_hops(first_group, 0, 1)
-    input_pair, first_group = tie(input_pair, first_group)
+    down_own = ctx_hops(down_own, 1, 2)
+    up_own = ctx_hops(fold(jnp.concatenate(up_pair, axis=2)[0], width), 0, 1)
+    input_pair, down_own, up_own = tie(input_pair, down_own, up_own)
     input_pair = scatter_hops(input_pair, 1, outer)
-    first_group = ctx_hops(first_group, 1, 2)
-    input_pair, first_group = tie(input_pair, first_group)
+    down_own = ctx_hops(down_own, 2, 3)
+    up_own = ctx_hops(up_own, 1, 2)
+    input_pair, down_own, up_own = tie(input_pair, down_own, up_own)
     input_own = jnp.concatenate(input_pair, axis=2)[0]
     extra = input_own[:small_lines, 4 * width :].reshape(-1)
     extra = jnp.pad(extra, (0, -extra.shape[0] % (16 * width))).reshape(-1, width)
-    second_group = jnp.concatenate((fold(input_own[:, : 4 * width], width), extra), axis=0)
-    for step in range(2, ctx_steps):
-        second_group = ctx_hops(second_group, step - 2, step - 1)
-        first_group = ctx_hops(first_group, step, step + 1)
-        first_group, second_group = tie(first_group, second_group)
-    second_group = ctx_hops(second_group, ctx_steps - 2, ctx_steps)
-    first_group = first_group.astype(jnp.float32)
-    second_group = second_group.astype(jnp.float32)
-    down_rows = down_own.shape[0]
-    sum_down = first_group[:down_rows]
-    sum_up = unfold(first_group[down_rows:], own_width)
-    sum_input = unfold(second_group[: 3 * own_width], own_width)
-    sum_out = second_group[3 * own_width : 4 * own_width]
+    input_own = jnp.concatenate((fold(input_own[:, : 4 * width], width), extra), axis=0)
+    for step in range(2, steps):
+        input_own = ctx_hops(input_own, step - 2, step - 1)
+        up_own = ctx_hops(up_own, step, step + 1)
+        if step + 1 < steps:
+            down_own = ctx_hops(down_own, step + 1, step + 2)
+        input_own, up_own, down_own = tie(input_own, up_own, down_own)
+    input_own = ctx_hops(input_own, steps - 2, steps).astype(jnp.float32)
+    sum_down = down_own.astype(jnp.float32)
+    sum_up = unfold(up_own.astype(jnp.float32), own_width)
+    sum_input = unfold(input_own[: 3 * own_width], own_width)
+    sum_out = input_own[3 * own_width : 4 * own_width]
+    second_group = input_own
     small_own = second_group[4 * own_width :].reshape(-1)
     owned, start = [], 0
     for item in small:

time: 564 us -> 541 us (0.959)
  waiting for transfers between devices: 141 us -> 207 us
  local copies, waits for them, and re-layouts: 107 us -> 54.7 us
  matrix products: 109 us -> 58.3 us
  Pallas kernels: 0 us -> 31.6 us
  other arithmetic: 96.9 us -> 71.7 us
  starting transfers between devices: 81.8 us -> 96.2 us
  blocking collectives: 15.9 us -> 9.02 us
    ppermute x45 -> x49, waiting for transfers between devices: 141 us -> 207 us  [swap(): return lax.ppermute(value, axis, [(at, at ^ mask) for at in range(size)])]
    pallas_call x0 -> x2, Pallas kernels: none -> 31.6 us  [attention_call(): pl.pallas_call(kernel, grid=(seqs, width // LANES), in_specs=[spec(item)...]
    dot_general x5 -> x0, matrix products: 28.1 us -> none  [the longest x1 8.41 us: per_device(): jnp.einsum('shqk,shkd->shqd', grad_score, key_part, preferred_element_typ...]
    ppermute x45 -> x49, starting transfers between devices: 81.8 us -> 96.2 us  [swap(): return lax.ppermute(value, axis, [(at, at ^ mask) for at in range(size)])]
    reshape x12, other arithmetic: 15.3 us -> 3.91 us  [scatter_hops(): blocks = add(parts[:, 0], came).reshape((-1,) + rest)]
    convert_element_type x4 -> x0, local copies, waits for them, and re-layouts: 10.7 us -> none  [the longest x1 2.94 us: per_device(): grad_keys = by_block(grad_key).astype(jnp.bfloat16)]
    unnamed x216 -> x188, local copies, waits for them, and re-layouts: 40.6 us -> 30.3 us
    concatenate x12, other arithmetic: 30.2 us -> 20.5 us  [gather_hop(): held = jnp.concatenate((held.reshape(split), other.reshape(split)), axis=1)]
  transfers between devices with their start and end apart: 45 -> 49, of which waited for: 15 -> 23; matrix products, arithmetic and copies ran while one was open for 38% -> 16% of each run, Pallas kernels for 0% -> 6%
where the time goes in v3:
time: 541 us; the launch traced here: 531 us
  waiting for transfers between devices  207 us (38%)
  starting transfers between devices  96.2 us (18%)
  other arithmetic  71.7 us (13%)
  matrix products  58.3 us (11%)
  local copies, waits for them, and re-layouts  54.7 us (10%)
  Pallas kernels  31.6 us (6%)
  blocking collectives  9.02 us (2%)
    ppermute x49, waiting for transfers between devices, swap(): return lax.ppermute(value, axis, [(at, at ^ mask) for at in range(size)])  207 us
    ppermute x49, starting transfers between devices, swap(): return lax.ppermute(value, axis, [(at, at ^ mask) for at in range(size)])  96.2 us
    pallas_call x2, Pallas kernels, attention_call(): pl.pallas_call(kernel, grid=(seqs, width // LANES), in_specs=[spec(item)...  31.6 us
    unnamed x188, local copies, waits for them, and re-layouts  30.3 us
    dot_general x6, matrix products, dot(): return jnp.dot(first, second, preferred_element_type=jnp.float32)  23.6 us
    dot_general x5, matrix products, dot_back(): lax.dot_general(first, second, (((1,), (1,)), ((), ())), preferred_elemen...  20.7 us
    concatenate x12, other arithmetic, gather_hop(): held = jnp.concatenate((held.reshape(split), other.reshape(split)), axis=1)  20.5 us
    dot_general x5, matrix products, dot_rows(): lax.dot_general(first, second, (((0,), (0,)), ((), ())), preferred_elemen...  14 us
  transfers between devices with their start and end apart: 49, of which 23 were waited for; matrix products, arithmetic and copies ran while one was open for 16% of the time, Pallas kernels for 6%

profile of v3, /device:TPU:0, one launch (start us, length us, event | category | flops | bytes accessed | tf_op | source)
XLA Modules:
  0.0 531.4 jit_solution(8090356589327844905)
XLA Ops:
  2.0 3.0 collective-permute-start
  6.5 3.6 collective-permute-start.12
  15.1 2.0 fusion.111
  19.4 2.0 fusion.109
  22.8 2.3 fusion.93
  25.1 9.9 %collective-permute-start.13 = (bf16[2,256,1024]{2,1,0:T(8,128)(2,1)}, bf16[2,256,1024]{2,1,0:T(8,128)(2,1)}, u32[]{:S(2)}, u32[]{:S(2)}) collective-permute-start(bf16[2,256,1024]{2,1,0:T(8,128)(2,1)} %get-tuple-element.168), channel_id=1, source_target_pairs={{0,8},{8,0},{16,24},{24,16},{1,9},{9,1},{17,25},{25,17},{2,10},{10... | collective-permute-start | bytes 3145736 | tf_op jit(solution)/shard_map/ppermute | solution.py:27
  35.1 9.0 %all-gather.1 = bf16[8,1,1536]{2,1,0:T(2,128)(2,1)S(1)} all-gather(bf16[1,1,1536]{2,1,0:T(2,128)(2,1)S(1)} %reshape.807), channel_id=2, replica_groups=mesh['ctx'=4,'fsdp'=8] {'fsdp'}, dimensions={0}, use_global_device_ids=true | all-gather | bytes 27648 | tf_op jit(solution)/shard_map/all_gather | solution.py:292
  52.2 5.6 %collective-permute-done.13 = bf16[2,256,1024]{2,1,0:T(8,128)(2,1)} collective-permute-done((bf16[2,256,1024]{2,1,0:T(8,128)(2,1)}, bf16[2,256,1024]{2,1,0:T(8,128)(2,1)}, u32[]{:S(2)}, u32[]{:S(2)}) %collective-permute-start.13) | collective-permute-done | bytes 1048608 | tf_op jit(solution)/shard_map/ppermute | solution.py:27
  60.3 16.1 %collective-permute-done.8 = bf16[1,512,512]{2,1,0:T(8,128)(2,1)S(1)} collective-permute-done((bf16[1,512,512]{2,1,0:T(8,128)(2,1)S(1)}, bf16[1,512,512]{2,1,0:T(8,128)(2,1)S(1)}, u32[]{:S(2)}, u32[]{:S(2)}) %collective-permute-start.8) | collective-permute-done | bytes 524320 | tf_op jit(solution)/shard_map/ppermute | solution.py:27
  82.0 2.3 fusion.17.v_ref
  86.5 2.3 convert_bitcast_fusion.k_ref
  88.9 10.3 %shard_map.262.o_ref = f32[1,256,1024]{2,1,0:T(8,128)S(1)} custom-call(bf16[1,256,1024]{2,1,0:T(8,128)(2,1)S(1)} %fusion.67.q_ref, bf16[1,1024,1024]{2,1,0:T(8,128)(2,1)S(1)} %convert_bitcast_fusion.k_ref, bf16[1,1024,1024]{2,1,0:T(8,128)(2,1)S(1)} %fusion.17.v_ref), custom_call_target="tpu_custom_call" | custom-call | flops 1073741824 | bytes 4718592 | tf_op jit(solution)/shard_map/pallas_call | solution.py:245
  99.2 3.5 collective-permute-done.9
  105.9 24.4 %collective-permute-done.5 = bf16[2,128,2560]{2,1,0:T(8,128)(2,1)S(1)} collective-permute-done((bf16[2,128,2560]{2,1,0:T(8,128)(2,1)S(1)}, bf16[2,128,2560]{2,1,0:T(8,128)(2,1)S(1)}, u32[]{:S(2)}, u32[]{:S(2)}) %collective-permute-start.5) | collective-permute-done | bytes 1310752 | tf_op jit(solution)/shard_map/ppermute | solution.py:27
  135.2 9.7 %collective-permute-done.19 = bf16[4,512,512]{2,1,0:T(8,128)(2,1)} collective-permute-done((bf16[4,512,512]{2,1,0:T(8,128)(2,1)}, bf16[4,512,512]{2,1,0:T(8,128)(2,1)}, u32[]{:S(2)}, u32[]{:S(2)}) %collective-permute-start.19) | collective-permute-done | bytes 2097184 | tf_op jit(solution)/shard_map/ppermute | solution.py:27
  144.9 2.6 pad_maximum_fusion.11
  148.7 4.7 pad_maximum_fusion.10
  153.4 2.4 copy.97
  155.8 3.1 pad_maximum_fusion.4
  160.6 2.0 copy-done.9
  163.5 15.0 %multiply_convert_fusion = (bf16[256,4096]{1,0:T(8,128)(2,1)S(1)}, f32[256,4096]{1,0:T(8,128)}, f32[256,4096]{1,0:T(8,128)}) fusion(f32[4096]{0:T(1024)S(1)} %bitcast.547, bf16[256,1024]{1,0:T(8,128)(2,1)S(1)} %constant_dynamic-update-slice_fusion.8, bf16[1024,2560]{1,0:T(8,128)(2,1)S(1)} %bitcast.493, bf16[1024,2560]{1,0:T(8,128)(2,1)S(1)} %bitcast.490), kind=kOutput, calls=%fused_computation.36 | convolution fusion | flops 2233466880 | bytes 21512192 | tf_op jit(solution)/shard_map/dot_general | solution.py:170
  178.8 1.9 copy-done.20
  180.7 2.5 fusion.149
  186.3 2.4 convolution_convert_fusion.1
  189.8 4.1 fusion.5
  203.3 1.9 add_convert_fusion
  205.2 2.4 convolution_convert_fusion
  207.7 2.4 slice_bitcast_fusion.2
  210.1 2.1 copy-done.6
  212.4 2.4 slice_bitcast_fusion.4
  218.2 2.0 copy.103
  220.2 1.9 convert_reduce_fusion
  222.3 5.2 fusion.3
  228.1 4.3 fusion.4
  234.0 5.1 fusion.7
  245.2 2.3 fusion.59
  248.0 2.1 convolution_convert_fusion.3
  250.1 38.4 %collective-permute-done.24 = bf16[2,1,512,512]{3,2,0,1:T(8,128)(2,1)S(1)} collective-permute-done((bf16[2,1,512,512]{3,2,0,1:T(8,128)(2,1)S(1)}, bf16[2,1,512,512]{3,2,0,1:T(8,128)(2,1)S(1)}, u32[]{:S(2)}, u32[]{:S(2)}) %collective-permute-start.24) | collective-permute-done | bytes 1048608 | tf_op jit(solution)/shard_map/ppermute | solution.py:27
  293.3 21.2 %shard_map.263 = (bf16[1,256,1024]{2,1,0:T(8,128)(2,1)S(1)}, bf16[1,1024,1024]{2,1,0:T(8,128)(2,1)S(1)}, bf16[1,1024,1024]{2,1,0:T(8,128)(2,1)S(1)}) custom-call(bf16[1,256,1024]{2,1,0:T(8,128)(2,1)S(1)} %fusion.67.q_ref, bf16[1,1024,1024]{2,1,0:T(8,128)(2,1)S(1)} %copy-done.3, bf16[1,1024,1024]{2,1,0:T(8,128)(2,1)S(1)} %copy-done.1, ...), custom_call_target="tpu_custom_call" | custom-call | flops 2684354560 | bytes 6291456 | tf_op jit(solution)/shard_map/pallas_call | solution.py:245
  316.2 6.4 %convolution_convert_fusion.2 = bf16[1024,2048]{1,0:T(8,128)(2,1)} fusion(bf16[1024,1024]{1,0:T(8,128)(2,1)S(1)} %copy-done.38, bf16[1024,1024]{1,0:T(8,128)(2,1)S(1)} %bitcast.447, bf16[1024,1024]{1,0:T(8,128)(2,1)S(1)} %bitcast.449), kind=kOutput, calls=%fused_computation.51 | convolution fusion | flops 4305453056 | bytes 10485760 | tf_op jit(solution)/shard_map/dot_general | solution.py:174
  322.6 2.4 pad_maximum_fusion.12
  326.1 4.0 fusion.1
  330.1 2.5 slice_bitcast_fusion
  332.6 2.2 copy-done.5
  337.0 8.4 %fusion.32 = bf16[1024,1024]{1,0:T(8,128)(2,1)S(1)} fusion(bf16[1024,2048]{1,0:T(8,128)(2,1)} %pad_maximum_fusion.12, bf16[1024,1536]{1,0:T(8,128)(2,1)} %bitcast.518, bf16[1024,1536]{1,0:T(8,128)(2,1)S(1)} %bitcast.514), kind=kOutput, calls=%fused_computation.82 | convolution fusion | flops 4304404480 | bytes 12582912 | tf_op jit(solution)/shard_map/dot_general | solution.py:180
  349.6 10.3 %collective-permute-done.31 = bf16[1,1,128,2048]{3,2,1,0:T(8,128)(2,1)S(1)} collective-permute-done((bf16[1,1,128,2048]{3,2,1,0:T(8,128)(2,1)S(1)}, bf16[1,1,128,2048]{3,2,1,0:T(8,128)(2,1)S(1)}, u32[]{:S(2)}, u32[]{:S(2)}) %collective-permute-start.31) | collective-permute-done | bytes 524320 | tf_op jit(solution)/shard_map/ppermute | solution.py:27
  361.3 3.3 fusion.2
  367.6 2.7 collective-permute-start.36
  373.0 26.2 %collective-permute-done.36 = bf16[512,256]{1,0:T(8,128)(2,1)S(1)} collective-permute-done((bf16[512,256]{1,0:T(8,128)(2,1)S(1)}, bf16[512,256]{1,0:T(8,128)(2,1)S(1)}, u32[]{:S(2)}, u32[]{:S(2)}) %collective-permute-start.36) | collective-permute-done | bytes 262176 | tf_op jit(solution)/shard_map/ppermute | solution.py:27
  399.2 7.4 %collective-permute-done.37 = bf16[512,512]{1,0:T(8,128)(2,1)S(1)} collective-permute-done((bf16[512,512]{1,0:T(8,128)(2,1)S(1)}, bf16[512,512]{1,0:T(8,128)(2,1)S(1)}, u32[]{:S(2)}, u32[]{:S(2)}) %collective-permute-start.37) | collective-permute-done | bytes 524320 | tf_op jit(solution)/shard_map/ppermute | solution.py:27
  407.2 3.8 collective-permute-start.33
  414.2 3.7 collective-permute-start.41
  417.9 11.7 %collective-permute-done.40 = bf16[512,256]{1,0:T(8,128)(2,1)S(1)} collective-permute-done((bf16[512,256]{1,0:T(8,128)(2,1)S(1)}, bf16[512,256]{1,0:T(8,128)(2,1)S(1)}, u32[]{:S(2)}, u32[]{:S(2)}) %collective-permute-start.40) | collective-permute-done | bytes 262176 | tf_op jit(solution)/shard_map/ppermute | solution.py:27
  429.7 3.2 collective-permute-done.41
  434.9 3.6 collective-permute-start.43
  438.6 25.8 %collective-permute-start.44 = (bf16[512,512]{1,0:T(8,128)(2,1)S(1)}, bf16[512,512]{1,0:T(8,128)(2,1)S(1)}, u32[]{:S(2)}, u32[]{:S(2)}) collective-permute-start(bf16[512,512]{1,0:T(8,128)(2,1)S(1)} %pad_maximum_fusion.41), channel_id=1, source_target_pairs={{0,8},{8,0},{16,24},{24,16},{1,9},{9,1},{17,25},{25,17},{2,10},{10... | collective-permute-start | bytes 1572872 | tf_op jit(solution)/shard_map/ppermute | solution.py:27
  464.6 12.6 %collective-permute-done.44 = bf16[512,512]{1,0:T(8,128)(2,1)S(1)} collective-permute-done((bf16[512,512]{1,0:T(8,128)(2,1)S(1)}, bf16[512,512]{1,0:T(8,128)(2,1)S(1)}, u32[]{:S(2)}, u32[]{:S(2)}) %collective-permute-start.44) | collective-permute-done | bytes 524320 | tf_op jit(solution)/shard_map/ppermute | solution.py:27
  477.5 8.3 %collective-permute-done.42 = bf16[528,512]{1,0:T(8,128)(2,1)S(1)} collective-permute-done((bf16[528,512]{1,0:T(8,128)(2,1)S(1)}, bf16[528,512]{1,0:T(8,128)(2,1)S(1)}, u32[]{:S(2)}, u32[]{:S(2)}) %collective-permute-start.42) | collective-permute-done | bytes 540704 | tf_op jit(solution)/shard_map/ppermute | solution.py:27
  486.1 2.2 collective-permute-start.45
  491.9 5.4 %collective-permute-done.45 = bf16[528,256]{1,0:T(8,128)(2,1)S(1)} collective-permute-done((bf16[528,256]{1,0:T(8,128)(2,1)S(1)}, bf16[528,256]{1,0:T(8,128)(2,1)S(1)}, u32[]{:S(2)}, u32[]{:S(2)}) %collective-permute-start.45) | collective-permute-done | bytes 270368 | tf_op jit(solution)/shard_map/ppermute | solution.py:27
  497.4 7.4 %collective-permute-done.46 = bf16[512,512]{1,0:T(8,128)(2,1)S(1)} collective-permute-done((bf16[512,512]{1,0:T(8,128)(2,1)S(1)}, bf16[512,512]{1,0:T(8,128)(2,1)S(1)}, u32[]{:S(2)}, u32[]{:S(2)}) %collective-permute-start.46) | collective-permute-done | bytes 524320 | tf_op jit(solution)/shard_map/ppermute | solution.py:27
  507.9 6.6 %collective-permute-done.47 = bf16[528,256]{1,0:T(8,128)(2,1)S(1)} collective-permute-done((bf16[528,256]{1,0:T(8,128)(2,1)S(1)}, bf16[528,256]{1,0:T(8,128)(2,1)S(1)}, u32[]{:S(2)}, u32[]{:S(2)}) %collective-permute-start.47) | collective-permute-done | bytes 270368 | tf_op jit(solution)/shard_map/ppermute | solution.py:27
  514.6 3.5 collective-permute-start.48
  521.4 5.6 %collective-permute-done.48 = bf16[528,512]{1,0:T(8,128)(2,1)S(1)} collective-permute-done((bf16[528,512]{1,0:T(8,128)(2,1)S(1)}, bf16[528,512]{1,0:T(8,128)(2,1)S(1)}, u32[]{:S(2)}, u32[]{:S(2)}) %collective-permute-start.48) | collective-permute-done | bytes 540704 | tf_op jit(solution)/shard_map/ppermute | solution.py:27
  (395 shorter events, 108.4 us)
Async XLA Ops:
  1.9 11.1 %copy-start.43 = (bf16[128]{0:T(256)(128)(2,1)S(1)}, bf16[128]{0:T(256)(128)(2,1)}, u32[]{:S(2)}) copy-start(bf16[128]{0:T(256)(128)(2,1)} %param.21) | copy-start | bytes 772
  1.9 11.3 %copy-start.44 = (bf16[128]{0:T(256)(128)(2,1)S(1)}, bf16[128]{0:T(256)(128)(2,1)}, u32[]{:S(2)}) copy-start(bf16[128]{0:T(256)(128)(2,1)} %param.22) | copy-start | bytes 772
  2.0 11.5 %copy-start.39 = (bf16[512]{0:T(512)(128)(2,1)S(1)}, bf16[512]{0:T(512)(128)(2,1)}, u32[]{:S(2)}) copy-start(bf16[512]{0:T(512)(128)(2,1)} %param.24) | copy-start | bytes 3076
  2.0 11.7 %copy-start.45 = (bf16[128]{0:T(256)(128)(2,1)S(1)}, bf16[128]{0:T(256)(128)(2,1)}, u32[]{:S(2)}) copy-start(bf16[128]{0:T(256)(128)(2,1)} %param.26) | copy-start | bytes 772
  2.0 11.9 %copy-start.46 = (bf16[128]{0:T(256)(128)(2,1)S(1)}, bf16[128]{0:T(256)(128)(2,1)}, u32[]{:S(2)}) copy-start(bf16[128]{0:T(256)(128)(2,1)} %param.27) | copy-start | bytes 772
  2.0 12.1 %copy-start.47 = (bf16[128]{0:T(256)(128)(2,1)S(1)}, bf16[128]{0:T(256)(128)(2,1)}, u32[]{:S(2)}) copy-start(bf16[128]{0:T(256)(128)(2,1)} %param.28) | copy-start | bytes 772
  2.0 12.3 %collective-permute-start = (bf16[1,128,1536]{2,1,0:T(8,128)(2,1)S(1)}, bf16[1,128,1536]{2,1,0:T(8,128)(2,1)S(1)}, u32[]{:S(2)}, u32[]{:S(2)}) collective-permute-start(bf16[1,128,1536]{2,1,0:T(8,128)(2,1)S(1)} %get-tuple-element.180), channel_id=1, source_target_pairs={{0,2},{1,3},{2,0},{3,1},{4,6},{5,7},{6,4},{7,5},{8,10},{9,11},{10,... | collective-permute-start | bytes 1179656 | tf_op jit(solution)/shard_map/ppermute | solution.py:27
  5.0 13.6 %collective-permute-start.2 = (bf16[1,128,1536]{2,1,0:T(8,128)(2,1)S(1)}, bf16[1,128,1536]{2,1,0:T(8,128)(2,1)S(1)}, u32[]{:S(2)}, u32[]{:S(2)}) collective-permute-start(bf16[1,128,1536]{2,1,0:T(8,128)(2,1)S(1)} %get-tuple-element.179), channel_id=1, source_target_pairs={{0,4},{1,5},{2,6},{3,7},{4,0},{5,1},{6,2},{7,3},{8,12},{9,13},{10,... | collective-permute-start | bytes 1179656 | tf_op jit(solution)/shard_map/ppermute | solution.py:27
  6.5 16.3 %collective-permute-start.12 = (bf16[1,256,1024]{2,1,0:T(8,128)(2,1)}, bf16[1,256,1024]{2,1,0:T(8,128)(2,1)}, u32[]{:S(2)}, u32[]{:S(2)}) collective-permute-start(bf16[1,256,1024]{2,1,0:T(8,128)(2,1)} %param.15), channel_id=1, source_target_pairs={{0,24},{8,16},{16,8},{24,0},{1,25},{9,17},{17,9},{25,1},{2,26},{10... | collective-permute-start | bytes 1572872 | tf_op jit(solution)/shard_map/ppermute | solution.py:27
  17.1 28.3 %collective-permute-start.1 = (bf16[2,128,1536]{2,1,0:T(8,128)(2,1)}, bf16[2,128,1536]{2,1,0:T(8,128)(2,1)}, u32[]{:S(2)}, u32[]{:S(2)}) collective-permute-start(bf16[2,128,1536]{2,1,0:T(8,128)(2,1)} %get-tuple-element.182), channel_id=1, source_target_pairs={{0,4},{1,5},{2,6},{3,7},{4,0},{5,1},{6,2},{7,3},{8,12},{9,13},{10,... | collective-permute-start | bytes 2359304 | tf_op jit(solution)/shard_map/ppermute | solution.py:27
  21.3 25.4 %collective-permute-start.3 = (bf16[2,128,1536]{2,1,0:T(8,128)(2,1)}, bf16[2,128,1536]{2,1,0:T(8,128)(2,1)}, u32[]{:S(2)}, u32[]{:S(2)}) collective-permute-start(bf16[2,128,1536]{2,1,0:T(8,128)(2,1)} %get-tuple-element.176), channel_id=1, source_target_pairs={{0,2},{1,3},{2,0},{3,1},{4,6},{5,7},{6,4},{7,5},{8,10},{9,11},{10,... | collective-permute-start | bytes 2359304 | tf_op jit(solution)/shard_map/ppermute | solution.py:27
  25.1 32.7 %collective-permute-start.13 = (bf16[2,256,1024]{2,1,0:T(8,128)(2,1)}, bf16[2,256,1024]{2,1,0:T(8,128)(2,1)}, u32[]{:S(2)}, u32[]{:S(2)}) collective-permute-start(bf16[2,256,1024]{2,1,0:T(8,128)(2,1)} %get-tuple-element.168), channel_id=1, source_target_pairs={{0,8},{8,0},{16,24},{24,16},{1,9},{9,1},{17,25},{25,17},{2,10},{10... | collective-permute-start | bytes 3145736 | tf_op jit(solution)/shard_map/ppermute | solution.py:27
  48.1 30.1 %collective-permute-start.4 = (bf16[1,128,2560]{2,1,0:T(8,128)(2,1)S(1)}, bf16[1,128,2560]{2,1,0:T(8,128)(2,1)S(1)}, u32[]{:S(2)}, u32[]{:S(2)}) collective-permute-start(bf16[1,128,2560]{2,1,0:T(8,128)(2,1)S(1)} %copy-done.27), channel_id=1, source_target_pairs={{0,2},{1,3},{2,0},{3,1},{4,6},{5,7},{6,4},{7,5},{8,10},{9,11},{10,... | collective-permute-start | bytes 1966088 | tf_op jit(solution)/shard_map/ppermute | solution.py:27
  48.8 30.4 %collective-permute-start.6 = (bf16[1,128,2560]{2,1,0:T(8,128)(2,1)S(1)}, bf16[1,128,2560]{2,1,0:T(8,128)(2,1)S(1)}, u32[]{:S(2)}, u32[]{:S(2)}) collective-permute-start(bf16[1,128,2560]{2,1,0:T(8,128)(2,1)S(1)} %get-tuple-element.72), channel_id=1, source_target_pairs={{0,4},{1,5},{2,6},{3,7},{4,0},{5,1},{6,2},{7,3},{8,12},{9,13},{10,... | collective-permute-start | bytes 1966088 | tf_op jit(solution)/shard_map/ppermute | solution.py:27
  50.1 26.3 %collective-permute-start.8 = (bf16[1,512,512]{2,1,0:T(8,128)(2,1)S(1)}, bf16[1,512,512]{2,1,0:T(8,128)(2,1)S(1)}, u32[]{:S(2)}, u32[]{:S(2)}) collective-permute-start(bf16[1,512,512]{2,1,0:T(8,128)(2,1)S(1)} %get-tuple-element.73), channel_id=1, source_target_pairs={{0,2},{1,3},{2,0},{3,1},{4,6},{5,7},{6,4},{7,5},{8,10},{9,11},{10,... | collective-permute-start | bytes 1572872 | tf_op jit(solution)/shard_map/ppermute | solution.py:27
  50.8 25.9 %collective-permute-start.10 = (bf16[1,512,512]{2,1,0:T(8,128)(2,1)S(1)}, bf16[1,512,512]{2,1,0:T(8,128)(2,1)S(1)}, u32[]{:S(2)}, u32[]{:S(2)}) collective-permute-start(bf16[1,512,512]{2,1,0:T(8,128)(2,1)S(1)} %get-tuple-element.74), channel_id=1, source_target_pairs={{0,4},{1,5},{2,6},{3,7},{4,0},{5,1},{6,2},{7,3},{8,12},{9,13},{10,... | collective-permute-start | bytes 1572872 | tf_op jit(solution)/shard_map/ppermute | solution.py:27
  57.8 23.0 %collective-permute-start.15 = (bf16[4,128,1536]{2,1,0:T(8,128)(2,1)S(1)}, bf16[4,128,1536]{2,1,0:T(8,128)(2,1)S(1)}, u32[]{:S(2)}, u32[]{:S(2)}) collective-permute-start(bf16[4,128,1536]{2,1,0:T(8,128)(2,1)S(1)} %bitcast.487), channel_id=1, source_target_pairs={{0,1},{1,0},{2,3},{3,2},{4,5},{5,4},{6,7},{7,6},{8,9},{9,8},{10,11... | collective-permute-start | bytes 4718600 | tf_op jit(solution)/shard_map/ppermute | solution.py:27
  60.3 25.1 %copy-start.37 = (bf16[1024,1024]{1,0:T(8,128)(2,1)}, bf16[1024,1024]{1,0:T(8,128)(2,1)S(1)}, u32[]{:S(2)}) copy-start(bf16[1024,1024]{1,0:T(8,128)(2,1)S(1)} %dynamic-slice_dynamic-update-slice_fusion.16) | copy-start | bytes 6291460
  76.4 8.0 %collective-permute-start.14 = (bf16[4,128,1536]{2,1,0:T(8,128)(2,1)S(1)}, bf16[4,128,1536]{2,1,0:T(8,128)(2,1)S(1)}, u32[]{:S(2)}, u32[]{:S(2)}) collective-permute-start(bf16[4,128,1536]{2,1,0:T(8,128)(2,1)S(1)} %bitcast.485), channel_id=1, source_target_pairs={{0,1},{1,0},{2,3},{3,2},{4,5},{5,4},{6,7},{7,6},{8,9},{9,8},{10,11... | collective-permute-start | bytes 4718600 | tf_op jit(solution)/shard_map/ppermute | solution.py:27
  76.7 26.0 %collective-permute-start.9 = (bf16[2,512,512]{2,1,0:T(8,128)(2,1)S(1)}, bf16[2,512,512]{2,1,0:T(8,128)(2,1)S(1)}, u32[]{:S(2)}, u32[]{:S(2)}) collective-permute-start(bf16[2,512,512]{2,1,0:T(8,128)(2,1)S(1)} %get-tuple-element.172), channel_id=1, source_target_pairs={{0,4},{1,5},{2,6},{3,7},{4,0},{5,1},{6,2},{7,3},{8,12},{9,13},{10,... | collective-permute-start | bytes 3145736 | tf_op jit(solution)/shard_map/ppermute | solution.py:27
  78.2 26.2 %collective-permute-start.11 = (bf16[2,512,512]{2,1,0:T(8,128)(2,1)S(1)}, bf16[2,512,512]{2,1,0:T(8,128)(2,1)S(1)}, u32[]{:S(2)}, u32[]{:S(2)}) collective-permute-start(bf16[2,512,512]{2,1,0:T(8,128)(2,1)S(1)} %get-tuple-element.170), channel_id=1, source_target_pairs={{0,2},{1,3},{2,0},{3,1},{4,6},{5,7},{6,4},{7,5},{8,10},{9,11},{10,... | collective-permute-start | bytes 3145736 | tf_op jit(solution)/shard_map/ppermute | solution.py:27
  79.1 51.1 %collective-permute-start.5 = (bf16[2,128,2560]{2,1,0:T(8,128)(2,1)S(1)}, bf16[2,128,2560]{2,1,0:T(8,128)(2,1)S(1)}, u32[]{:S(2)}, u32[]{:S(2)}) collective-permute-start(bf16[2,128,2560]{2,1,0:T(8,128)(2,1)S(1)} %get-tuple-element.149), channel_id=1, source_target_pairs={{0,4},{1,5},{2,6},{3,7},{4,0},{5,1},{6,2},{7,3},{8,12},{9,13},{10,... | collective-permute-start | bytes 3932168 | tf_op jit(solution)/shard_map/ppermute | solution.py:27
  80.8 51.2 %collective-permute-start.7 = (bf16[2,128,2560]{2,1,0:T(8,128)(2,1)S(1)}, bf16[2,128,2560]{2,1,0:T(8,128)(2,1)S(1)}, u32[]{:S(2)}, u32[]{:S(2)}) collective-permute-start(bf16[2,128,2560]{2,1,0:T(8,128)(2,1)S(1)} %get-tuple-element.147), channel_id=1, source_target_pairs={{0,2},{1,3},{2,0},{3,1},{4,6},{5,7},{6,4},{7,5},{8,10},{9,11},{10,... | collective-permute-start | bytes 3932168 | tf_op jit(solution)/shard_map/ppermute | solution.py:27
  133.7 22.1 %collective-permute-start.16 = (bf16[4,128,2560]{2,1,0:T(8,128)(2,1)}, bf16[4,128,2560]{2,1,0:T(8,128)(2,1)}, u32[]{:S(2)}, u32[]{:S(2)}) collective-permute-start(bf16[4,128,2560]{2,1,0:T(8,128)(2,1)} %bitcast.23), channel_id=1, source_target_pairs={{0,1},{1,0},{2,3},{3,2},{4,5},{5,4},{6,7},{7,6},{8,9},{9,8},{10,11... | collective-permute-start | bytes 7864328 | tf_op jit(solution)/shard_map/ppermute | solution.py:27
  133.7 11.2 %collective-permute-start.19 = (bf16[4,512,512]{2,1,0:T(8,128)(2,1)}, bf16[4,512,512]{2,1,0:T(8,128)(2,1)}, u32[]{:S(2)}, u32[]{:S(2)}) collective-permute-start(bf16[4,512,512]{2,1,0:T(8,128)(2,1)} %bitcast.45), channel_id=1, source_target_pairs={{0,1},{1,0},{2,3},{3,2},{4,5},{5,4},{6,7},{7,6},{8,9},{9,8},{10,11... | collective-permute-start | bytes 6291464 | tf_op jit(solution)/shard_map/ppermute | solution.py:27
  134.2 14.5 %collective-permute-start.18 = (bf16[4,512,512]{2,1,0:T(8,128)(2,1)}, bf16[4,512,512]{2,1,0:T(8,128)(2,1)}, u32[]{:S(2)}, u32[]{:S(2)}) collective-permute-start(bf16[4,512,512]{2,1,0:T(8,128)(2,1)} %bitcast.37), channel_id=1, source_target_pairs={{0,1},{1,0},{2,3},{3,2},{4,5},{5,4},{6,7},{7,6},{8,9},{9,8},{10,11... | collective-permute-start | bytes 6291464 | tf_op jit(solution)/shard_map/ppermute | solution.py:27
  134.3 26.3 %collective-permute-start.17 = (bf16[4,128,2560]{2,1,0:T(8,128)(2,1)}, bf16[4,128,2560]{2,1,0:T(8,128)(2,1)S(1)}, u32[]{:S(2)}, u32[]{:S(2)}) collective-permute-start(bf16[4,128,2560]{2,1,0:T(8,128)(2,1)} %bitcast.462), channel_id=1, source_target_pairs={{0,1},{1,0},{2,3},{3,2},{4,5},{5,4},{6,7},{7,6},{8,9},{9,8},{10,11... | collective-permute-start | bytes 7864328 | tf_op jit(solution)/shard_map/ppermute | solution.py:27
  135.2 23.7 %copy-start.30 = (bf16[256,1024]{1,0:T(8,128)(2,1)}, bf16[256,1024]{1,0:T(8,128)(2,1)S(1)}, u32[]{:S(2)}) copy-start(bf16[256,1024]{1,0:T(8,128)(2,1)S(1)} %constant_dynamic-update-slice_fusion) | copy-start | bytes 1572868
  163.4 15.1 %copy-start.15 = (bf16[4,2,1,128,2560]{4,3,1,0,2:T(8,128)(2,1)}, bf16[4,2,1,128,2560]{4,3,1,0,2:T(8,128)(2,1)S(1)}, u32[]{:S(2)}) copy-start(bf16[4,2,1,128,2560]{4,3,1,0,2:T(8,128)(2,1)S(1)} %copy.95) | copy-start | bytes 15728644
  163.5 15.3 %copy-start.22 = (bf16[4,2,1,512,512]{4,3,1,0,2:T(8,128)(2,1)S(1)}, bf16[4,2,1,512,512]{4,3,1,0,2:T(8,128)(2,1)}, u32[]{:S(2)}) copy-start(bf16[4,2,1,512,512]{4,3,1,0,2:T(8,128)(2,1)} %copy.97) | copy-start | bytes 12582916
  188.8 23.7 %copy-start.4 = (bf16[4096,1024]{1,0:T(8,128)(2,1)}, bf16[4096,1024]{1,0:T(8,128)(2,1)S(1)}, u32[]{:S(2)}) copy-start(bf16[4096,1024]{1,0:T(8,128)(2,1)S(1)} %convolution_convert_fusion.1) | copy-start | bytes 25165828
  212.2 10.1 %collective-permute-start.21 = (bf16[4,128,4096]{2,1,0:T(8,128)(2,1)}, bf16[4,128,4096]{2,1,0:T(8,128)(2,1)}, u32[]{:S(2)}, u32[]{:S(2)}) collective-permute-start(bf16[4,128,4096]{2,1,0:T(8,128)(2,1)} %slice_bitcast_fusion.2), channel_id=1, source_target_pairs={{0,1},{1,0},{2,3},{3,2},{4,5},{5,4},{6,7},{7,6},{8,9},{9,8},{10,11... | collective-permute-start | bytes 12582920 | tf_op jit(solution)/shard_map/ppermute | solution.py:27
  214.8 13.2 %collective-permute-start.20 = (bf16[4,512,1024]{2,1,0:T(8,128)(2,1)}, bf16[4,512,1024]{2,1,0:T(8,128)(2,1)}, u32[]{:S(2)}, u32[]{:S(2)}) collective-permute-start(bf16[4,512,1024]{2,1,0:T(8,128)(2,1)} %slice_bitcast_fusion.4), channel_id=1, source_target_pairs={{0,1},{1,0},{2,3},{3,2},{4,5},{5,4},{6,7},{7,6},{8,9},{9,8},{10,11... | collective-permute-start | bytes 12582920 | tf_op jit(solution)/shard_map/ppermute | solution.py:27
  240.6 50.8 %collective-permute-start.22 = (bf16[2,1,128,2048]{3,2,0,1:T(8,128)(2,1)S(1)}, bf16[2,1,128,2048]{3,2,0,1:T(8,128)(2,1)S(1)}, u32[]{:S(2)}, u32[]{:S(2)}) collective-permute-start(bf16[2,1,128,2048]{3,2,0,1:T(8,128)(2,1)S(1)} %slice_bitcast_fusion.18), channel_id=1, source_target_pairs={{0,2},{1,3},{2,0},{3,1},{4,6},{5,7},{6,4},{7,5},{8,10},{9,11},{10,... | collective-permute-start | bytes 3145736 | tf_op jit(solution)/shard_map/ppermute | solution.py:27
  241.5 50.5 %collective-permute-start.23 = (bf16[1,2,128,2048]{3,2,1,0:T(8,128)(2,1)S(1)}, bf16[1,2,128,2048]{3,2,1,0:T(8,128)(2,1)S(1)}, u32[]{:S(2)}, u32[]{:S(2)}) collective-permute-start(bf16[1,2,128,2048]{3,2,1,0:T(8,128)(2,1)S(1)} %slice_bitcast_fusion.16), channel_id=1, source_target_pairs={{0,4},{1,5},{2,6},{3,7},{4,0},{5,1},{6,2},{7,3},{8,12},{9,13},{10,... | collective-permute-start | bytes 3145736 | tf_op jit(solution)/shard_map/ppermute | solution.py:27
  243.0 45.5 %collective-permute-start.24 = (bf16[2,1,512,512]{3,2,0,1:T(8,128)(2,1)S(1)}, bf16[2,1,512,512]{3,2,0,1:T(8,128)(2,1)S(1)}, u32[]{:S(2)}, u32[]{:S(2)}) collective-permute-start(bf16[2,1,512,512]{3,2,0,1:T(8,128)(2,1)S(1)} %slice_bitcast_fusion.14), channel_id=1, source_target_pairs={{0,2},{1,3},{2,0},{3,1},{4,6},{5,7},{6,4},{7,5},{8,10},{9,11},{10,... | collective-permute-start | bytes 3145736 | tf_op jit(solution)/shard_map/ppermute | solution.py:27
  243.8 45.1 %collective-permute-start.25 = (bf16[1,2,512,512]{3,2,1,0:T(8,128)(2,1)S(1)}, bf16[1,2,512,512]{3,2,1,0:T(8,128)(2,1)S(1)}, u32[]{:S(2)}, u32[]{:S(2)}) collective-permute-start(bf16[1,2,512,512]{3,2,1,0:T(8,128)(2,1)S(1)} %slice_bitcast_fusion.12), channel_id=1, source_target_pairs={{0,4},{1,5},{2,6},{3,7},{4,0},{5,1},{6,2},{7,3},{8,12},{9,13},{10,... | collective-permute-start | bytes 3145736 | tf_op jit(solution)/shard_map/ppermute | solution.py:27
  289.3 25.3 %collective-permute-start.26 = (bf16[1,1,512,512]{3,2,1,0:T(8,128)(2,1)S(1)}, bf16[1,1,512,512]{3,2,1,0:T(8,128)(2,1)S(1)}, u32[]{:S(2)}, u32[]{:S(2)}) collective-permute-start(bf16[1,1,512,512]{3,2,1,0:T(8,128)(2,1)S(1)} %slice_bitcast_fusion.32), channel_id=1, source_target_pairs={{0,4},{1,5},{2,6},{3,7},{4,0},{5,1},{6,2},{7,3},{8,12},{9,13},{10,... | collective-permute-start | bytes 1572872 | tf_op jit(solution)/shard_map/ppermute | solution.py:27
  290.8 24.0 %collective-permute-start.27 = (bf16[1,1,512,512]{3,2,1,0:T(8,128)(2,1)S(1)}, bf16[1,1,512,512]{3,2,1,0:T(8,128)(2,1)S(1)}, u32[]{:S(2)}, u32[]{:S(2)}) collective-permute-start(bf16[1,1,512,512]{3,2,1,0:T(8,128)(2,1)S(1)} %slice_bitcast_fusion.30), channel_id=1, source_target_pairs={{0,2},{1,3},{2,0},{3,1},{4,6},{5,7},{6,4},{7,5},{8,10},{9,11},{10,... | collective-permute-start | bytes 1572872 | tf_op jit(solution)/shard_map/ppermute | solution.py:27
  334.8 26.4 %collective-permute-start.28 = (bf16[4,128,4224]{2,1,0:T(8,128)(2,1)}, bf16[4,128,4224]{2,1,0:T(8,128)(2,1)}, u32[]{:S(2)}, u32[]{:S(2)}) collective-permute-start(bf16[4,128,4224]{2,1,0:T(8,128)(2,1)} %slice_bitcast_fusion), channel_id=1, source_target_pairs={{0,1},{1,0},{2,3},{3,2},{4,5},{5,4},{6,7},{7,6},{8,9},{9,8},{10,11... | collective-permute-start | bytes 12976136 | tf_op jit(solution)/shard_map/ppermute | solution.py:27
  334.9 26.3 %slice-start.2 = ((s8[8650752]{0:T(1024)(128)(4,1)}), s8[4194304]{0:T(1024)(128)(4,1)S(1)}, s32[]{:S(2)}) async-start(s8[8650752]{0:T(1024)(128)(4,1)} %bitcast.457), calls=%async_computation.2 | async-start | bytes 8388608
  335.0 26.3 %slice-start.3 = ((s8[8650752]{0:T(1024)(128)(4,1)}), s8[4194304]{0:T(1024)(128)(4,1)S(1)}, s32[]{:S(2)}) async-start(s8[8650752]{0:T(1024)(128)(4,1)} %bitcast.457), calls=%async_computation.3 | async-start | bytes 8388608
  335.0 26.3 %slice-start.4 = ((s8[8650752]{0:T(1024)(128)(4,1)}), s8[262144]{0:T(1024)(128)(4,1)S(1)}, s32[]{:S(2)}) async-start(s8[8650752]{0:T(1024)(128)(4,1)} %bitcast.457), calls=%async_computation.4 | async-start | bytes 524288
  335.0 14.4 %collective-permute-start.29 = (bf16[512,512]{1,0:T(8,128)(2,1)S(1)}, bf16[512,512]{1,0:T(8,128)(2,1)S(1)}, u32[]{:S(2)}, u32[]{:S(2)}) collective-permute-start(bf16[512,512]{1,0:T(8,128)(2,1)S(1)} %dynamic-slice_bitcast_fusion), channel_id=1, source_target_pairs={{0,8},{8,0},{16,24},{24,16},{1,9},{9,1},{17,25},{25,17},{2,10},{10... | collective-permute-start | bytes 1572872 | tf_op jit(solution)/shard_map/ppermute | solution.py:27
  345.5 14.4 %collective-permute-start.31 = (bf16[1,1,128,2048]{3,2,1,0:T(8,128)(2,1)S(1)}, bf16[1,1,128,2048]{3,2,1,0:T(8,128)(2,1)S(1)}, u32[]{:S(2)}, u32[]{:S(2)}) collective-permute-start(bf16[1,1,128,2048]{3,2,1,0:T(8,128)(2,1)S(1)} %slice_bitcast_fusion.26), channel_id=1, source_target_pairs={{0,2},{1,3},{2,0},{3,1},{4,6},{5,7},{6,4},{7,5},{8,10},{9,11},{10,... | collective-permute-start | bytes 1572872 | tf_op jit(solution)/shard_map/ppermute | solution.py:27
  347.0 14.1 %collective-permute-start.30 = (bf16[1,1,128,2048]{3,2,1,0:T(8,128)(2,1)S(1)}, bf16[1,1,128,2048]{3,2,1,0:T(8,128)(2,1)S(1)}, u32[]{:S(2)}, u32[]{:S(2)}) collective-permute-start(bf16[1,1,128,2048]{3,2,1,0:T(8,128)(2,1)S(1)} %slice_bitcast_fusion.28), channel_id=1, source_target_pairs={{0,4},{1,5},{2,6},{3,7},{4,0},{5,1},{6,2},{7,3},{8,12},{9,13},{10,... | collective-permute-start | bytes 1572872 | tf_op jit(solution)/shard_map/ppermute | solution.py:27
  365.2 41.6 %collective-permute-start.32 = (bf16[2,256,1024]{2,1,0:T(8,128)(2,1)S(1)}, bf16[2,256,1024]{2,1,0:T(8,128)(2,1)S(1)}, u32[]{:S(2)}, u32[]{:S(2)}) collective-permute-start(bf16[2,256,1024]{2,1,0:T(8,128)(2,1)S(1)} %slice_bitcast_fusion.10), channel_id=1, source_target_pairs={{0,8},{8,0},{16,24},{24,16},{1,9},{9,1},{17,25},{25,17},{2,10},{10... | collective-permute-start | bytes 3145736 | tf_op jit(solution)/shard_map/ppermute | solution.py:27
  367.0 44.0 %collective-permute-start.34 = (bf16[2,1,128,2048]{3,2,0,1:T(8,128)(2,1)S(1)}, bf16[2,1,128,2048]{3,2,0,1:T(8,128)(2,1)S(1)}, u32[]{:S(2)}, u32[]{:S(2)}) collective-permute-start(bf16[2,1,128,2048]{3,2,0,1:T(8,128)(2,1)S(1)} %slice_bitcast_fusion.8), channel_id=1, source_target_pairs={{0,2},{1,3},{2,0},{3,1},{4,6},{5,7},{6,4},{7,5},{8,10},{9,11},{10,... | collective-permute-start | bytes 3145736 | tf_op jit(solution)/shard_map/ppermute | solution.py:27
  367.6 31.5 %collective-permute-start.36 = (bf16[512,256]{1,0:T(8,128)(2,1)S(1)}, bf16[512,256]{1,0:T(8,128)(2,1)S(1)}, u32[]{:S(2)}, u32[]{:S(2)}) collective-permute-start(bf16[512,256]{1,0:T(8,128)(2,1)S(1)} %constant_dynamic-slice_fusion.4), channel_id=1, source_target_pairs={{0,24},{8,16},{16,8},{24,0},{1,25},{9,17},{17,9},{25,1},{2,26},{10... | collective-permute-start | bytes 786440 | tf_op jit(solution)/shard_map/ppermute | solution.py:27
  370.6 36.0 %collective-permute-start.37 = (bf16[512,512]{1,0:T(8,128)(2,1)S(1)}, bf16[512,512]{1,0:T(8,128)(2,1)S(1)}, u32[]{:S(2)}, u32[]{:S(2)}) collective-permute-start(bf16[512,512]{1,0:T(8,128)(2,1)S(1)} %constant_dynamic-slice_fusion.3), channel_id=1, source_target_pairs={{0,8},{8,0},{16,24},{24,16},{1,9},{9,1},{17,25},{25,17},{2,10},{10... | collective-permute-start | bytes 1572872 | tf_op jit(solution)/shard_map/ppermute | solution.py:27
  371.3 40.1 %collective-permute-start.35 = (bf16[1,2,128,2176]{3,2,1,0:T(8,128)(2,1)S(1)}, bf16[1,2,128,2176]{3,2,1,0:T(8,128)(2,1)S(1)}, u32[]{:S(2)}, u32[]{:S(2)}) collective-permute-start(bf16[1,2,128,2176]{3,2,1,0:T(8,128)(2,1)S(1)} %slice_bitcast_fusion.6), channel_id=1, source_target_pairs={{0,4},{1,5},{2,6},{3,7},{4,0},{5,1},{6,2},{7,3},{8,12},{9,13},{10,... | collective-permute-start | bytes 3342344 | tf_op jit(solution)/shard_map/ppermute | solution.py:27
  407.2 25.7 %collective-permute-start.33 = (bf16[1,256,1024]{2,1,0:T(8,128)(2,1)S(1)}, bf16[1,256,1024]{2,1,0:T(8,128)(2,1)S(1)}, u32[]{:S(2)}, u32[]{:S(2)}) collective-permute-start(bf16[1,256,1024]{2,1,0:T(8,128)(2,1)S(1)} %slice_bitcast_fusion.24), channel_id=1, source_target_pairs={{0,24},{8,16},{16,8},{24,0},{1,25},{9,17},{17,9},{25,1},{2,26},{10... | collective-permute-start | bytes 1572872 | tf_op jit(solution)/shard_map/ppermute | solution.py:27
  411.7 22.2 %collective-permute-start.38 = (bf16[1,1,128,2048]{3,2,1,0:T(8,128)(2,1)S(1)}, bf16[1,1,128,2048]{3,2,1,0:T(8,128)(2,1)S(1)}, u32[]{:S(2)}, u32[]{:S(2)}) collective-permute-start(bf16[1,1,128,2048]{3,2,1,0:T(8,128)(2,1)S(1)} %slice_bitcast_fusion.22), channel_id=1, source_target_pairs={{0,4},{1,5},{2,6},{3,7},{4,0},{5,1},{6,2},{7,3},{8,12},{9,13},{10,... | collective-permute-start | bytes 1572872 | tf_op jit(solution)/shard_map/ppermute | solution.py:27
  412.5 17.1 %collective-permute-start.40 = (bf16[512,256]{1,0:T(8,128)(2,1)S(1)}, bf16[512,256]{1,0:T(8,128)(2,1)S(1)}, u32[]{:S(2)}, u32[]{:S(2)}) collective-permute-start(bf16[512,256]{1,0:T(8,128)(2,1)S(1)} %add_convert_fusion.9), channel_id=1, source_target_pairs={{0,24},{8,16},{16,8},{24,0},{1,25},{9,17},{17,9},{25,1},{2,26},{10... | collective-permute-start | bytes 786440 | tf_op jit(solution)/shard_map/ppermute | solution.py:27
  412.7 21.4 %collective-permute-start.39 = (bf16[1,1,128,2176]{3,2,1,0:T(8,128)(2,1)S(1)}, bf16[1,1,128,2176]{3,2,1,0:T(8,128)(2,1)S(1)}, u32[]{:S(2)}, u32[]{:S(2)}) collective-permute-start(bf16[1,1,128,2176]{3,2,1,0:T(8,128)(2,1)S(1)} %slice_bitcast_fusion.20), channel_id=1, source_target_pairs={{0,2},{1,3},{2,0},{3,1},{4,6},{5,7},{6,4},{7,5},{8,10},{9,11},{10,... | collective-permute-start | bytes 1671176 | tf_op jit(solution)/shard_map/ppermute | solution.py:27
  414.2 18.7 %collective-permute-start.41 = (bf16[512,256]{1,0:T(8,128)(2,1)S(1)}, bf16[512,256]{1,0:T(8,128)(2,1)S(1)}, u32[]{:S(2)}, u32[]{:S(2)}) collective-permute-start(bf16[512,256]{1,0:T(8,128)(2,1)S(1)} %constant_dynamic-slice_fusion.2), channel_id=1, source_target_pairs={{0,24},{8,16},{16,8},{24,0},{1,25},{9,17},{17,9},{25,1},{2,26},{10... | collective-permute-start | bytes 786440 | tf_op jit(solution)/shard_map/ppermute | solution.py:27
  434.9 29.6 %collective-permute-start.43 = (bf16[512,256]{1,0:T(8,128)(2,1)S(1)}, bf16[512,256]{1,0:T(8,128)(2,1)S(1)}, u32[]{:S(2)}, u32[]{:S(2)}) collective-permute-start(bf16[512,256]{1,0:T(8,128)(2,1)S(1)} %add_convert_fusion.8), channel_id=1, source_target_pairs={{0,24},{8,16},{16,8},{24,0},{1,25},{9,17},{17,9},{25,1},{2,26},{10... | collective-permute-start | bytes 786440 | tf_op jit(solution)/shard_map/ppermute | solution.py:27
  438.6 38.7 %collective-permute-start.44 = (bf16[512,512]{1,0:T(8,128)(2,1)S(1)}, bf16[512,512]{1,0:T(8,128)(2,1)S(1)}, u32[]{:S(2)}, u32[]{:S(2)}) collective-permute-start(bf16[512,512]{1,0:T(8,128)(2,1)S(1)} %pad_maximum_fusion.41), channel_id=1, source_target_pairs={{0,8},{8,0},{16,24},{24,16},{1,9},{9,1},{17,25},{25,17},{2,10},{10... | collective-permute-start | bytes 1572872 | tf_op jit(solution)/shard_map/ppermute | solution.py:27
  464.4 21.4 %collective-permute-start.42 = (bf16[528,512]{1,0:T(8,128)(2,1)S(1)}, bf16[528,512]{1,0:T(8,128)(2,1)S(1)}, u32[]{:S(2)}, u32[]{:S(2)}) collective-permute-start(bf16[528,512]{1,0:T(8,128)(2,1)S(1)} %constant_dynamic-slice_fusion.1), channel_id=1, source_target_pairs={{0,8},{8,0},{16,24},{24,16},{1,9},{9,1},{17,25},{25,17},{2,10},{10... | collective-permute-start | bytes 1622024 | tf_op jit(solution)/shard_map/ppermute | solution.py:27
  486.0 20.7 %copy-start.11 = (f32[256,1024]{1,0:T(8,128)S(1)}, f32[256,1024]{1,0:T(8,128)}, u32[]{:S(2)}) copy-start(f32[256,1024]{1,0:T(8,128)} %copy-done.10) | copy-start | bytes 3145732
  486.1 11.3 %collective-permute-start.45 = (bf16[528,256]{1,0:T(8,128)(2,1)S(1)}, bf16[528,256]{1,0:T(8,128)(2,1)S(1)}, u32[]{:S(2)}, u32[]{:S(2)}) collective-permute-start(bf16[528,256]{1,0:T(8,128)(2,1)S(1)} %constant_dynamic-slice_fusion), channel_id=1, source_target_pairs={{0,24},{8,16},{16,8},{24,0},{1,25},{9,17},{17,9},{25,1},{2,26},{10... | collective-permute-start | bytes 811016 | tf_op jit(solution)/shard_map/ppermute | solution.py:27
  488.3 16.5 %collective-permute-start.46 = (bf16[512,512]{1,0:T(8,128)(2,1)S(1)}, bf16[512,512]{1,0:T(8,128)(2,1)S(1)}, u32[]{:S(2)}, u32[]{:S(2)}) collective-permute-start(bf16[512,512]{1,0:T(8,128)(2,1)S(1)} %pad_maximum_fusion.42), channel_id=1, source_target_pairs={{0,8},{8,0},{16,24},{24,16},{1,9},{9,1},{17,25},{25,17},{2,10},{10... | collective-permute-start | bytes 1572872 | tf_op jit(solution)/shard_map/ppermute | solution.py:27
  505.1 9.4 %collective-permute-start.47 = (bf16[528,256]{1,0:T(8,128)(2,1)S(1)}, bf16[528,256]{1,0:T(8,128)(2,1)S(1)}, u32[]{:S(2)}, u32[]{:S(2)}) collective-permute-start(bf16[528,256]{1,0:T(8,128)(2,1)S(1)} %add_convert_fusion.7), channel_id=1, source_target_pairs={{0,24},{8,16},{16,8},{24,0},{1,25},{9,17},{17,9},{25,1},{2,26},{10... | collective-permute-start | bytes 811016 | tf_op jit(solution)/shard_map/ppermute | solution.py:27
  514.6 12.4 %collective-permute-start.48 = (bf16[528,512]{1,0:T(8,128)(2,1)S(1)}, bf16[528,512]{1,0:T(8,128)(2,1)S(1)}, u32[]{:S(2)}, u32[]{:S(2)}) collective-permute-start(bf16[528,512]{1,0:T(8,128)(2,1)S(1)} %pad_maximum_fusion.40), channel_id=1, source_target_pairs={{0,8},{8,0},{16,24},{24,16},{1,9},{9,1},{17,25},{25,17},{2,10},{10... | collective-permute-start | bytes 1622024 | tf_op jit(solution)/shard_map/ppermute | solution.py:27
  (38 other events, 161.1 us)
